TPU v7x, 128 devices: a whole 4x4x4 slice. The times are simulated.
128 devices in a mesh: head: 2 (over core), blk: 32 (over x_hi, y, z), seq: 2 (over x_lo).
Axes of the slice: x: 4 (x_hi: 2, x_lo: 2; x = x_hi * 2 + x_lo), y: 4, z: 4, core: 2. Of those that a mesh axis runs over, the one named last changes fastest.
Arguments:
- inputs: bfloat16 [2, 8192, 1600], P('seq', ('head', 'blk')), may hold values from -6 to 6
- segment_ids: int32 [2, 8192], P('seq'), may hold values from 0 to 11, as said below
- out_grad: bfloat16 [2, 8192, 1600], P('seq', ('head', 'blk')), may hold values from -6 to 6
- norm_gain: float32 [1600], replicated, may hold values from 0.5 to 1.5
- w_query: bfloat16 [1600, 1600], P(('blk', 'seq'), 'head'), may hold values from -0.15625 to 0.15625
- w_key: bfloat16 [1600, 320], P(('blk', 'seq'), 'head'), may hold values from -0.15625 to 0.15625
- w_value: bfloat16 [1600, 320], P(('blk', 'seq'), 'head'), may hold values from -0.15625 to 0.15625
- w_attn_out: bfloat16 [1600, 1600], P(('blk', 'seq'), 'head'), may hold values from -0.15625 to 0.15625
- w_mamba_in: bfloat16 [1600, 6400], P(('blk', 'seq'), 'head'), may hold values from -0.15625 to 0.15625
- conv_weight: float32 [4, 3200], replicated, may hold values from -3 to 3
- conv_bias: float32 [3200], replicated, may hold values from -3 to 3
- w_select: bfloat16 [3200, 132], P(('blk', 'seq'), 'head'), may hold values from -0.21875 to 0.21875
- w_step: bfloat16 [3200, 100], P(('blk', 'seq'), 'head'), may hold values from -0.625 to 0.625
- step_bias: float32 [3200], replicated, may hold values from -6 to -2
- log_decay: float32 [16, 3200], replicated, may hold values from -4.6 to 0
- skip_gain: float32 [3200], replicated, may hold values from 0.5 to 1.5
- w_mamba_out: bfloat16 [3200, 1600], P(('blk', 'seq'), 'head'), may hold values from -0.109375 to 0.109375
- attn_gain: float32 [1600], replicated, may hold values from 0.5 to 1.5
- mamba_gain: float32 [1600], replicated, may hold values from 0.5 to 1.5
- ffn_norm_gain: float32 [1600], replicated, may hold values from 0.5 to 1.5
- w_gate: bfloat16 [1600, 5504], P(('blk', 'seq'), 'head'), may hold values from -0.15625 to 0.15625
- w_up: bfloat16 [1600, 5504], P(('blk', 'seq'), 'head'), may hold values from -0.15625 to 0.15625
- w_down: bfloat16 [5504, 1600], P(('blk', 'seq'), 'head'), may hold values from -0.078125 to 0.078125
Outputs:
- output: bfloat16 [2, 8192, 1600], P('seq', ('head', 'blk'))
- input_grad: bfloat16 [2, 8192, 1600], P('seq', ('head', 'blk'))
- grad_norm_gain: float32 [1600], replicated
- grad_query: float32 [1600, 1600], P(('blk', 'seq'), 'head')
- grad_key: float32 [1600, 320], P(('blk', 'seq'), 'head')
- grad_value: float32 [1600, 320], P(('blk', 'seq'), 'head')
- grad_attn_out: float32 [1600, 1600], P(('blk', 'seq'), 'head')
- grad_mamba_in: float32 [1600, 6400], P(('blk', 'seq'), 'head')
- grad_conv_weight: float32 [4, 3200], replicated
- grad_conv_bias: float32 [3200], replicated
- grad_select: float32 [3200, 132], P(('blk', 'seq'), 'head')
- grad_step: float32 [3200, 100], P(('blk', 'seq'), 'head')
- grad_step_bias: float32 [3200], replicated
- grad_log_decay: float32 [16, 3200], replicated
- grad_skip_gain: float32 [3200], replicated
- grad_mamba_out: float32 [3200, 1600], P(('blk', 'seq'), 'head')
- grad_attn_gain: float32 [1600], replicated
- grad_mamba_gain: float32 [1600], replicated
- grad_ffn_norm_gain: float32 [1600], replicated
- grad_gate: float32 [1600, 5504], P(('blk', 'seq'), 'head')
- grad_up: float32 [1600, 5504], P(('blk', 'seq'), 'head')
- grad_down: float32 [5504, 1600], P(('blk', 'seq'), 'head')
Inputs may be any that keep to these rules, and one draw needn't show every extreme that they name: `segment_ids`: segment numbers start at 0, never fall along a sequence and rise by at most 1 from one position to the next; every sequence holds exactly 12 documents, whose lengths differ widely, and the longest of them holds at least an eighth of the sequence's positions.
All inputs are finite; a program needn't handle non-finite values.
Results may differ from a plain program's by a relative error of at most 0.018.
Values may be sent and summed in bfloat16 or wider, within the bound.
No kernel may reach another device: no remote copies, remote signals or barrier semaphores. Data moves between devices by JAX's collectives and lax.ppermute only.
A program may use at most 576 MiB of HBM per device.

v0:
```python
import math

import jax
import jax.numpy as jnp
from jax import lax
from jax.sharding import Mesh
from jax.sharding import PartitionSpec as P

HEADS = 25
KV_HEADS = 5
HEAD_DIM = 64
WINDOW = 1024
RANK = 100
BLK_SEQ = ("blk_0", "blk_1", "blk_2", "seq")
HEAD_BLK = ("head", "blk_0", "blk_1", "blk_2")
HEAD_BLK_SEQ = ("head", "blk_0", "blk_1", "blk_2", "seq")


EPSILON = 1e-06


def laid_out(tiles, dim):
    tiles = jnp.moveaxis(tiles, 0, dim)
    shape = tiles.shape
    return tiles.reshape(*shape[:dim], shape[dim] * shape[dim + 1], *shape[dim + 2 :])


def gather_together(arrays, axis, dims):
    ravelled = jnp.concatenate([a.reshape(-1) for a in arrays])
    lines, at, finished = (lax.all_gather(ravelled, axis), 0, [])
    for a, dim in zip(arrays, dims):
        tiles = lines[:, at : at + a.size].reshape(-1, *a.shape)
        finished.append(laid_out(tiles, dim))
        at += a.size
    return tuple(finished)


def sent_together(arrays, axis, dim, along):
    widths = [a.shape[along] for a in arrays]
    both = jnp.concatenate(arrays, axis=along)
    whole = lax.all_gather(both, axis, axis=dim, tiled=True)
    return tuple(jnp.split(whole, [sum(widths[:k]) for k in range(1, len(widths))], axis=along))


def sent_together_2(arrays, axis, dim, along):
    widths = [a.shape[along] for a in arrays]
    both = jnp.concatenate(arrays, axis=along)
    whole = lax.psum_scatter(both, axis, scatter_dimension=dim, tiled=True)
    return tuple(jnp.split(whole, [sum(widths[:k]) for k in range(1, len(widths))], axis=along))


def passed_along(block, axis, distance):
    devices = range(lax.axis_size(axis))
    route = [(i - distance, i) for i in devices if i - distance in devices]
    return lax.ppermute(block, axis, route)


def nothing_yet(value, identity):
    return jax.tree.map(
        lambda a, e: jnp.broadcast_to(jnp.asarray(e, a.dtype), a.shape), value, identity
    )


def carried_in(value, axes, combine, identity, reverse):
    before = start = nothing_yet(value, identity)
    subtotal = value
    for axis in reversed(axes):
        length, mine = (lax.axis_size(axis), lax.axis_index(axis))
        pieces = jax.tree.map(lambda part: lax.all_gather(part, axis), subtotal)
        inside, subtotal = (start, start)
        for k in reversed(range(length)) if reverse else range(length):
            passed = k > mine if reverse else k < mine
            subtotal = combine(subtotal, jax.tree.map(lambda part: part[k], pieces))
            inside = jax.tree.map(lambda new, old: jnp.where(passed, new, old), subtotal, inside)
        before = combine(inside, before)
    return before


def shortened(value):
    return jax.tree.map(lambda a: a.astype(jnp.bfloat16) if a.dtype == jnp.float32 else a, value)


def rms_scale(values, gain):
    return values * lax.rsqrt(jnp.mean(values * values, axis=-1, keepdims=True) + EPSILON) * gain


def to_low(values):
    return values.astype(jnp.bfloat16)


def product(left, right):
    return jnp.dot(left, right, preferred_element_type=jnp.float32)


def product_tn(left, right):
    return lax.dot_general(
        left, right, (((0,), (0,)), ((), ())), preferred_element_type=jnp.float32
    )


def product_nt(left, right):
    return lax.dot_general(
        left, right, (((1,), (1,)), ((), ())), preferred_element_type=jnp.float32
    )


def chain_combine(earlier, later):
    return (earlier[0] * later[0], later[0] * earlier[1] + later[1])


def gather_weights(
    w_query,
    w_key,
    w_value,
    w_attn_out,
    w_mamba_in,
    w_select,
    w_step,
    w_mamba_out,
    w_gate,
    w_up,
    w_down,
):
    rows_all = gather_together(
        (
            w_query,
            w_key,
            w_value,
            w_attn_out,
            w_mamba_in,
            w_select,
            w_step,
            w_mamba_out,
            w_gate,
            w_up,
            w_down,
        ),
        BLK_SEQ,
        (0, 0, 0, 0, 0, 0, 0, 0, 0, 0, 0),
    )
    return (
        lax.all_gather(rows_all[0], "head", axis=1, tiled=True),
        *sent_together((rows_all[1], rows_all[2]), "head", 1, 0),
        lax.all_gather(rows_all[3], "head", axis=1, tiled=True),
        lax.all_gather(rows_all[4], "head", axis=1, tiled=True),
        lax.all_gather(rows_all[5], "head", axis=1, tiled=True),
        lax.all_gather(rows_all[6], "head", axis=1, tiled=True),
        lax.all_gather(rows_all[7], "head", axis=1, tiled=True),
        *sent_together((rows_all[8], rows_all[9]), "head", 1, 0),
        lax.all_gather(rows_all[10], "head", axis=1, tiled=True),
    )


def sum_weights(
    g_one, g_two, g_three, g_four, g_five, g_six, g_seven, g_eight, g_nine, g_ten, g_eleven
):
    grads = (
        g_one,
        g_two,
        g_three,
        g_four,
        g_five,
        g_six,
        g_seven,
        g_eight,
        g_nine,
        g_ten,
        g_eleven,
    )
    grads = (
        lax.psum_scatter(
            g_one.astype(jnp.bfloat16), "head", scatter_dimension=1, tiled=True
        ).astype(jnp.float32),
        *tuple(
            (
                part.astype(jnp.float32)
                for part in sent_together_2(
                    (g_two.astype(jnp.bfloat16), g_three.astype(jnp.bfloat16)), "head", 1, 0
                )
            )
        ),
        lax.psum_scatter(
            g_four.astype(jnp.bfloat16), "head", scatter_dimension=1, tiled=True
        ).astype(jnp.float32),
        lax.psum_scatter(
            g_five.astype(jnp.bfloat16), "head", scatter_dimension=1, tiled=True
        ).astype(jnp.float32),
        lax.psum_scatter(
            g_six.astype(jnp.bfloat16), "head", scatter_dimension=1, tiled=True
        ).astype(jnp.float32),
        lax.psum_scatter(
            g_seven.astype(jnp.bfloat16), "head", scatter_dimension=1, tiled=True
        ).astype(jnp.float32),
        lax.psum_scatter(
            g_eight.astype(jnp.bfloat16), "head", scatter_dimension=1, tiled=True
        ).astype(jnp.float32),
        *tuple(
            (
                part.astype(jnp.float32)
                for part in sent_together_2(
                    (g_nine.astype(jnp.bfloat16), g_ten.astype(jnp.bfloat16)), "head", 1, 0
                )
            )
        ),
        lax.psum_scatter(
            g_eleven.astype(jnp.bfloat16), "head", scatter_dimension=1, tiled=True
        ).astype(jnp.float32),
    )
    return (
        lax.psum_scatter(grads[0], BLK_SEQ, scatter_dimension=0, tiled=True),
        lax.psum_scatter(grads[1], BLK_SEQ, scatter_dimension=0, tiled=True),
        lax.psum_scatter(grads[2], BLK_SEQ, scatter_dimension=0, tiled=True),
        lax.psum_scatter(grads[3], BLK_SEQ, scatter_dimension=0, tiled=True),
        lax.psum_scatter(grads[4], BLK_SEQ, scatter_dimension=0, tiled=True),
        lax.psum_scatter(grads[5], BLK_SEQ, scatter_dimension=0, tiled=True),
        lax.psum_scatter(grads[6], BLK_SEQ, scatter_dimension=0, tiled=True),
        lax.psum_scatter(grads[7], BLK_SEQ, scatter_dimension=0, tiled=True),
        lax.psum_scatter(grads[8], BLK_SEQ, scatter_dimension=0, tiled=True),
        lax.psum_scatter(grads[9], BLK_SEQ, scatter_dimension=0, tiled=True),
        lax.psum_scatter(grads[10], BLK_SEQ, scatter_dimension=0, tiled=True),
    )


def conv_silu(padded, conv_weight, conv_bias):
    tap_count = conv_weight.shape[0]
    length = padded.shape[0] - tap_count + 1
    total_sum = conv_bias
    for tap_index in range(tap_count):
        total_sum = total_sum + conv_weight[tap_index] * padded[tap_index : tap_index + length]
    return jax.nn.silu(total_sum)


def rate_piece(step_pre, step_bias, log_decay):
    return (jax.nn.softplus(step_pre + step_bias), -jnp.exp(log_decay))


def local_scan(step_size, decay_rate, conv_values, in_mat, out_mat):
    rows_total = step_size.shape[0]
    block_rows = math.gcd(rows_total, 16)

    def local_one_block(state, members):
        step_block, conv_block, in_block, out_block = members
        log_decays = jnp.cumsum(step_block, axis=0)[:, None, :] * decay_rate[None]
        drive_terms = in_block[:, :, None] * (step_block * conv_block)[:, None, :]
        gathered = jnp.cumsum(jnp.exp(-log_decays) * drive_terms, axis=0)
        states = jnp.exp(log_decays) * (state[None] + gathered)
        return (states[-1], jnp.sum(out_block[:, :, None] * states, axis=1))

    shaped = tuple(
        (
            member.reshape(rows_total // block_rows, block_rows, member.shape[1])
            for member in (step_size, conv_values, in_mat, out_mat)
        )
    )
    start_state = jnp.zeros(decay_rate.shape, jnp.float32)
    end_state, outputs = lax.scan(jax.checkpoint(local_one_block), start_state, shaped)
    decay_total = jnp.exp(jnp.sum(step_size, axis=0)[None, :] * decay_rate)
    return (outputs.reshape(rows_total, decay_rate.shape[1]), end_state, decay_total)


def carry_in(step_size, decay_rate, out_mat, state_in):
    rows_total = step_size.shape[0]
    block_rows = math.gcd(rows_total, 16)

    def carry_one_block(running, members):
        step_block, out_block = members
        totals = running[None] + jnp.cumsum(step_block, axis=0)
        weights = jnp.exp(totals[:, None, :] * decay_rate[None])
        return (totals[-1], jnp.sum(out_block[:, :, None] * weights * state_in[None], axis=1))

    shaped = (
        step_size.reshape(rows_total // block_rows, block_rows, step_size.shape[1]),
        out_mat.reshape(rows_total // block_rows, block_rows, out_mat.shape[1]),
    )
    running_end, outputs = lax.scan(
        jax.checkpoint(carry_one_block), jnp.zeros((decay_rate.shape[1],), jnp.float32), shaped
    )
    return outputs.reshape(rows_total, decay_rate.shape[1])


def gate_piece(local_out, carried_out, conv_values, gate_z, skip_gain):
    return (local_out + carried_out + skip_gain * conv_values) * jax.nn.silu(gate_z)


def merge_piece(tokens, attn_out, mamba_out, attn_gain, mamba_gain):
    return tokens + 0.5 * (rms_scale(attn_out, attn_gain) + rms_scale(mamba_out, mamba_gain))


def swiglu(gate_val, up_val):
    return jax.nn.silu(gate_val) * up_val


def group_scores(queries, window_keys, allowed, group_index, group_size, score_scale):
    query_part = queries[
        :, group_index * group_size * HEAD_DIM : (group_index + 1) * group_size * HEAD_DIM
    ].reshape(queries.shape[0], group_size, HEAD_DIM)
    key_part = window_keys[:, group_index * HEAD_DIM : (group_index + 1) * HEAD_DIM]
    raw_scores = (
        jnp.einsum("qgd,sd->gqs", query_part, key_part, preferred_element_type=jnp.float32)
        * score_scale
    )
    return (jnp.where(allowed[None], raw_scores, -1e30), query_part, key_part)


def shards(
    inputs,
    segment_ids,
    out_grad,
    norm_gain,
    w_query,
    w_key,
    w_value,
    w_attn_out,
    w_mamba_in,
    conv_weight,
    conv_bias,
    w_select,
    w_step,
    step_bias,
    log_decay,
    skip_gain,
    w_mamba_out,
    attn_gain,
    mamba_gain,
    ffn_norm_gain,
    w_gate,
    w_up,
    w_down,
):
    rows_dev = inputs.shape[1]
    inner_width = conv_weight.shape[1]
    edge_count = conv_weight.shape[0] - 1
    rank_width = RANK
    state_width = log_decay.shape[0]
    reach_blocks = WINDOW // rows_dev
    group_size = HEADS // KV_HEADS
    score_scale = 1.0 / math.sqrt(HEAD_DIM)
    position = lax.axis_index(HEAD_BLK)
    tokens = inputs[0].astype(jnp.float32)

    def project(pairs):
        outs = [product(pair[0], pair[1]) for pair in pairs]
        return outs

    def project_back(triples):
        grads_low = [triple[0] for triple in triples]
        weight_grads = [product_tn(triple[1], grad) for triple, grad in zip(triples, grads_low)]
        input_grads = [product_nt(grad, triple[2]) for triple, grad in zip(triples, grads_low)]
        return (weight_grads, input_grads)

    weights_full = gather_weights(
        w_query,
        w_key,
        w_value,
        w_attn_out,
        w_mamba_in,
        w_select,
        w_step,
        w_mamba_out,
        w_gate,
        w_up,
        w_down,
    )
    normed, norm_back = jax.vjp(rms_scale, tokens, norm_gain)
    normed_low = to_low(normed)
    normed_all = [normed_low][0]
    query_f, key_f, value_f, mixed_in = project(
        [
            (normed_all, weights_full[0]),
            (normed_all, weights_full[1]),
            (normed_all, weights_full[2]),
            (normed_all, weights_full[4]),
        ]
    )
    queries = to_low(query_f)
    keys_low = to_low(key_f)
    values_low = to_low(value_f)
    conv_in = to_low(mixed_in[:, :inner_width])
    gate_z = mixed_in[:, inner_width:]
    key_blocks = [keys_low]
    value_blocks = [values_low]
    current = (keys_low, values_low, conv_in[rows_dev - edge_count :])
    edge_rows = current[2]
    for offset in range(1, reach_blocks + 1):
        current = passed_along((current[0], current[1], current[2]), HEAD_BLK, 1)
        key_blocks.append(current[0])
        value_blocks.append(current[1])
        if offset == 1:
            edge_rows = current[2]
    window_keys = jnp.concatenate(key_blocks[::-1], axis=0)
    window_values = jnp.concatenate(value_blocks[::-1], axis=0)
    span_keys = (reach_blocks + 1) * rows_dev
    segment_row = segment_ids[0]
    padded_segs = jnp.concatenate(
        [jnp.full((reach_blocks * rows_dev,), -1, jnp.int32), segment_row]
    )
    key_segs = lax.dynamic_slice_in_dim(padded_segs, position * rows_dev, span_keys)
    query_segs = lax.dynamic_slice_in_dim(segment_row, position * rows_dev, rows_dev)
    gaps = (reach_blocks * rows_dev + jnp.arange(rows_dev, dtype=jnp.int32))[:, None] - jnp.arange(
        span_keys, dtype=jnp.int32
    )[None, :]
    allowed = (gaps >= 0) & (gaps < WINDOW) & (query_segs[:, None] == key_segs[None, :])
    head_outputs = []
    log_totals = []
    for group_index in range(KV_HEADS):
        scores, query_part, key_part = group_scores(
            queries, window_keys, allowed, group_index, group_size, score_scale
        )
        row_max = jnp.max(scores, axis=-1, keepdims=True)
        exp_scores = jnp.exp(scores - row_max)
        row_total = jnp.sum(exp_scores, axis=-1, keepdims=True)
        log_totals.append(row_max + jnp.log(row_total))
        weights_low = to_low(exp_scores / row_total)
        value_part = window_values[:, group_index * HEAD_DIM : (group_index + 1) * HEAD_DIM]
        head_outputs.append(
            jnp.einsum(
                "gqs,sd->qgd", weights_low, value_part, preferred_element_type=jnp.float32
            ).reshape(rows_dev, group_size * HEAD_DIM)
        )
    heads_low = to_low(jnp.concatenate(head_outputs, axis=1))
    padded_in = jnp.concatenate([edge_rows, conv_in], axis=0).astype(jnp.float32)
    conved, conv_back = jax.vjp(conv_silu, padded_in, conv_weight, conv_bias)
    conved_low = to_low(conved)
    conv_values = conved_low.astype(jnp.float32)
    conved_all = [conved_low][0]
    selected = project([(conved_all, weights_full[5])])[0]
    step_raw = to_low(selected[:, :rank_width])
    in_mat = selected[:, rank_width : rank_width + state_width]
    out_mat = selected[:, rank_width + state_width :]
    step_all = [step_raw][0]
    step_pre = [product_nt(step_all, weights_full[6])][0]
    (step_size, decay_rate), rate_back = jax.vjp(rate_piece, step_pre, step_bias, log_decay)
    (local_out, end_state, decay_total), local_back = jax.vjp(
        local_scan, step_size, decay_rate, conv_values, in_mat, out_mat
    )
    state_in = carried_in(
        (decay_total, end_state),
        HEAD_BLK,
        chain_combine,
        (jnp.ones_like(decay_total), jnp.zeros_like(end_state)),
        False,
    )[1]
    carried_out, carry_back = jax.vjp(carry_in, step_size, decay_rate, out_mat, state_in)
    gated, gate_back = jax.vjp(gate_piece, local_out, carried_out, conv_values, gate_z, skip_gain)
    gated_low = to_low(gated)
    heads_all, gated_all = [heads_low, gated_low]
    attn_out, mamba_out = project([(heads_all, weights_full[3]), (gated_all, weights_full[7])])
    hidden_mid, merge_back = jax.vjp(
        merge_piece, tokens, attn_out, mamba_out, attn_gain, mamba_gain
    )
    normed_two, norm_two_back = jax.vjp(rms_scale, hidden_mid, ffn_norm_gain)
    normed_two_low = to_low(normed_two)
    normed_two_all = [normed_two_low][0]
    gate_val, up_val = project(
        [(normed_two_all, weights_full[8]), (normed_two_all, weights_full[9])]
    )
    act_val, act_back = jax.vjp(swiglu, gate_val, up_val)
    act_low = to_low(act_val)
    act_all = [act_low][0]
    down_val = project([(act_all, weights_full[10])])[0]
    result = hidden_mid + down_val
    output = to_low(result)[None]
    weights_back = gather_weights(
        w_query,
        w_key,
        w_value,
        w_attn_out,
        w_mamba_in,
        w_select,
        w_step,
        w_mamba_out,
        w_gate,
        w_up,
        w_down,
    )
    grad_out = out_grad[0]
    down_grads, down_inputs = project_back([(grad_out, act_all, weights_back[10])])
    grad_down = down_grads[0]
    d_gate, d_up = act_back(down_inputs[0])
    d_gate_low = to_low(d_gate)
    d_up_low = to_low(d_up)
    ffn_grads, ffn_inputs = project_back(
        [(d_gate_low, normed_two_all, weights_back[8]), (d_up_low, normed_two_all, weights_back[9])]
    )
    d_normed_two = ffn_inputs[0] + ffn_inputs[1]
    d_mid_norm, grad_ffn_norm = norm_two_back(d_normed_two)
    d_mid = grad_out.astype(jnp.float32) + d_mid_norm
    d_tokens_res, d_attn_out, d_mamba_out, grad_attn_gain, grad_mamba_gain = merge_back(d_mid)
    d_attn_low = to_low(d_attn_out)
    d_mamba_low = to_low(d_mamba_out)
    branch_grads, branch_inputs = project_back(
        [(d_attn_low, heads_all, weights_back[3]), (d_mamba_low, gated_all, weights_back[7])]
    )
    d_heads = to_low(branch_inputs[0])
    d_gated = branch_inputs[1]
    query_grads = []
    key_grads = []
    value_grads = []
    for group_index in range(KV_HEADS):
        scores, query_part, key_part = group_scores(
            queries, window_keys, allowed, group_index, group_size, score_scale
        )
        weights_now = jnp.exp(scores - log_totals[group_index])
        weights_low = to_low(weights_now)
        value_part = window_values[:, group_index * HEAD_DIM : (group_index + 1) * HEAD_DIM]
        head_grad = d_heads[
            :, group_index * group_size * HEAD_DIM : (group_index + 1) * group_size * HEAD_DIM
        ].reshape(rows_dev, group_size, HEAD_DIM)
        d_weights = jnp.einsum(
            "qgd,sd->gqs", head_grad, value_part, preferred_element_type=jnp.float32
        )
        d_scores = to_low(
            weights_now * (d_weights - jnp.sum(weights_now * d_weights, axis=-1, keepdims=True))
        )
        query_grads.append(
            jnp.einsum(
                "gqs,sd->qgd", d_scores, key_part, preferred_element_type=jnp.float32
            ).reshape(rows_dev, group_size * HEAD_DIM)
            * score_scale
        )
        key_grads.append(
            jnp.einsum("gqs,qgd->sd", d_scores, query_part, preferred_element_type=jnp.float32)
            * score_scale
        )
        value_grads.append(
            jnp.einsum("gqs,qgd->sd", weights_low, head_grad, preferred_element_type=jnp.float32)
        )
    d_queries = to_low(jnp.concatenate(query_grads, axis=1))
    key_window_grad = jnp.concatenate(key_grads, axis=1)
    value_window_grad = jnp.concatenate(value_grads, axis=1)
    d_local, d_carried, d_conv_gate, d_gate_z, grad_skip = gate_back(d_gated)
    d_step_first, d_rate_first, d_out_first, d_state_in = carry_back(d_carried)
    d_end = carried_in(
        (decay_total, d_state_in),
        HEAD_BLK,
        chain_combine,
        (jnp.ones_like(decay_total), jnp.zeros_like(d_state_in)),
        True,
    )[1]
    d_step_second, d_rate_second, d_conv_scan, d_in_mat, d_out_second = local_back(
        (d_local, d_end, d_end * state_in)
    )
    d_step_pre, grad_step_bias, grad_log_decay = rate_back(
        (d_step_first + d_step_second, d_rate_first + d_rate_second)
    )
    d_step_low = to_low(d_step_pre)
    d_step_all = [d_step_low][0]
    grad_step_w = product_tn(d_step_all, step_all)
    d_step_raw = project([(d_step_all, weights_back[6])])[0]
    d_selected = to_low(jnp.concatenate([d_step_raw, d_in_mat, d_out_first + d_out_second], axis=1))
    select_grads, select_inputs = project_back([(d_selected, conved_all, weights_back[5])])
    d_conved = select_inputs[0] + d_conv_gate + d_conv_scan
    d_padded, grad_conv_w, grad_conv_b = conv_back(d_conved)

    def window_slice(values, offset):
        return values[(reach_blocks - offset) * rows_dev : (reach_blocks - offset + 1) * rows_dev]

    zero_edge = jnp.zeros((edge_count, inner_width), jnp.float32)
    carried = (
        window_slice(key_window_grad, reach_blocks),
        window_slice(value_window_grad, reach_blocks),
        zero_edge,
    )
    for offset in range(reach_blocks - 1, -1, -1):
        sending = d_padded[:edge_count] if offset == 0 else zero_edge
        moved = (
            passed_along(shortened(carried[0]), HEAD_BLK, -1),
            passed_along(shortened(carried[1]), HEAD_BLK, -1),
            passed_along(sending.astype(jnp.bfloat16), HEAD_BLK, -1).astype(sending.dtype),
        )
        carried = (
            moved[0] + window_slice(key_window_grad, offset),
            moved[1] + window_slice(value_window_grad, offset),
            moved[2],
        )
    d_keys = to_low(carried[0])
    d_values = to_low(carried[1])
    d_conv_in = d_padded[edge_count:] + jnp.concatenate(
        [jnp.zeros((rows_dev - edge_count, inner_width), jnp.float32), carried[2]], axis=0
    )
    d_mixed = to_low(jnp.concatenate([d_conv_in, d_gate_z], axis=1))
    first_grads, first_inputs = project_back(
        [
            (d_queries, normed_all, weights_back[0]),
            (d_keys, normed_all, weights_back[1]),
            (d_values, normed_all, weights_back[2]),
            (d_mixed, normed_all, weights_back[4]),
        ]
    )
    d_normed = first_inputs[0] + first_inputs[1] + first_inputs[2] + first_inputs[3]
    d_tokens_norm, grad_norm = norm_back(d_normed)
    input_grad = to_low(d_tokens_res + d_tokens_norm)[None]
    weight_sums = sum_weights(
        first_grads[0],
        first_grads[1],
        first_grads[2],
        branch_grads[0],
        first_grads[3],
        select_grads[0],
        grad_step_w,
        branch_grads[1],
        ffn_grads[0],
        ffn_grads[1],
        grad_down,
    )
    small_totals = lax.psum(
        (
            grad_norm,
            grad_conv_w,
            grad_conv_b,
            grad_step_bias,
            grad_log_decay,
            grad_skip,
            grad_attn_gain,
            grad_mamba_gain,
            grad_ffn_norm,
        ),
        HEAD_BLK_SEQ,
    )
    return (
        output,
        input_grad,
        small_totals[0],
        weight_sums[0],
        weight_sums[1],
        weight_sums[2],
        weight_sums[3],
        weight_sums[4],
        small_totals[1],
        small_totals[2],
        weight_sums[5],
        weight_sums[6],
        small_totals[3],
        small_totals[4],
        small_totals[5],
        weight_sums[7],
        small_totals[6],
        small_totals[7],
        small_totals[8],
        weight_sums[8],
        weight_sums[9],
        weight_sums[10],
    )


def solution(mesh):
    torus = Mesh(
        mesh.devices.reshape(mesh.shape["head"], 2, 4, 4, mesh.shape["seq"]),
        ("head", "blk_0", "blk_1", "blk_2", "seq"),
    )
    in_specs = (
        P("seq", HEAD_BLK, None),
        P("seq", None),
        P("seq", HEAD_BLK, None),
        P(),
        P(BLK_SEQ, "head"),
        P(BLK_SEQ, "head"),
        P(BLK_SEQ, "head"),
        P(BLK_SEQ, "head"),
        P(BLK_SEQ, "head"),
        P(),
        P(),
        P(BLK_SEQ, "head"),
        P(BLK_SEQ, "head"),
        P(),
        P(),
        P(),
        P(BLK_SEQ, "head"),
        P(),
        P(),
        P(),
        P(BLK_SEQ, "head"),
        P(BLK_SEQ, "head"),
        P(BLK_SEQ, "head"),
    )
    out_specs = (
        P("seq", HEAD_BLK, None),
        P("seq", HEAD_BLK, None),
        P(),
        P(BLK_SEQ, "head"),
        P(BLK_SEQ, "head"),
        P(BLK_SEQ, "head"),
        P(BLK_SEQ, "head"),
        P(BLK_SEQ, "head"),
        P(),
        P(),
        P(BLK_SEQ, "head"),
        P(BLK_SEQ, "head"),
        P(),
        P(),
        P(),
        P(BLK_SEQ, "head"),
        P(),
        P(),
        P(),
        P(BLK_SEQ, "head"),
        P(BLK_SEQ, "head"),
        P(BLK_SEQ, "head"),
    )
    return jax.shard_map(
        shards, mesh=torus, in_specs=in_specs, out_specs=out_specs, check_vma=False
    )
```

profile of v0, /device:TPU:0, one launch (start us, length us, event | category | flops | bytes accessed | tf_op | source)
XLA Modules:
  0.0 5623.5 jit_solution(3924340289263482642)
XLA Ops:
  26.6 15.4 broadcast.349
  54.7 434.1 %all-reduce.46.cloned.1.call-done = bf16[24332800]{0:T(1024)(128)(2,1)} async-done(((bf16[24332800]{0:T(1024)(128)(2,1)}), bf16[24332800]{0:T(1024)(128)(2,1)}) %all-reduce.46.cloned.1.call-update) | async-done | bytes 48665616
  488.8 107.4 %reshape.599 = bf16[64,380200]{1,0:T(8,128)(2,1)} reshape(bf16[24332800]{0:T(1024)(128)(2,1)} %all-reduce.46.cloned.1.call-done) | data formatting | bytes 97331200 | tf_op jit(solution)/shard_map/all_gather | solution.py:30
  636.6 17.7 reshape_reshape.48
  654.4 22.5 fusion.241
  676.9 19.0 reshape_reshape.54
  853.8 22.7 copy.224
  913.8 16.3 fusion.250
  960.5 78.0 %while.76 = (s32[]{:T(128)}, f32[16,3200]{1,0:T(8,128)}, f32[8,16,3200]{2,1,0:T(8,128)}, f32[8,16,3200]{2,1,0:T(8,128)}, f32[8,16,3200]{2,1,0:T(8,128)}, /*index...) while((s32[]{:T(128)}, f32[16,3200]{1,0:T(8,128)}, ...), condition=%wide.region_16.17_spmd, body=%wide.region_12.16_spmd.sunk | while | flops 20428800 | bytes 7788713 | solution.py:256
  1038.4 21.1 all-gather.2
  1073.8 20.5 all_gather.127
  1131.4 63.0 %while.77 = (s32[]{:T(128)}, f32[3200]{0:T(1024)S(1)}, f32[8,16,3200]{2,1,0:T(8,128)}, f32[8,3200]{1,0:T(8,128)}, f32[8,16,3200]{2,1,0:T(8,128)}, /*index=5*/f32...) while((s32[]{:T(128)}, f32[3200]{0:T(1024)S(1)}, ...), condition=%wide.region_21.22_spmd, body=%wide.region_18.21_spmd.sunk | while | flops 4044802 | bytes 2550409 | solution.py:275
  1207.9 16.4 fusion.42
  1236.7 22.3 fusion.40
  1259.1 16.1 multiply_reduce_fusion.19
  1294.4 86.5 %while.78 = (s32[]{:T(128)}, f32[16,3200]{1,0:T(8,128)S(1)}, f32[16,3200]{1,0:T(8,128)S(1)}, f32[3200]{0:T(1024)S(1)}, f32[8,16,3200]{2,1,0:T(8,128)S(1)}, /*ind...) while((s32[]{:T(128)}, f32[16,3200]{1,0:T(8,128)S(1)}, ...), condition=%wide.region_40.41_spmd.clone, body=%wide.region_32.40_spmd.clone.sunk | while | flops 12386948 | bytes 5632723 | solution.py:275
  1447.2 94.8 %while.79 = (s32[]{:T(128)}, f32[16,3200]{1,0:T(8,128)S(1)}, f32[16,3200]{1,0:T(8,128)S(1)}, f32[8,16,3200]{2,1,0:T(8,128)}, f32[8,16,3200]{2,1,0:T(8,128)}, /*i...) while((s32[]{:T(128)}, f32[16,3200]{1,0:T(8,128)S(1)}, ...), condition=%wide.region_53.54_spmd.clone, body=%wide.region_42.53_spmd.clone.sunk | while | flops 57343488 | bytes 31984352 | solution.py:256
  1676.0 25.1 pad_maximum_fusion
  1701.1 47.0 copy.294
  1750.6 41.6 fusion.234
  1859.2 14.9 dynamic-slice_convert_fusion
  1877.2 16.6 fusion.244
  1918.5 1057.0 %fusion.233 = (f32[32,3200]{1,0:T(8,128)S(1)}, f32[32,2752]{1,0:T(8,128)S(1)}) fusion(f32[1600,3200]{1,0:T(8,128)} %dynamic-slice_convert_fusion, f32[1600,2752]{1,0:T(8,128)} %convert_element_type.366), kind=kCustom, calls=%all-reduce-scatter.5 | all-reduce-scatter fusion | flops 12189697 | bytes 38855168
  3012.3 490.6 %fusion.4 = f32[32,2752]{1,0:T(8,128)S(1)} fusion(f32[1600,2752]{1,0:T(8,128)} %convert_element_type.367), kind=kCustom, calls=%all-reduce-scatter.4 | all-reduce-scatter fusion | flops 5636097 | bytes 17965568
  3564.9 14.9 collective-permute-start.56
  3659.9 25.2 collective-permute-start.70
  3707.2 22.7 collective-permute-start.46
  3755.4 1637.4 %all-reduce.53 = (f32[1600,800]{0,1:T(8,128)}, f32[1600,800]{0,1:T(8,128)}, f32[3200,800]{0,1:T(8,128)}, f32[5504,800]{0,1:T(8,128)}) all-reduce(bf16[1600,800]{0,1:T(8,128)(2,1)} %reduce-scatter.28.cloned.1.call-done, ...), channel_id=7, replica_groups=mesh['head'=2,'blk_0'=2,'blk_1'=4,'blk_2'=4,'seq'=2] {'blk_0','blk_1','b..., use_global_device_ids=true, to_apply=%region_58.59.clone | all-reduce | flops 9523200 | bytes 57139200
  5408.1 19.2 collective-permute-start.40
  5445.8 46.3 concatenate.77
  5508.8 46.6 concatenate.78
  5557.3 45.1 concatenate.74
  (1207 shorter events, 1298.4 us)
Async XLA Ops:
  7.2 481.6 %all-reduce.46.cloned.1.call-start = ((), (), s32[]{:S(2)}) async-start(), calls=%async_computation.19 | async-start | bytes 97333248
  54.5 683.6 %all-gather.14.cloned.1.call-start = ((), (), s32[]{:S(2)}) async-start(), calls=%async_computation.6 | async-start | bytes 3072000 | tf_op jit(solution)/shard_map/all_gather | solution.py:41
  601.9 282.1 %all-gather.16.cloned.1.call-start = ((), (), s32[]{:S(2)}) async-start(), calls=%async_computation.7 | async-start | bytes 7987200 | tf_op jit(solution)/shard_map/all_gather | solution.py:142
  616.8 289.7 %all-gather.18.cloned.1.call-start = ((), (), s32[]{:S(2)}) async-start(), calls=%async_computation.8 | async-start | bytes 7987200 | tf_op jit(solution)/shard_map/all_gather | solution.py:144
  626.6 287.2 %all-gather.20.cloned.1.call-start = ((), (), s32[]{:S(2)}) async-start(), calls=%async_computation.9 | async-start | bytes 30720000 | tf_op jit(solution)/shard_map/all_gather | solution.py:145
  654.4 279.7 %all-gather.26.cloned.1.call-start = ((), (), s32[]{:S(2)}) async-start(), calls=%async_computation.12 | async-start | bytes 26419200 | tf_op jit(solution)/shard_map/all_gather | solution.py:150
  709.3 489.9 %all-gather.22.cloned.1.call-start = ((), (), s32[]{:S(2)}) async-start(), calls=%async_computation.10 | async-start | bytes 15360000 | tf_op jit(solution)/shard_map/all_gather | solution.py:148
  736.8 471.1 %all-gather.24.cloned.1.call-start = ((), (), s32[]{:S(2)}) async-start(), calls=%async_computation.11 | async-start | bytes 52838400 | tf_op jit(solution)/shard_map/all_gather | solution.py:41
  876.6 927.4 %reduce-scatter.30.cloned.1.call-start = ((), (), s32[]{:S(2)}) async-start(), calls=%async_computation.14 | async-start | bytes 3072000 | tf_op jit(solution)/shard_map/reduce_scatter | solution.py:48
  1629.3 229.9 %all-reduce.48.cloned.1.call-start = ((), (), s32[]{:S(2)}) async-start(), calls=%async_computation.21 | async-start | bytes 40960000
  1654.8 222.3 %reduce-scatter.38.cloned.1.call-start = ((), (), s32[]{:S(2)}) async-start(), calls=%async_computation.20 | async-start | bytes 52838400
  1748.1 1952.4 %all-reduce.52.cloned.1.call-start = ((), (), s32[]{:S(2)}) async-start(), calls=%async_computation.23 | async-start | bytes 7536640
  1807.0 1900.3 %reduce-scatter.28.cloned.1.call-start = ((), (), s32[]{:S(2)}) async-start(), calls=%async_computation.13 | async-start | bytes 7987200 | tf_op jit(solution)/shard_map/reduce_scatter | solution.py:171
  1816.9 1890.3 %reduce-scatter.32.cloned.1.call-start = ((), (), s32[]{:S(2)}) async-start(), calls=%async_computation.15 | async-start | bytes 7987200 | tf_op jit(solution)/shard_map/reduce_scatter | solution.py:182
  1822.9 1884.3 %reduce-scatter.34.cloned.1.call-start = ((), (), s32[]{:S(2)}) async-start(), calls=%async_computation.17 | async-start | bytes 15360000 | tf_op jit(solution)/shard_map/reduce_scatter | solution.py:194
  1829.4 1877.8 %reduce-scatter.36.cloned.1.call-start = ((), (), s32[]{:S(2)}) async-start(), calls=%async_computation.18 | async-start | bytes 26419200 | tf_op jit(solution)/shard_map/reduce_scatter | solution.py:205
  1841.7 3762.5 %all-reduce.44.cloned.1.call-start = ((), (), s32[]{:S(2)}) async-start(), calls=%async_computation.16 | async-start | bytes 409600 | tf_op jit(solution)/shard_map/psum | solution.py:606
  1847.6 3756.6 %all-reduce.50.cloned.1.call-start = ((), (), s32[]{:S(2)}) async-start(), calls=%async_computation.22 | async-start | bytes 266240 | tf_op jit(solution)/shard_map/psum | solution.py:606
  2975.5 547.2 %collective-permute-start.63 = (f32[25,2752]{1,0:T(8,128)S(1)}, f32[25,2752]{1,0:T(8,128)}, u32[]{:S(2)}, u32[]{:S(2)}) collective-permute-start(f32[25,2752]{1,0:T(8,128)S(1)} %slice.600), channel_id=1, source_target_pairs={{0,14},{1,15},{2,16},{3,17},{4,18},{5,19},{6,20},{7,21},{8,22},{9,... | collective-permute-start | bytes 825608
  3707.2 1698.5 %collective-permute-start.46 = (f32[32,3200]{1,0:T(8,128)S(1)}, f32[32,3200]{1,0:T(8,128)S(1)}, u32[]{:S(2)}, u32[]{:S(2)}) collective-permute-start(f32[32,3200]{1,0:T(8,128)S(1)} %get-tuple-element.1221), channel_id=1, source_target_pairs={{0,13},{1,14},{2,15},{3,16},{4,17},{5,18},{6,19},{7,20},{8,21},{9,... | collective-permute-start | bytes 1228808
  3729.9 1678.2 %collective-permute-start.45 = (f32[32,3200]{1,0:T(8,128)S(1)}, f32[32,3200]{1,0:T(8,128)S(1)}, u32[]{:S(2)}, u32[]{:S(2)}) collective-permute-start(f32[32,3200]{1,0:T(8,128)S(1)} %get-tuple-element.1221), channel_id=1, source_target_pairs={{0,12},{1,13},{2,14},{3,15},{4,16},{5,17},{6,18},{7,19},{8,20},{9,... | collective-permute-start | bytes 1228808
  3733.9 1693.5 %collective-permute-start.44 = (f32[32,3200]{1,0:T(8,128)S(1)}, f32[32,3200]{1,0:T(8,128)S(1)}, u32[]{:S(2)}, u32[]{:S(2)}) collective-permute-start(f32[32,3200]{1,0:T(8,128)S(1)} %get-tuple-element.1221), channel_id=1, source_target_pairs={{0,11},{1,12},{2,13},{3,14},{4,15},{5,16},{6,17},{7,18},{8,19},{9,... | collective-permute-start | bytes 1228808
  3746.9 1646.0 %collective-permute-start.65 = (f32[32,2752]{1,0:T(8,128)S(1)}, f32[32,2752]{1,0:T(8,128)}, u32[]{:S(2)}, u32[]{:S(2)}) collective-permute-start(f32[32,2752]{1,0:T(8,128)S(1)} %fusion.4), channel_id=1, source_target_pairs={{0,2},{1,3},{2,4},{3,5},{4,6},{5,7},{6,8},{7,9},{8,10},{9,11},{10,... | collective-permute-start | bytes 1056776
  3748.9 1648.1 %collective-permute-start.64 = (f32[32,2752]{1,0:T(8,128)S(1)}, f32[32,2752]{1,0:T(8,128)}, u32[]{:S(2)}, u32[]{:S(2)}) collective-permute-start(f32[32,2752]{1,0:T(8,128)S(1)} %fusion.4), channel_id=1, source_target_pairs={{0,1},{1,2},{2,3},{3,4},{4,5},{5,6},{6,7},{7,8},{8,9},{9,10},{10,1... | collective-permute-start | bytes 1056776
  5392.8 99.3 %collective-permute-start.43 = (f32[32,3200]{1,0:T(8,128)S(1)}, f32[32,3200]{1,0:T(8,128)S(1)}, u32[]{:S(2)}, u32[]{:S(2)}) collective-permute-start(f32[32,3200]{1,0:T(8,128)S(1)} %get-tuple-element.1221), channel_id=1, source_target_pairs={{0,10},{1,11},{2,12},{3,13},{4,14},{5,15},{6,16},{7,17},{8,18},{9,... | collective-permute-start | bytes 1228808
  5397.0 96.8 %collective-permute-start.42 = (f32[32,3200]{1,0:T(8,128)S(1)}, f32[32,3200]{1,0:T(8,128)}, u32[]{:S(2)}, u32[]{:S(2)}) collective-permute-start(f32[32,3200]{1,0:T(8,128)S(1)} %get-tuple-element.1221), channel_id=1, source_target_pairs={{0,9},{1,10},{2,11},{3,12},{4,13},{5,14},{6,15},{7,16},{8,17},{9,1... | collective-permute-start | bytes 1228808
  5405.7 92.0 %collective-permute-start.41 = (f32[32,3200]{1,0:T(8,128)S(1)}, f32[32,3200]{1,0:T(8,128)}, u32[]{:S(2)}, u32[]{:S(2)}) collective-permute-start(f32[32,3200]{1,0:T(8,128)S(1)} %get-tuple-element.1221), channel_id=1, source_target_pairs={{0,8},{1,9},{2,10},{3,11},{4,12},{5,13},{6,14},{7,15},{8,16},{9,17... | collective-permute-start | bytes 1228808
  5408.1 91.7 %collective-permute-start.40 = (f32[32,3200]{1,0:T(8,128)S(1)}, f32[32,3200]{1,0:T(8,128)}, u32[]{:S(2)}, u32[]{:S(2)}) collective-permute-start(f32[32,3200]{1,0:T(8,128)S(1)} %get-tuple-element.1221), channel_id=1, source_target_pairs={{0,7},{1,8},{2,9},{3,10},{4,11},{5,12},{6,13},{7,14},{8,15},{9,16}... | collective-permute-start | bytes 1228808
  5427.4 76.4 %collective-permute-start.39 = (f32[32,3200]{1,0:T(8,128)S(1)}, f32[32,3200]{1,0:T(8,128)}, u32[]{:S(2)}, u32[]{:S(2)}) collective-permute-start(f32[32,3200]{1,0:T(8,128)S(1)} %get-tuple-element.1221), channel_id=1, source_target_pairs={{0,6},{1,7},{2,8},{3,9},{4,10},{5,11},{6,12},{7,13},{8,14},{9,15},... | collective-permute-start | bytes 1228808
  5492.1 65.1 %collective-permute-start.38 = (f32[32,3200]{1,0:T(8,128)S(1)}, f32[32,3200]{1,0:T(8,128)S(1)}, u32[]{:S(2)}, u32[]{:S(2)}) collective-permute-start(f32[32,3200]{1,0:T(8,128)S(1)} %get-tuple-element.1221), channel_id=1, source_target_pairs={{0,5},{1,6},{2,7},{3,8},{4,9},{5,10},{6,11},{7,12},{8,13},{9,14},{... | collective-permute-start | bytes 1228808
  5493.8 63.4 %collective-permute-start.37 = (f32[32,3200]{1,0:T(8,128)S(1)}, f32[32,3200]{1,0:T(8,128)}, u32[]{:S(2)}, u32[]{:S(2)}) collective-permute-start(f32[32,3200]{1,0:T(8,128)S(1)} %get-tuple-element.1221), channel_id=1, source_target_pairs={{0,4},{1,5},{2,6},{3,7},{4,8},{5,9},{6,10},{7,11},{8,12},{9,13},{1... | collective-permute-start | bytes 1228808
  5497.7 59.5 %collective-permute-start.36 = (f32[32,3200]{1,0:T(8,128)S(1)}, f32[32,3200]{1,0:T(8,128)}, u32[]{:S(2)}, u32[]{:S(2)}) collective-permute-start(f32[32,3200]{1,0:T(8,128)S(1)} %get-tuple-element.1221), channel_id=1, source_target_pairs={{0,3},{1,4},{2,5},{3,6},{4,7},{5,8},{6,9},{7,10},{8,11},{9,12},{10... | collective-permute-start | bytes 1228808
  (245 other events, 8776.1 us)
Sparse Core Ops, SparseCore 0:
  54.6 434.1 all-reduce.45
  602.0 11.5 all-gather.13
  616.9 17.8 all-gather.15
  636.4 19.3 all-gather.17
  657.4 39.3 all-gather.19
  709.4 33.9 all-gather.25
  745.2 26.6 all-gather.21
  876.7 68.4 all-gather.23
  1629.4 47.3 reduce-scatter.29
  1679.3 90.3 all-reduce.47
  1772.2 104.9 reduce-scatter.37
  1883.6 161.2 all-reduce.51
  2047.4 16.7 reduce-scatter.27
  2066.5 17.3 reduce-scatter.31
  2086.3 26.0 reduce-scatter.33
  2114.8 47.6 reduce-scatter.35
  2168.4 142.0 all-reduce.43
  3628.7 287.5 all-reduce.49
where the time goes:
time: 5650 us; the launch traced here: 5620 us
  blocking collectives  3390 us (60%)
  local copies, waits for them, and re-layouts  786 us (14%)
  waiting for transfers between devices  493 us (9%)
  starting transfers between devices  366 us (6%)
  other arithmetic  315 us (6%)
  matrix products  248 us (4%)
    unnamed x4, blocking collectives  3230 us
    unnamed x66, waiting for transfers between devices  447 us
    unnamed x417, local copies, waits for them, and re-layouts  314 us
    unnamed x48, starting transfers between devices  290 us
    all_gather x15, blocking collectives, carried_in(): pieces = jax.tree.map(lambda part: lax.all_gather(part, axis), subtotal)  152 us
    another operation x15, local copies, waits for them, and re-layouts, laid_out(): tiles.reshape(*shape[:dim], shape[dim] * shape[dim + 1], *shape[dim + 2:])  123 us
  transfers between devices with their start and end apart: 96, of which 19 were waited for; matrix products, arithmetic and copies ran while one was open for 44% of the time, Pallas kernels for 0%

commit v1 on v0

v1 whole, which is shorter than its diff:
```python
import functools
import math

import jax
import jax.numpy as jnp
import numpy as np
from jax import lax
from jax.experimental import pallas as pl
from jax.experimental.pallas import tpu as pltpu
from jax.sharding import Mesh
from jax.sharding import PartitionSpec as P

HEADS = 25
KV_HEADS = 5
HEAD_DIM = 64
WINDOW = 1024
RANK = 100
X_RING = ("xh", "xl")
ROWS = ("head", "xh", "y")
EVERY = ("head", "xh", "y", "z", "xl")
Y_RING = "y"
Z_RING = "z"
BLK_SEQ = ("xh", "y", "z", "xl")
HEAD_BLK = ("head", "xh", "y", "z")
EPSILON = 1e-06
LOG2_E = 1.0 / math.log(2.0)
FF_PAD = 88


def received(a, axis, d):
    n = lax.axis_size(axis)
    return lax.ppermute(a, axis, [((i + d) % n, i) for i in range(n)])


def other_core(a):
    return received(a, "head", 1)


def shifted(a, distance, axis=HEAD_BLK):
    n = lax.axis_size(axis)
    return lax.ppermute(a, axis, [(i - distance, i) for i in range(n) if 0 <= i - distance < n])


def after(value, *others):
    return lax.optimization_barrier((value, *others))[0]


def dealt(blocks, axis):
    return lax.all_to_all(blocks, axis, 0, 0, tiled=True)


def shown(a, axis):
    return dealt(jnp.broadcast_to(a[None], (lax.axis_size(axis), *a.shape)), axis)


def summed(blocks, axis):
    return jnp.sum(dealt(blocks, axis).astype(jnp.float32), axis=0)


ORDER_A = (("y", "z"), X_RING)
ORDER_B = (("xh", "z", "xl"), Y_RING)
ORDER_C = (("xh", "y", "xl"), Z_RING)


def ring_pieces(a, axis):
    half = a.shape[0] // 2
    up, down = received(a, axis, 1), received(a, axis, -1)
    return [a, up, received(up[:half], axis, 1), received(down[half:], axis, -1), down]


def in_order(pieces, axis):
    own, up, far_low, far_high, down = pieces
    me = lax.axis_index(axis)
    out = jnp.zeros((4, *own.shape), own.dtype)
    out = lax.dynamic_update_index_in_dim(out, own, me, 0)
    out = lax.dynamic_update_index_in_dim(out, up, lax.rem(me + 1, 4), 0)
    out = lax.dynamic_update_index_in_dim(out, down, lax.rem(me + 3, 4), 0)
    far = lax.rem(me + 2, 4)
    out = lax.dynamic_update_slice(out, far_low[None], (far, 0, 0))
    out = lax.dynamic_update_slice(out, far_high[None], (far, far_low.shape[0], 0))
    return out.reshape(4 * own.shape[0], own.shape[1])


def ring_whole(a, axis):
    return jnp.concatenate([a] + [received(a, axis, j) for j in (1, 2, 3)], axis=0)


def ring_in_order(a, axis):
    me = lax.axis_index(axis)
    out = jnp.zeros((4, *a.shape), a.dtype)
    for j, part in enumerate([a] + [received(a, axis, j) for j in (1, 2, 3)]):
        out = lax.dynamic_update_index_in_dim(out, part, lax.rem(me + j, 4), 0)
    return out.reshape(4 * a.shape[0], a.shape[1])


def plane(shard, order):
    return shown(shard, order[0]).reshape(16 * shard.shape[0], shard.shape[1])


def ring_sum(pieces, axis):
    own, up, far_low, far_high, down = pieces
    half = far_low.shape[0]
    low = own.dtype
    from_down, from_up = received(far_low, axis, -1), received(far_high, axis, 1)
    to_up = jnp.concatenate(
        [(up[:half].astype(jnp.float32) + from_down.astype(jnp.float32)).astype(low), up[half:]]
    )
    to_down = jnp.concatenate(
        [down[:half], (down[half:].astype(jnp.float32) + from_up.astype(jnp.float32)).astype(low)]
    )
    return (
        own.astype(jnp.float32)
        + received(to_up, axis, -1).astype(jnp.float32)
        + received(to_down, axis, 1).astype(jnp.float32)
    )


def ring_sum_whole(whole, axis):
    rows = whole.shape[0] // 4
    total = whole[:rows].astype(jnp.float32)
    for j in (1, 2, 3):
        total = total + received(whole[j * rows : (j + 1) * rows], axis, -j).astype(jnp.float32)
    return total


def plane_sum(whole, order, rows):
    return summed(to_low(whole).reshape(16, rows, whole.shape[1]), order[0])


def turned_pieces(whole, axis):
    rows = whole.shape[0] // 4
    blocks = whole.reshape(4, rows, whole.shape[1])
    me = lax.axis_index(axis)

    def block(j):
        return lax.dynamic_index_in_dim(blocks, lax.rem(me + j, 4), 0, keepdims=False)

    far = block(2)
    return [block(0), block(1), far[: rows // 2], far[rows // 2 :], block(3)]


def ring_sum_in_order(whole, axis):
    rows = whole.shape[0] // 4
    blocks = whole.reshape(4, rows, whole.shape[1])
    me = lax.axis_index(axis)
    total = 0.0
    for j in range(4):
        block = lax.dynamic_index_in_dim(blocks, lax.rem(me + j, 4), 0, keepdims=False)
        total = total + (received(block, axis, -j) if j else block).astype(jnp.float32)
    return total


def picker(order, rows):
    ring, inside = np.indices((4, 16 * rows))
    turned = lax.rem(lax.axis_index(order[1]) + jnp.asarray(ring, jnp.int32), 4)
    block, row = inside // rows, jnp.asarray(inside % rows, jnp.int32)
    if order is ORDER_A:
        xh, y, z, xl = turned // 2, block // 4, block % 4, turned % 2
    elif order is ORDER_B:
        xh, y, z, xl = block // 8, turned, block // 2 % 4, block % 2
    else:
        xh, y, z, xl = block // 8, block // 2 % 4, turned, block % 2
    return ((((xh * 4 + y) * 4 + z) * 2 + xl) * rows + row).reshape(-1)


def ff_picker(rows):
    y, x, z, row = (jnp.asarray(j, jnp.int32) for j in np.indices((4, 4, 4, rows)))
    y = lax.rem(lax.axis_index(Y_RING) + y, 4)
    x = lax.rem(lax.axis_index(X_RING) + x, 4)
    return (((((x // 2) * 4 + y) * 4 + z) * 2 + x % 2) * rows + row).reshape(-1)


def one_hot(index, rows):
    return (jnp.arange(rows, dtype=jnp.int32)[:, None] == index[None, :]).astype(jnp.bfloat16)


def piece_bounds(total):
    k = total // 8
    return [(0, 2 * k), (2 * k, 4 * k), (4 * k, 5 * k), (5 * k, 6 * k), (6 * k, 8 * k)]


def by_pieces(left, pieces):
    total = 0.0
    for (start, stop), piece in zip(piece_bounds(left.shape[1]), pieces):
        total = total + product(left[:, start:stop], piece)
    return total


def by_pieces_nt(left, pieces):
    return jnp.concatenate([product_nt(left, piece) for piece in pieces], axis=1)


def grad_pieces(left, right):
    return [to_low(product_tn(left[:, start:stop], right)) for start, stop in piece_bounds(left.shape[1])]


def to_channels(a):
    lead, width = a.shape[:-1], a.shape[-1]
    return lax.optimization_barrier(
        jnp.swapaxes(a.reshape(*lead, 2, 16, 2, width // 64), -3, -2).reshape(*lead, width)
    )


def from_channels(a):
    lead, width = a.shape[:-1], a.shape[-1]
    a = lax.optimization_barrier(a)
    return jnp.swapaxes(a.reshape(*lead, 2, 2, 16, width // 64), -3, -2).reshape(*lead, width)


def join_columns(mine, got):
    first = lax.axis_index("head") == 0
    return jnp.concatenate([jnp.where(first, mine, got), jnp.where(first, got, mine)], axis=1)


def own_tokens(both):
    rows = both.shape[0] // 2
    return join_columns(both[:rows], other_core(both[rows:]))


def own_columns(a):
    first = lax.axis_index("head") == 0
    low, high = jnp.split(a, 2, axis=1)
    mine, theirs = jnp.where(first, low, high), jnp.where(first, high, low)
    return jnp.concatenate([mine, other_core(theirs)], axis=0)


def both_tokens(a):
    return jnp.concatenate([a, other_core(a)], axis=0)


def sum_cores(both):
    rows = both.shape[0] // 2
    return both[:rows] + other_core(to_low(both[rows:])).astype(jnp.float32)


def chain_kernel(reverse, packed_ref, rate_ref, out_ref):
    rate = rate_ref[...] * LOG2_E
    count, states = packed_ref.shape[0], rate.shape[0]

    def one(k, state):
        p = count - 1 - k if reverse else k
        out_ref[p] = state
        packed = packed_ref[p].astype(jnp.float32)
        total = packed[states : states + 1] + packed[states + 1 : states + 2]
        return jnp.exp2(total * rate) * state + packed[:states]

    lax.fori_loop(0, count, one, jnp.zeros(rate.shape, jnp.float32))


def chain_carry(total_step, state, decay_rate, reverse):
    count = lax.axis_size(HEAD_BLK)
    states, channels = state.shape
    high = lax.reduce_precision(total_step, 8, 7)
    packed = jnp.concatenate([state, high[None], (total_step - high)[None]]).astype(jnp.bfloat16)

    def tiles(a):
        padded = jnp.pad(a, ((0, 0), (0, count * 128 - channels)))
        return padded.reshape(a.shape[0], count, 128).transpose(1, 0, 2)

    rate = lax.dynamic_index_in_dim(tiles(decay_rate), lax.axis_index(HEAD_BLK), 0, keepdims=False)
    chained = pl.pallas_call(
        functools.partial(chain_kernel, reverse),
        out_shape=jax.ShapeDtypeStruct((count, states, 128), jnp.float32),
    )(dealt(tiles(packed), HEAD_BLK), rate)
    got = dealt(to_low(chained), HEAD_BLK)[: channels // 128]
    return got.transpose(1, 0, 2).reshape(states, channels).astype(jnp.float32)


def sum_all(values):
    count = lax.axis_size(EVERY)
    lines = values.reshape(-1, 128)
    each = -(-lines.shape[0] // count)
    padded = jnp.pad(lines, ((0, count * each - lines.shape[0]), (0, 0)))
    mine = summed(padded.reshape(count, each, 128), EVERY)
    return shown(mine, EVERY).reshape(-1, 128)[: lines.shape[0]].reshape(values.shape)


def rms_scale(values, gain):
    return values * lax.rsqrt(jnp.mean(values * values, axis=-1, keepdims=True) + EPSILON) * gain


def to_low(values):
    return values.astype(jnp.bfloat16)


def product(left, right):
    return jnp.dot(left, right, preferred_element_type=jnp.float32)


def product_tn(left, right):
    return lax.dot_general(
        left, right, (((0,), (0,)), ((), ())), preferred_element_type=jnp.float32
    )


def product_nt(left, right):
    return lax.dot_general(
        left, right, (((1,), (1,)), ((), ())), preferred_element_type=jnp.float32
    )


def chain_combine(earlier, later):
    return (earlier[0] * later[0], later[0] * earlier[1] + later[1])


def conv_silu(padded, conv_weight, conv_bias):
    tap_count = conv_weight.shape[0]
    length = padded.shape[0] - tap_count + 1
    total_sum = conv_bias
    for tap_index in range(tap_count):
        total_sum = total_sum + conv_weight[tap_index] * padded[tap_index : tap_index + length]
    return jax.nn.silu(total_sum)


def rate_piece(step_pre, step_bias, log_decay):
    return (jax.nn.softplus(step_pre + step_bias), -jnp.exp(log_decay))


def gate_piece(scan_out, conv_values, gate_z, skip_gain):
    return (scan_out + skip_gain * conv_values) * jax.nn.silu(gate_z)


def merge_piece(tokens, attn_out, mamba_out, attn_gain, mamba_gain):
    return tokens + 0.5 * (rms_scale(attn_out, attn_gain) + rms_scale(mamba_out, mamba_gain))


def swiglu(gate_val, up_val):
    return jax.nn.silu(gate_val) * up_val


def group_scores(queries, window_keys, allowed, group_index, group_size, score_scale):
    query_part = queries[
        :, group_index * group_size * HEAD_DIM : (group_index + 1) * group_size * HEAD_DIM
    ].reshape(queries.shape[0], group_size, HEAD_DIM)
    key_part = window_keys[:, group_index * HEAD_DIM : (group_index + 1) * HEAD_DIM]
    raw_scores = (
        jnp.einsum("qgd,sd->gqs", query_part, key_part, preferred_element_type=jnp.float32)
        * score_scale
    )
    return (jnp.where(allowed[None], raw_scores, -1e30), query_part, key_part)


SCAN_TILE = 640


def scan_state_kernel(step_ref, drive_ref, in_ref, rate_ref, end_ref):
    rate = rate_ref[...] * LOG2_E
    width = rate.shape[1]

    def eight(k, state):
        base = pl.multiple_of(k * 8, 8)
        step, drive = step_ref[pl.ds(base, 8), :], drive_ref[pl.ds(base, 8), :]
        for i in range(8):
            decay = jnp.exp2(step[i : i + 1] * rate)
            in_now = jnp.tile(in_ref[base + i], (1, width // 128))
            state = decay * state + in_now * drive[i : i + 1]
        return state

    end_ref[...] = lax.fori_loop(0, step_ref.shape[0] // 8, eight, jnp.zeros(rate.shape, jnp.float32))


def scan_full_kernel(step_ref, drive_ref, in_ref, out_ref, rate_ref, start_ref, y_ref):
    rate = rate_ref[...] * LOG2_E
    width = rate.shape[1]

    def eight(k, state):
        base = pl.multiple_of(k * 8, 8)
        step, drive = step_ref[pl.ds(base, 8), :], drive_ref[pl.ds(base, 8), :]
        rows = []
        for i in range(8):
            decay = jnp.exp2(step[i : i + 1] * rate)
            in_now = jnp.tile(in_ref[base + i], (1, width // 128))
            out_now = jnp.tile(out_ref[base + i], (1, width // 128))
            state = decay * state + in_now * drive[i : i + 1]
            rows.append(jnp.sum(out_now * state, axis=0, keepdims=True))
        y_ref[pl.ds(base, 8), :] = jnp.concatenate(rows, axis=0)
        return state

    lax.fori_loop(0, step_ref.shape[0] // 8, eight, start_ref[...])


def adjoint_state_kernel(step_ref, d_scan_ref, out_ref, rate_ref, d_start_ref):
    rate = rate_ref[...] * LOG2_E
    width = rate.shape[1]
    blocks = step_ref.shape[0] // 8

    def eight(k, carry):
        base = pl.multiple_of((blocks - 1 - k) * 8, 8)
        step, d_scan = step_ref[pl.ds(base, 8), :], d_scan_ref[pl.ds(base, 8), :]
        for i in range(7, -1, -1):
            out_now = jnp.tile(out_ref[base + i], (1, width // 128))
            carry = jnp.exp2(step[i : i + 1] * rate) * (out_now * d_scan[i : i + 1] + carry)
        return carry

    d_start_ref[...] = lax.fori_loop(0, blocks, eight, jnp.zeros(rate.shape, jnp.float32))


def scan_back_kernel(
    step_ref,
    conv_ref,
    d_scan_ref,
    in_ref,
    out_ref,
    rate_ref,
    start_ref,
    d_end_ref,
    d_step_ref,
    d_conv_ref,
    d_rate_ref,
    d_in_ref,
    d_out_ref,
    states_ref,
    decays_ref,
):
    true_rate = rate_ref[...]
    rate = true_rate * LOG2_E
    width = rate.shape[1]
    tiles = width // 128
    blocks = step_ref.shape[0] // 8

    @pl.when(pl.program_id(0) == 0)
    def _():
        d_in_ref[...] = jnp.zeros(d_in_ref.shape, jnp.float32)
        d_out_ref[...] = jnp.zeros(d_out_ref.shape, jnp.float32)

    def folded(a):
        total = a[:, :128]
        for j in range(1, tiles):
            total = total + a[:, j * 128 : (j + 1) * 128]
        return total

    states_ref[0] = start_ref[...]

    def forward(k, state):
        base = pl.multiple_of(k * 8, 8)
        step, conv = step_ref[pl.ds(base, 8), :], conv_ref[pl.ds(base, 8), :]
        d_scan = d_scan_ref[pl.ds(base, 8), :]
        drive = step * conv
        for i in range(8):
            decay = jnp.exp2(step[i : i + 1] * rate)
            in_now = jnp.tile(in_ref[base + i], (1, tiles))
            state = decay * state + in_now * drive[i : i + 1]
            decays_ref[base + i] = decay
            states_ref[base + i + 1] = state
            d_out_ref[base + i] += folded(d_scan[i : i + 1] * state)
        return state

    lax.fori_loop(0, blocks, forward, start_ref[...])

    def backward(k, carried):
        carry, d_rate = carried
        base = pl.multiple_of((blocks - 1 - k) * 8, 8)
        step, conv = step_ref[pl.ds(base, 8), :], conv_ref[pl.ds(base, 8), :]
        d_scan = d_scan_ref[pl.ds(base, 8), :]
        drive = step * conv
        through_rate, through_drive = [], []
        for i in range(7, -1, -1):
            in_now = jnp.tile(in_ref[base + i], (1, tiles))
            out_now = jnp.tile(out_ref[base + i], (1, tiles))
            adjoint = out_now * d_scan[i : i + 1] + carry
            carry = decays_ref[base + i] * adjoint
            before = carry * states_ref[base + i]
            d_rate = d_rate + before * step[i : i + 1]
            through_rate.append(jnp.sum(true_rate * before, axis=0, keepdims=True))
            through_drive.append(jnp.sum(adjoint * in_now, axis=0, keepdims=True))
            d_in_ref[base + i] += folded(adjoint * drive[i : i + 1])
        by_rate = jnp.concatenate(through_rate[::-1], axis=0)
        by_drive = jnp.concatenate(through_drive[::-1], axis=0)
        d_step_ref[pl.ds(base, 8), :] = by_rate + by_drive * conv
        d_conv_ref[pl.ds(base, 8), :] = by_drive * step
        return carry, d_rate

    zero = jnp.zeros(rate.shape, jnp.float32)
    d_rate_ref[...] = lax.fori_loop(0, blocks, backward, (d_end_ref[...], zero))[1]


def scan_specs(rows, states):
    tokens = pl.BlockSpec((rows, SCAN_TILE), lambda i: (0, i))
    maps = pl.BlockSpec((rows, states, 128), lambda i: (0, 0, 0))
    state = pl.BlockSpec((states, SCAN_TILE), lambda i: (0, i))
    return tokens, maps, state


def scan_call(kernel, operands, in_kinds, outs, out_kinds, scratch=(), flops=8, exps=1):
    rows, channels = operands[0].shape
    states = 16
    kinds = dict(zip("tms", scan_specs(rows, states)))
    shapes = {"t": (rows, channels), "m": (rows, states, 128), "s": (states, channels)}
    work = rows * states * channels
    return pl.pallas_call(
        kernel,
        grid=(channels // SCAN_TILE,),
        in_specs=[kinds[k] for k in in_kinds],
        out_specs=[kinds[k] for k in out_kinds],
        out_shape=[jax.ShapeDtypeStruct(shapes[k], jnp.float32) for k in out_kinds],
        scratch_shapes=scratch,
        compiler_params=pltpu.CompilerParams(
            dimension_semantics=("arbitrary",), vmem_limit_bytes=(36 if scratch else 16) * 2**20
        ),
        cost_estimate=pl.CostEstimate(
            flops=work * flops, bytes_accessed=4 * rows * channels * 4, transcendentals=work * exps
        ),
    )(*operands)


def lanes(a):
    return jnp.broadcast_to(a[:, :, None], (*a.shape, 128))


def scan_state(step_size, drive, in_lanes, decay_rate):
    return scan_call(scan_state_kernel, (step_size, drive, in_lanes, decay_rate), "ttms", 1, "s")[0]


def scan_full(step_size, drive, in_lanes, out_lanes, decay_rate, state_in):
    operands = (step_size, drive, in_lanes, out_lanes, decay_rate, state_in)
    return scan_call(scan_full_kernel, operands, "ttmmss", 1, "t")[0]


def adjoint_state(step_size, d_scan, out_lanes, decay_rate):
    return scan_call(adjoint_state_kernel, (step_size, d_scan, out_lanes, decay_rate), "ttms", 1, "s")[0]


def scan_back(step_size, conv_values, d_scan, in_lanes, out_lanes, decay_rate, state_in, d_end):
    rows, states = step_size.shape[0], decay_rate.shape[0]
    scratch = (
        pltpu.VMEM((rows + 1, states, SCAN_TILE), jnp.float32),
        pltpu.VMEM((rows, states, SCAN_TILE), jnp.float32),
    )
    operands = (step_size, conv_values, d_scan, in_lanes, out_lanes, decay_rate, state_in, d_end)
    d_step, d_conv, d_rate, d_in, d_out = scan_call(
        scan_back_kernel, operands, "tttmmsss", 5, "ttsmm", scratch, flops=24
    )
    return d_step, d_conv, d_rate, jnp.sum(d_in, axis=-1), jnp.sum(d_out, axis=-1)


def shards(
    inputs,
    segment_ids,
    out_grad,
    norm_gain,
    w_query,
    w_key,
    w_value,
    w_attn_out,
    w_mamba_in,
    conv_weight,
    conv_bias,
    w_select,
    w_step,
    step_bias,
    log_decay,
    skip_gain,
    w_mamba_out,
    attn_gain,
    mamba_gain,
    ffn_norm_gain,
    w_gate,
    w_up,
    w_down,
):
    rows_dev, width = inputs.shape[1:]
    inner = conv_weight.shape[1]
    edge_count = conv_weight.shape[0] - 1
    rank_width = RANK
    state_width = log_decay.shape[0]
    reach_blocks = WINDOW // rows_dev
    group_size = HEADS // KV_HEADS
    score_scale = 1.0 / math.sqrt(HEAD_DIM)
    position = lax.axis_index(HEAD_BLK)
    core = lax.axis_index("head")
    first_core = core == 0
    tokens = inputs[0].astype(jnp.float32)

    conv_weight, conv_bias, step_bias, log_decay, skip_gain = (
        to_channels(v) for v in (conv_weight, conv_bias, step_bias, log_decay, skip_gain)
    )

    d_rows = w_query.shape[0]
    c_rows = w_select.shape[0]
    sel_half, step_half = w_select.shape[1], w_step.shape[1]
    mamba_in = to_channels(w_mamba_in)
    cut_a, cut_b = 1024, 2176
    plane_b = plane(mamba_in[:, cut_a:cut_b], ORDER_B)
    in_b = ring_pieces(plane_b, ORDER_B[1])
    plane_a = plane(after(mamba_in[:, :cut_a], plane_b), ORDER_A)
    in_a = ring_pieces(plane_a, ORDER_A[1])
    plane_c = plane(after(mamba_in[:, cut_b:], plane_a), ORDER_C)
    in_c = ring_pieces(plane_c, ORDER_C[1])
    select_step = jnp.pad(
        jnp.concatenate([w_select, w_step], axis=1), ((0, 0), (0, 128 - sel_half - step_half))
    )
    select_mine = shown(after(select_step, plane_c), ("xh", "xl", "y", "z")).reshape(inner, 128)
    select_got = other_core(select_mine)
    select_full = join_columns(select_mine[:, :sel_half], select_got[:, :sel_half])
    step_full = join_columns(
        select_mine[:, sel_half : sel_half + step_half], select_got[:, sel_half : sel_half + step_half]
    )

    plane_out_a = plane(after(w_mamba_out, select_mine), ORDER_A)
    mamba_out_a = in_order(ring_pieces(plane_out_a, ORDER_A[1]), ORDER_A[1])
    qkv_shard = jnp.concatenate([w_query, w_key, w_value], axis=1)
    plane_qkv = plane(after(qkv_shard, plane_out_a), ORDER_C)
    qkv_c = ring_pieces(plane_qkv, ORDER_C[1])
    plane_out_b = plane(after(w_attn_out, plane_qkv), ORDER_B)
    attn_out_b = ring_pieces(plane_out_b, ORDER_B[1])

    ff_rows = w_down.shape[0]

    def to_units(w):
        split = w.reshape(d_rows, 4, 4, 2, ff_rows).transpose(2, 0, 3, 1, 4)
        return jnp.pad(split, ((0, 0),) * 4 + ((0, FF_PAD - ff_rows),)).reshape(4, d_rows, 8 * FF_PAD)

    def from_units(g):
        split = g.reshape(4, d_rows, 2, 4, FF_PAD)[..., :ff_rows]
        return split.transpose(1, 3, 0, 2, 4).reshape(d_rows, 32 * ff_rows)

    units = 8 * FF_PAD
    gate_up = jnp.concatenate([to_units(w_gate), to_units(w_up)], axis=2)
    gate_up = dealt(after(gate_up, plane_out_b), Z_RING).reshape(4 * d_rows, 2 * units)
    gate_up = ring_pieces(ring_whole(gate_up, X_RING), Y_RING)
    down_cols = jnp.pad(after(w_down, plane_c), ((0, FF_PAD - ff_rows), (0, 0)))
    down_cols = in_order(ring_pieces(ring_in_order(down_cols, Y_RING), X_RING), X_RING)
    down_low, down_high = down_cols[:units], down_cols[units:]
    down_mine = jnp.where(first_core, down_low, down_high)
    down_theirs = jnp.where(first_core, down_high, down_low)
    down = join_columns(down_mine, other_core(down_theirs))

    def group_tokens(a):
        return both_tokens(ring_whole(a, Z_RING))

    def group_sum(both):
        return ring_sum_whole(to_low(sum_cores(both)), Z_RING)

    grad_out = out_grad[0]
    grad_out_group = group_tokens(after(grad_out, plane_c))

    pick_a, pick_b, pick_c = (
        one_hot(picker(order, d_rows), width) for order in (ORDER_A, ORDER_B, ORDER_C)
    )
    pick_ff = one_hot(ff_picker(d_rows), width)

    def permuted(a, hot):
        return to_low(product(a, hot))

    normed, norm_back = jax.vjp(rms_scale, tokens, norm_gain)
    normed_low = to_low(normed)
    normed_chip = both_tokens(normed_low)
    normed_a, normed_b, normed_c = (permuted(normed_chip, hot) for hot in (pick_a, pick_b, pick_c))

    mixed_half = jnp.concatenate(
        [by_pieces(normed_a, in_a), by_pieces(normed_b, in_b), by_pieces(normed_c, in_c)], axis=1
    )
    mixed_mine = mixed_half[:rows_dev]
    mixed_got = other_core(to_low(mixed_half[rows_dev:]))
    conv_in = jnp.where(first_core, to_low(mixed_mine), mixed_got)
    gate_z = jnp.where(first_core, mixed_got.astype(jnp.float32), mixed_mine)

    qkv_half = to_low(by_pieces(normed_c, qkv_c))
    q_cols, k_cols = w_query.shape[1], w_key.shape[1]
    qkv_mine, qkv_got = qkv_half[:rows_dev], other_core(qkv_half[rows_dev:])
    queries = join_columns(qkv_mine[:, :q_cols], qkv_got[:, :q_cols])
    keys_low = join_columns(qkv_mine[:, q_cols : q_cols + k_cols], qkv_got[:, q_cols : q_cols + k_cols])
    values_low = join_columns(qkv_mine[:, q_cols + k_cols :], qkv_got[:, q_cols + k_cols :])

    edge_rows = shifted(conv_in[rows_dev - edge_count :], 1)
    key_value = jnp.concatenate([keys_low, values_low], axis=1)
    along_z = lax.axis_index(Z_RING)
    kv_cols = KV_HEADS * HEAD_DIM
    row = ring_in_order(key_value, Z_RING).reshape(4, rows_dev, 2 * kv_cols)
    window = jnp.concatenate([shifted(row, 2, ROWS), shifted(row, 1, ROWS), row])
    window = lax.dynamic_slice_in_dim(window, along_z, reach_blocks + 1).reshape(-1, key_value.shape[1])
    window_keys, window_values = window[:, :kv_cols], window[:, kv_cols:]

    padded_in = jnp.concatenate([edge_rows, conv_in], axis=0).astype(jnp.float32)
    conved, conv_back = jax.vjp(conv_silu, padded_in, conv_weight, conv_bias)
    conved_low = to_low(conved)
    conv_values = conved_low.astype(jnp.float32)
    selected = product(conved_low, select_full)
    step_raw = to_low(selected[:, :rank_width])
    in_mat = selected[:, rank_width : rank_width + state_width]
    out_mat = selected[:, rank_width + state_width :]
    step_pre = product_nt(step_raw, step_full)
    (step_size, decay_rate), rate_back = jax.vjp(rate_piece, step_pre, step_bias, log_decay)
    total_step = jnp.sum(step_size, axis=0)
    drive = step_size * conv_values
    in_lanes, out_lanes = lanes(in_mat), lanes(out_mat)
    end_state = scan_state(step_size, drive, in_lanes, decay_rate)
    state_in = chain_carry(total_step, end_state, decay_rate, False)
    scan_out = scan_full(step_size, drive, in_lanes, out_lanes, decay_rate, state_in)
    gated, gate_back = jax.vjp(gate_piece, scan_out, conv_values, gate_z, skip_gain)
    gated_low = to_low(gated)

    span_keys = (reach_blocks + 1) * rows_dev
    segment_row = segment_ids[0]
    padded_segs = jnp.concatenate(
        [jnp.full((reach_blocks * rows_dev,), -1, jnp.int32), segment_row]
    )
    key_segs = lax.dynamic_slice_in_dim(padded_segs, position * rows_dev, span_keys)
    query_segs = lax.dynamic_slice_in_dim(segment_row, position * rows_dev, rows_dev)
    gaps = (reach_blocks * rows_dev + jnp.arange(rows_dev, dtype=jnp.int32))[:, None] - jnp.arange(
        span_keys, dtype=jnp.int32
    )[None, :]
    allowed = (gaps >= 0) & (gaps < WINDOW) & (query_segs[:, None] == key_segs[None, :])
    head_outputs = []
    log_totals = []
    for group_index in range(KV_HEADS):
        scores, query_part, key_part = group_scores(
            queries, window_keys, allowed, group_index, group_size, score_scale
        )
        row_max = jnp.max(scores, axis=-1, keepdims=True)
        exp_scores = jnp.exp(scores - row_max)
        row_total = jnp.sum(exp_scores, axis=-1, keepdims=True)
        log_totals.append(row_max + jnp.log(row_total))
        weights_low = to_low(exp_scores / row_total)
        value_part = window_values[:, group_index * HEAD_DIM : (group_index + 1) * HEAD_DIM]
        head_outputs.append(
            jnp.einsum(
                "gqs,sd->qgd", weights_low, value_part, preferred_element_type=jnp.float32
            ).reshape(rows_dev, group_size * HEAD_DIM)
        )
    heads_low = to_low(jnp.concatenate(head_outputs, axis=1))

    heads_b = both_tokens(permuted(heads_low, pick_b))
    gated_chip = both_tokens(gated_low)
    branch_out = jnp.concatenate([by_pieces(heads_b, attn_out_b), product(gated_chip, mamba_out_a)], axis=1)
    half_width = width // 2
    out_mine, out_got = branch_out[:rows_dev], other_core(branch_out[rows_dev:])
    attn_out = join_columns(out_mine[:, :half_width], out_got[:, :half_width])
    mamba_out = join_columns(out_mine[:, half_width:], out_got[:, half_width:])
    hidden_mid, merge_back = jax.vjp(
        merge_piece, tokens, attn_out, mamba_out, attn_gain, mamba_gain
    )
    normed_two, norm_two_back = jax.vjp(rms_scale, hidden_mid, ffn_norm_gain)
    normed_two_ff = group_tokens(permuted(to_low(normed_two), pick_ff))
    gate_up_val = by_pieces(normed_two_ff, gate_up)
    act_val, act_back = jax.vjp(swiglu, gate_up_val[:, :units], gate_up_val[:, units:])
    act_low = to_low(act_val)
    d_act = product_nt(grad_out_group, down)
    d_gate, d_up = act_back(d_act)
    d_gate_up = jnp.concatenate([to_low(d_gate), to_low(d_up)], axis=1)
    d_normed_two = group_sum(by_pieces_nt(d_gate_up, gate_up))
    grad_gate_up = grad_pieces(normed_two_ff, d_gate_up)
    grad_down = to_low(product_tn(act_low, grad_out_group))
    output = to_low(hidden_mid + group_sum(product(act_low, down)))[None]

    gate_up_sum = ring_sum_whole(to_low(ring_sum(grad_gate_up, Y_RING)), X_RING)
    gate_up_sum = dealt(to_low(gate_up_sum).reshape(4, d_rows, 2 * units), Z_RING).astype(jnp.float32)
    grad_gate, grad_up = from_units(gate_up_sum[..., :units]), from_units(gate_up_sum[..., units:])
    down_l, down_r = jnp.split(grad_down, 2, axis=1)
    down_mine = jnp.where(first_core, down_l, down_r)
    down_got = other_core(jnp.where(first_core, down_r, down_l))
    grad_down = jnp.concatenate(
        [jnp.where(first_core, down_mine, down_got), jnp.where(first_core, down_got, down_mine)], axis=0
    )
    grad_down = to_low(ring_sum(turned_pieces(grad_down, X_RING), X_RING))
    grad_down = ring_sum_in_order(grad_down, Y_RING)[:ff_rows]

    def unpermuted(a, hot):
        high = lax.reduce_precision(a, 8, 7)
        return product_nt(to_low(high), hot) + product_nt(to_low(a - high), hot)

    d_mid_norm, grad_ffn_norm = norm_two_back(unpermuted(d_normed_two, pick_ff))
    d_mid = grad_out.astype(jnp.float32) + d_mid_norm
    d_tokens_res, d_attn_out, d_mamba_out, grad_attn_gain, grad_mamba_gain = merge_back(d_mid)
    d_attn_low, d_mamba_low = to_low(d_attn_out), to_low(d_mamba_out)
    d_branch = jnp.concatenate(
        [d_attn_low[:, :half_width], d_mamba_low[:, :half_width], d_attn_low[:, half_width:], d_mamba_low[:, half_width:]],
        axis=1,
    )
    d_branch_half = own_columns(d_branch)
    d_attn_half, d_mamba_half = d_branch_half[:, :half_width], d_branch_half[:, half_width:]
    d_gated = sum_cores(product_nt(d_mamba_half, mamba_out_a))
    d_heads_b = sum_cores(by_pieces_nt(d_attn_half, attn_out_b))
    d_heads = to_low(product_nt(to_low(d_heads_b), pick_b))
    grad_attn_out = plane_sum(ring_sum(grad_pieces(heads_b, d_attn_half), ORDER_B[1]), ORDER_B, d_rows)
    grad_mamba_out = turned_pieces(to_low(product_tn(gated_chip, d_mamba_half)), ORDER_A[1])
    grad_mamba_out = plane_sum(ring_sum(grad_mamba_out, ORDER_A[1]), ORDER_A, c_rows)

    query_grads = []
    key_grads = []
    value_grads = []
    for group_index in range(KV_HEADS):
        scores, query_part, key_part = group_scores(
            queries, window_keys, allowed, group_index, group_size, score_scale
        )
        weights_now = jnp.exp(scores - log_totals[group_index])
        weights_low = to_low(weights_now)
        value_part = window_values[:, group_index * HEAD_DIM : (group_index + 1) * HEAD_DIM]
        head_grad = d_heads[
            :, group_index * group_size * HEAD_DIM : (group_index + 1) * group_size * HEAD_DIM
        ].reshape(rows_dev, group_size, HEAD_DIM)
        d_weights = jnp.einsum(
            "qgd,sd->gqs", head_grad, value_part, preferred_element_type=jnp.float32
        )
        d_scores = to_low(
            weights_now * (d_weights - jnp.sum(weights_now * d_weights, axis=-1, keepdims=True))
        )
        query_grads.append(
            jnp.einsum(
                "gqs,sd->qgd", d_scores, key_part, preferred_element_type=jnp.float32
            ).reshape(rows_dev, group_size * HEAD_DIM)
            * score_scale
        )
        key_grads.append(
            jnp.einsum("gqs,qgd->sd", d_scores, query_part, preferred_element_type=jnp.float32)
            * score_scale
        )
        value_grads.append(
            jnp.einsum("gqs,qgd->sd", weights_low, head_grad, preferred_element_type=jnp.float32)
        )
    d_queries = to_low(jnp.concatenate(query_grads, axis=1))
    d_window = jnp.concatenate(key_grads + value_grads, axis=1)
    d_rows_z = jnp.zeros((12, rows_dev, d_window.shape[1]), jnp.bfloat16)
    d_rows_z = lax.dynamic_update_slice_in_dim(
        d_rows_z, to_low(d_window).reshape(reach_blocks + 1, rows_dev, -1), along_z, 0
    )
    d_row = (
        d_rows_z[8:].astype(jnp.float32)
        + shifted(d_rows_z[4:8], -1, ROWS).astype(jnp.float32)
        + shifted(d_rows_z[:4], -2, ROWS).astype(jnp.float32)
    )
    d_key_value = ring_sum_in_order(to_low(d_row).reshape(4 * rows_dev, 2 * kv_cols), Z_RING)
    d_keys, d_values = to_low(d_key_value[:, :kv_cols]), to_low(d_key_value[:, kv_cols:])

    d_scan, d_conv_gate, d_gate_z, grad_skip = gate_back(d_gated)
    d_state_in = adjoint_state(step_size, d_scan, out_lanes, decay_rate)
    d_end = chain_carry(total_step, d_state_in, decay_rate, True)
    d_step, d_conv_scan, d_rate, d_in_mat, d_out_mat = scan_back(
        step_size, conv_values, d_scan, in_lanes, out_lanes, decay_rate, state_in, d_end
    )
    d_step_pre, grad_step_bias, grad_log_decay = rate_back((d_step, d_rate))
    d_step_low = to_low(d_step_pre)
    grad_step_w = product_tn(d_step_low, step_raw)
    d_step_raw = product(d_step_low, step_full)
    d_selected = to_low(jnp.concatenate([d_step_raw, d_in_mat, d_out_mat], axis=1))
    grad_select = product_tn(conved_low, d_selected)
    d_conved = product_nt(d_selected, select_full) + d_conv_gate + d_conv_scan
    d_padded, grad_conv_w, grad_conv_b = conv_back(d_conved)
    edge_back = shifted(to_low(d_padded[:edge_count]), -1).astype(jnp.float32)
    d_conv_in = d_padded[edge_count:] + jnp.concatenate(
        [jnp.zeros((rows_dev - edge_count, inner), jnp.float32), edge_back], axis=0
    )
    d_mixed_half = own_columns(to_low(jnp.concatenate([d_conv_in, d_gate_z], axis=1)))
    kv_half = kv_cols // 2
    d_qkv_half = own_columns(
        jnp.concatenate(
            [
                d_queries[:, : q_cols],
                d_keys[:, :kv_half],
                d_values[:, :kv_half],
                d_queries[:, q_cols :],
                d_keys[:, kv_half:],
                d_values[:, kv_half:],
            ],
            axis=1,
        )
    )
    d_mixed_a, d_mixed_b = d_mixed_half[:, :cut_a], d_mixed_half[:, cut_a:cut_b]
    d_mixed_c = jnp.concatenate([d_mixed_half[:, cut_b:], d_qkv_half], axis=1)

    both_halves = [
        jnp.pad(
            jnp.concatenate([sel, stp], axis=1), ((0, 0), (0, 128 - sel_half - step_half))
        )
        for sel, stp in zip(jnp.split(grad_select, 2, axis=1), jnp.split(grad_step_w, 2, axis=1))
    ]
    select_mine = jnp.where(first_core, both_halves[0], both_halves[1])
    select_theirs = jnp.where(first_core, both_halves[1], both_halves[0])
    select_sum = to_low(select_mine + other_core(to_low(select_theirs)).astype(jnp.float32))
    select_sum = summed(select_sum.reshape(64, c_rows, 128), ("xh", "xl", "y", "z"))
    ring_a = ring_sum(grad_pieces(normed_a, d_mixed_a), ORDER_A[1])
    ring_b = ring_sum(grad_pieces(normed_b, d_mixed_b), ORDER_B[1])
    ring_c = ring_sum(grad_pieces(normed_c, d_mixed_c), ORDER_C[1])
    sum_a = plane_sum(ring_a, ORDER_A, d_rows)
    sum_b = plane_sum(ring_b, ORDER_B, d_rows)
    sum_c = plane_sum(ring_c, ORDER_C, d_rows)
    mixed_c = inner - cut_b
    grad_mamba_in = from_channels(
        jnp.concatenate([sum_a, sum_b, sum_c[:, :mixed_c]], axis=1)
    )
    grad_query = sum_c[:, mixed_c : mixed_c + q_cols]
    grad_key = sum_c[:, mixed_c + q_cols : mixed_c + q_cols + k_cols]
    grad_value = sum_c[:, mixed_c + q_cols + k_cols :]
    grad_select, grad_step = select_sum[:, :sel_half], select_sum[:, sel_half : sel_half + step_half]

    d_normed_c = by_pieces_nt(d_mixed_c[:, :mixed_c], in_c) + by_pieces_nt(d_qkv_half, qkv_c)
    d_normed = (
        product_nt(to_low(by_pieces_nt(d_mixed_a, in_a)), pick_a)
        + product_nt(to_low(by_pieces_nt(d_mixed_b, in_b)), pick_b)
        + product_nt(to_low(d_normed_c), pick_c)
    )
    d_tokens_norm, grad_norm = norm_back(sum_cores(d_normed))
    input_grad = to_low(d_tokens_res + d_tokens_norm)[None]

    smalls = (
        grad_norm,
        grad_conv_w,
        grad_conv_b,
        grad_step_bias,
        grad_log_decay,
        grad_skip,
        grad_attn_gain,
        grad_mamba_gain,
        grad_ffn_norm,
    )
    channel_rows = [a.reshape(-1, inner) for a in smalls[1:6]]
    gains = jnp.concatenate([smalls[0], *smalls[6:]]).reshape(-1, inner)
    totals = sum_all(jnp.concatenate([gains, *channel_rows]))
    gain_sums = totals[: gains.shape[0]].reshape(4, width)
    at, channel_sums = gains.shape[0], []
    for a in channel_rows:
        channel_sums.append(from_channels(totals[at : at + a.shape[0]]))
        at += a.shape[0]
    totals = [
        gain_sums[0],
        channel_sums[0],
        *(channel_sums[k][0] for k in (1, 2)),
        channel_sums[3],
        channel_sums[4][0],
        *gain_sums[1:],
    ]
    return (
        output,
        input_grad,
        totals[0],
        grad_query,
        grad_key,
        grad_value,
        grad_attn_out,
        grad_mamba_in,
        totals[1],
        totals[2],
        grad_select,
        grad_step,
        totals[3],
        totals[4],
        totals[5],
        grad_mamba_out,
        totals[6],
        totals[7],
        totals[8],
        grad_gate,
        grad_up,
        grad_down,
    )


def solution(mesh):
    torus = Mesh(
        mesh.devices.reshape(mesh.shape["head"], 2, 4, 4, mesh.shape["seq"]),
        ("head", "xh", "y", "z", "xl"),
    )
    weight = P(BLK_SEQ, "head")
    rows = P("xl", HEAD_BLK, None)
    in_specs = (rows, P("xl", None), rows, P()) + (weight,) * 5
    in_specs += (P(), P(), weight, weight, P(), P(), P(), weight, P(), P(), P()) + (weight,) * 3
    out_specs = (rows, rows, P()) + (weight,) * 5
    out_specs += (P(), P(), weight, weight, P(), P(), P(), weight, P(), P(), P()) + (weight,) * 3
    return jax.shard_map(
        shards, mesh=torus, in_specs=in_specs, out_specs=out_specs, check_vma=False
    )
```

time: 5650 us -> 1320 us (0.23)
  blocking collectives: 3390 us -> 0 us
  local copies, waits for them, and re-layouts: 786 us -> 241 us
  waiting for transfers between devices: 493 us -> 292 us
  other arithmetic: 315 us -> 149 us
  starting transfers between devices: 366 us -> 301 us
    unnamed x4 -> x0, blocking collectives: 3230 us -> none
    unnamed x66 -> x0, waiting for transfers between devices: 447 us -> none
    unnamed x48 -> x0, starting transfers between devices: 290 us -> none
    unnamed x417 -> x600, local copies, waits for them, and re-layouts: 314 us -> 37.2 us
    all_gather x17 -> x0, blocking collectives: 164 us -> none  [the longest x15 152 us: carried_in(): pieces = jax.tree.map(lambda part: lax.all_gather(part, axis), subtotal)]
    all_to_all x0 -> x21, starting transfers between devices: none -> 145 us  [dealt(): return lax.all_to_all(blocks, axis, 0, 0, tiled=True)]
    another operation x34 -> x5, local copies, waits for them, and re-layouts: 144 us -> 3.52 us  [the longest x2 1.49 us: shards(): channel_sums[k][0]]
    all_to_all x0 -> x21, waiting for transfers between devices: none -> 130 us  [dealt(): return lax.all_to_all(blocks, axis, 0, 0, tiled=True)]
  transfers between devices with their start and end apart: 96 -> 137, of which waited for: 19 -> 44; matrix products, arithmetic and copies ran while one was open for 44% -> 44% of each run, Pallas kernels for 0% -> 4%
where the time goes in v1:
time: 1320 us; the launch traced here: 1310 us
  starting transfers between devices  301 us (23%)
  waiting for transfers between devices  292 us (22%)
  matrix products  263 us (20%)
  local copies, waits for them, and re-layouts  241 us (18%)
  other arithmetic  149 us (11%)
  Pallas kernels  54.4 us (4%)
    ppermute x110, starting transfers between devices, received(): return lax.ppermute(a, axis, [((i + d) % n, i) for i in range(n)])  146 us
    all_to_all x21, starting transfers between devices, dealt(): return lax.all_to_all(blocks, axis, 0, 0, tiled=True)  145 us
    ppermute x110, waiting for transfers between devices, received(): return lax.ppermute(a, axis, [((i + d) % n, i) for i in range(n)])  141 us
    all_to_all x21, waiting for transfers between devices, dealt(): return lax.all_to_all(blocks, axis, 0, 0, tiled=True)  130 us
    dot_general x39, matrix products, product(): return jnp.dot(left, right, preferred_element_type=jnp.float32)  91.9 us
    dot_general x40, matrix products, product_nt(): lax.dot_general(left, right, (((1,), (1,)), ((), ())), preferred_element_...  84.4 us
    dot_general x29, matrix products, product_tn(): lax.dot_general(left, right, (((0,), (0,)), ((), ())), preferred_element_...  51.5 us
    pallas_call x4, Pallas kernels, scan_call(): pl.pallas_call(kernel, grid=(channels // SCAN_TILE,), in_specs=[kinds[k]...  48.9 us
  transfers between devices with their start and end apart: 137, of which 44 were waited for; matrix products, arithmetic and copies ran while one was open for 44% of the time, Pallas kernels for 4%

profile of v1, /device:TPU:0, one launch (start us, length us, event | category | flops | bytes accessed | tf_op | source)
XLA Modules:
  0.0 1305.9 jit_solution(18221530109878289507)
XLA Ops:
  4.6 8.1 all-to-all-start
  56.4 17.3 %all-to-all-done.1 = bf16[16,25,1024]{2,1,0:T(8,128)(2,1)S(1)} async-done(((bf16[16,25,1024]{2,1,0:T(8,128)(2,1)}), bf16[16,25,1024]{2,1,0:T(8,128)(2,1)S(1)}, u32[]{:S(2)}, u32[]{:S(2)}) %all-to-all-start.1) | async-done | bytes 819232 | tf_op jit(solution)/shard_map/all_to_all | solution.py:49
  96.2 12.2 collective-permute-done.23
  116.8 8.9 all-to-all-start.3
  169.2 10.5 collective-permute-done.27
  212.2 12.3 all-to-all-start.7
  229.0 8.2 all-to-all-done.7.packed_ref
  273.6 8.5 all-to-all-start.8
  311.9 10.7 shard_map.545
  323.7 19.9 %all-to-all-done.5 = bf16[16,25,1120]{2,1,0:T(8,128)(2,1)} async-done(((bf16[16,25,1120]{2,1,0:T(8,128)(2,1)}), bf16[16,25,1120]{2,1,0:T(8,128)(2,1)}, u32[]{:S(2)}, u32[]{:S(2)}) %all-to-all-start.5) | async-done | bytes 896032 | tf_op jit(solution)/shard_map/all_to_all | solution.py:49
  367.7 10.2 collective-permute-done.3
  445.3 7.9 collective-permute-done.9
  453.2 8.8 collective-permute-start.42
  507.2 27.8 %collective-permute-done.13 = bf16[200,800]{1,0:T(8,128)(2,1)S(1)} collective-permute-done((bf16[200,800]{1,0:T(8,128)(2,1)S(1)}, bf16[200,800]{1,0:T(8,128)(2,1)S(1)}, u32[]{:S(2)}, u32[]{:S(2)}) %collective-permute-start.13) | collective-permute-done | bytes 320032 | tf_op jit(solution)/shard_map/ppermute | solution.py:32
  564.2 16.9 %collective-permute-done.37 = bf16[128,1600]{0,1:T(8,128)(2,1)S(1)} collective-permute-done((bf16[128,1600]{0,1:T(8,128)(2,1)S(1)}, bf16[128,1600]{0,1:T(8,128)(2,1)S(1)}, u32[]{:S(2)}, u32[]{:S(2)}) %collective-permute-start.37) | collective-permute-done | bytes 409632 | tf_op jit(solution)/shard_map/ppermute | solution.py:32
  604.2 8.9 add_add_fusion
  613.0 9.5 fusion.31
  735.7 8.6 collective-permute-done.65
  802.2 8.6 copy.429
  833.4 7.5 multiply_reduce_fusion
  840.8 7.3 multiply_convert_fusion.2
  881.5 14.0 %all-to-all-start.10 = ((bf16[64,18,128]{2,1,0:T(8,128)(2,1)}), bf16[64,18,128]{2,1,0:T(8,128)(2,1)S(1)}, u32[]{:S(2)}, u32[]{:S(2)}) async-start(bf16[64,18,128]{2,1,0:T(8,128)(2,1)} %bitcast.716), calls=%async_computation.10 | async-start | bytes 786432 | tf_op jit(solution)/shard_map/all_to_all | solution.py:49
  918.4 9.2 all-to-all-start.11
  948.6 26.7 %shard_map.548 = (f32[128,3200]{1,0:T(8,128)S(1)}, f32[128,3200]{1,0:T(8,128)S(1)}, f32[16,3200]{1,0:T(8,128)S(1)}, f32[128,16,128]{2,1,0:T(8,128)S(1)}, f32[128,16,128]{2,1,0:T(8,128)S(1)}) custom-call(f32[128,3200]{1,0:T(8,128)S(1)} %get-tuple-element.143.step_ref, f32[128,3200]{1,0:T(8,128)S(1)} %copy-done.4, f32[128,3200]{1,0:T(8,128)S(1)} %copy-done.6, ...), custom_call_target="tpu_custom_call" | custom-call | flops 157286400 | bytes 6553600 | tf_op jit(solution)/shard_map/pallas_call | solution.py:490
  1065.2 8.1 collective-permute-done.90
  1097.5 10.2 all-to-all-start.12
  1109.8 11.1 all-to-all-done.12
  1136.6 8.4 all-to-all-done.18
  1159.2 12.2 all-to-all-done.19
  1172.3 8.5 all-to-all-start.13
  1213.1 28.5 %all-to-all-done.16 = bf16[16,25,1024]{2,1,0:T(8,128)(2,1)} async-done(((bf16[16,25,1024]{2,1,0:T(8,128)(2,1)}), bf16[16,25,1024]{2,1,0:T(8,128)(2,1)}, u32[]{:S(2)}, u32[]{:S(2)}) %all-to-all-start.16) | async-done | bytes 819232 | tf_op jit(solution)/shard_map/all_to_all | solution.py:49
  1287.9 11.0 all-to-all-done.14
  (1349 shorter events, 913.5 us)
Async XLA Ops:
  35.4 51.9 %collective-permute-start.22 = (bf16[400,1152]{1,0:T(8,128)(2,1)S(1)}, bf16[400,1152]{1,0:T(8,128)(2,1)}, u32[]{:S(2)}, u32[]{:S(2)}) collective-permute-start(bf16[400,1152]{1,0:T(8,128)(2,1)S(1)} %reshape.634), channel_id=1, source_target_pairs={{24,0},{0,8},{8,16},{16,24},{25,1},{1,9},{9,17},{17,25},{26,2},{2,... | collective-permute-start | bytes 2764808 | tf_op jit(solution)/shard_map/ppermute | solution.py:32
  37.0 53.3 %collective-permute-start.20 = (bf16[400,1152]{1,0:T(8,128)(2,1)S(1)}, bf16[400,1152]{1,0:T(8,128)(2,1)}, u32[]{:S(2)}, u32[]{:S(2)}) collective-permute-start(bf16[400,1152]{1,0:T(8,128)(2,1)S(1)} %reshape.634), channel_id=1, source_target_pairs={{8,0},{16,8},{24,16},{0,24},{9,1},{17,9},{25,17},{1,25},{10,2},{18... | collective-permute-start | bytes 2764808 | tf_op jit(solution)/shard_map/ppermute | solution.py:32
  74.9 57.9 %collective-permute-start.18 = (bf16[400,1024]{1,0:T(8,128)(2,1)}, bf16[400,1024]{1,0:T(8,128)(2,1)}, u32[]{:S(2)}, u32[]{:S(2)}) collective-permute-start(bf16[400,1024]{1,0:T(8,128)(2,1)} %reshape.635), channel_id=1, source_target_pairs={{33,0},{0,1},{1,32},{32,33},{35,2},{2,3},{3,34},{34,35},{37,4},{4,... | collective-permute-start | bytes 2457608 | tf_op jit(solution)/shard_map/ppermute | solution.py:32
  76.4 60.9 %collective-permute-start.16 = (bf16[400,1024]{1,0:T(8,128)(2,1)}, bf16[400,1024]{1,0:T(8,128)(2,1)}, u32[]{:S(2)}, u32[]{:S(2)}) collective-permute-start(bf16[400,1024]{1,0:T(8,128)(2,1)} %reshape.635), channel_id=1, source_target_pairs={{1,0},{32,1},{33,32},{0,33},{3,2},{34,3},{35,34},{2,35},{5,4},{36,... | collective-permute-start | bytes 2457608 | tf_op jit(solution)/shard_map/ppermute | solution.py:32
  113.1 52.8 %collective-permute-start.24 = (bf16[400,1024]{1,0:T(8,128)(2,1)S(1)}, bf16[400,1024]{1,0:T(8,128)(2,1)S(1)}, u32[]{:S(2)}, u32[]{:S(2)}) collective-permute-start(bf16[400,1024]{1,0:T(8,128)(2,1)S(1)} %reshape.636), channel_id=1, source_target_pairs={{2,0},{4,2},{6,4},{0,6},{3,1},{5,3},{7,5},{1,7},{10,8},{12,10},{14... | collective-permute-start | bytes 2457608 | tf_op jit(solution)/shard_map/ppermute | solution.py:32
  125.6 101.6 %collective-permute-start.60 = (bf16[128,1600]{0,1:T(8,128)(2,1)}, bf16[128,1600]{0,1:T(8,128)(2,1)}, u32[]{:S(2)}, u32[]{:S(2)}) collective-permute-start(bf16[128,1600]{0,1:T(8,128)(2,1)} %bitcast.68), channel_id=1, source_target_pairs={{2,0},{4,2},{6,4},{0,6},{3,1},{5,3},{7,5},{1,7},{10,8},{12,10},{14... | collective-permute-start | bytes 1228808 | tf_op jit(solution)/shard_map/ppermute | solution.py:32
  154.6 87.7 %collective-permute-start.61 = (bf16[128,1600]{0,1:T(8,128)(2,1)}, bf16[128,1600]{0,1:T(8,128)(2,1)}, u32[]{:S(2)}, u32[]{:S(2)}) collective-permute-start(bf16[128,1600]{0,1:T(8,128)(2,1)} %bitcast.68), channel_id=1, source_target_pairs={{4,0},{6,2},{0,4},{2,6},{5,1},{7,3},{1,5},{3,7},{12,8},{14,10},{8,... | collective-permute-start | bytes 1228808 | tf_op jit(solution)/shard_map/ppermute | solution.py:32
  157.8 86.4 %collective-permute-start.62 = (bf16[128,1600]{0,1:T(8,128)(2,1)}, bf16[128,1600]{0,1:T(8,128)(2,1)}, u32[]{:S(2)}, u32[]{:S(2)}) collective-permute-start(bf16[128,1600]{0,1:T(8,128)(2,1)} %bitcast.68), channel_id=1, source_target_pairs={{6,0},{0,2},{2,4},{4,6},{7,1},{1,3},{3,5},{5,7},{14,8},{8,10},{10,... | collective-permute-start | bytes 1228808 | tf_op jit(solution)/shard_map/ppermute | solution.py:32
  179.8 67.1 %collective-permute-start.51 = (bf16[352,800]{0,1:T(8,128)(2,1)}, bf16[352,800]{0,1:T(8,128)(2,1)}, u32[]{:S(2)}, u32[]{:S(2)}) collective-permute-start(bf16[352,800]{0,1:T(8,128)(2,1)} %copy.354), channel_id=1, source_target_pairs={{1,0},{32,1},{33,32},{0,33},{3,2},{34,3},{35,34},{2,35},{5,4},{36,... | collective-permute-start | bytes 1689608 | tf_op jit(solution)/shard_map/ppermute | solution.py:32
  192.1 57.0 %collective-permute-start.52 = (bf16[352,800]{0,1:T(8,128)(2,1)}, bf16[352,800]{0,1:T(8,128)(2,1)}, u32[]{:S(2)}, u32[]{:S(2)}) collective-permute-start(bf16[352,800]{0,1:T(8,128)(2,1)} %copy.354), channel_id=1, source_target_pairs={{33,0},{0,1},{1,32},{32,33},{35,2},{2,3},{3,34},{34,35},{37,4},{4,... | collective-permute-start | bytes 1689608 | tf_op jit(solution)/shard_map/ppermute | solution.py:32
  289.5 71.0 %collective-permute-start.32 = (bf16[800,800]{1,0:T(8,128)(2,1)}, bf16[800,800]{1,0:T(8,128)(2,1)}, u32[]{:S(2)}, u32[]{:S(2)}) collective-permute-start(bf16[800,800]{1,0:T(8,128)(2,1)} %reshape.638), channel_id=1, source_target_pairs={{1,0},{32,1},{33,32},{0,33},{3,2},{34,3},{35,34},{2,35},{5,4},{36,... | collective-permute-start | bytes 3840008 | tf_op jit(solution)/shard_map/ppermute | solution.py:32
  293.3 72.3 %collective-permute-start.33 = (bf16[800,800]{1,0:T(8,128)(2,1)}, bf16[800,800]{1,0:T(8,128)(2,1)}, u32[]{:S(2)}, u32[]{:S(2)}) collective-permute-start(bf16[800,800]{1,0:T(8,128)(2,1)} %reshape.638), channel_id=1, source_target_pairs={{33,0},{0,1},{1,32},{32,33},{35,2},{2,3},{3,34},{34,35},{37,4},{4,... | collective-permute-start | bytes 3840008 | tf_op jit(solution)/shard_map/ppermute | solution.py:32
  362.6 54.9 %collective-permute-start.34 = (bf16[400,800]{1,0:T(8,128)(2,1)}, bf16[400,800]{1,0:T(8,128)(2,1)}, u32[]{:S(2)}, u32[]{:S(2)}) collective-permute-start(bf16[400,800]{1,0:T(8,128)(2,1)} %slice.1004), channel_id=1, source_target_pairs={{1,0},{32,1},{33,32},{0,33},{3,2},{34,3},{35,34},{2,35},{5,4},{36,... | collective-permute-start | bytes 1920008 | tf_op jit(solution)/shard_map/ppermute | solution.py:32
  367.7 70.1 %collective-permute-start.35 = (bf16[400,800]{1,0:T(8,128)(2,1)}, bf16[400,800]{1,0:T(8,128)(2,1)}, u32[]{:S(2)}, u32[]{:S(2)}) collective-permute-start(bf16[400,800]{1,0:T(8,128)(2,1)} %slice.1005), channel_id=1, source_target_pairs={{33,0},{0,1},{1,32},{32,33},{35,2},{2,3},{3,34},{34,35},{37,4},{4,... | collective-permute-start | bytes 1920008 | tf_op jit(solution)/shard_map/ppermute | solution.py:32
  424.8 65.9 %collective-permute-start.31 = (bf16[128,3200]{1,0:T(8,128)(2,1)}, bf16[128,3200]{1,0:T(8,128)(2,1)}, u32[]{:S(2)}, u32[]{:S(2)}) collective-permute-start(bf16[128,3200]{1,0:T(8,128)(2,1)} %multiply_convert_fusion.7), channel_id=1, source_target_pairs={{64,0},{0,64},{65,1},{1,65},{66,2},{2,66},{67,3},{3,67},{68,4},{4,... | collective-permute-start | bytes 2457608 | tf_op jit(solution)/shard_map/ppermute | solution.py:32
  425.9 72.2 %collective-permute-start.12 = (bf16[400,800]{1,0:T(8,128)(2,1)S(1)}, bf16[400,800]{1,0:T(8,128)(2,1)}, u32[]{:S(2)}, u32[]{:S(2)}) collective-permute-start(bf16[400,800]{1,0:T(8,128)(2,1)S(1)} %reshape.651), channel_id=1, source_target_pairs={{8,0},{16,8},{24,16},{0,24},{9,1},{17,9},{25,17},{1,25},{10,2},{18... | collective-permute-start | bytes 1920008 | tf_op jit(solution)/shard_map/ppermute | solution.py:32
  550.8 51.3 %collective-permute-start.45 = (bf16[200,1408]{1,0:T(8,128)(2,1)}, bf16[200,1408]{1,0:T(8,128)(2,1)}, u32[]{:S(2)}, u32[]{:S(2)}) collective-permute-start(bf16[200,1408]{1,0:T(8,128)(2,1)} %slice.1012), channel_id=1, source_target_pairs={{8,0},{16,8},{24,16},{0,24},{9,1},{17,9},{25,17},{1,25},{10,2},{18... | collective-permute-start | bytes 1689608 | tf_op jit(solution)/shard_map/ppermute | solution.py:32
  707.4 64.8 %collective-permute-start.112 = (bf16[352,800]{0,1:T(8,128)(2,1)}, bf16[352,800]{0,1:T(8,128)(2,1)}, u32[]{:S(2)}, u32[]{:S(2)}) collective-permute-start(bf16[352,800]{0,1:T(8,128)(2,1)} %copy.405), channel_id=1, source_target_pairs={{1,0},{32,1},{33,32},{0,33},{3,2},{34,3},{35,34},{2,35},{5,4},{36,... | collective-permute-start | bytes 1689608 | tf_op jit(solution)/shard_map/ppermute | solution.py:32
  714.0 60.4 %collective-permute-start.110 = (bf16[352,800]{0,1:T(8,128)(2,1)}, bf16[352,800]{0,1:T(8,128)(2,1)}, u32[]{:S(2)}, u32[]{:S(2)}) collective-permute-start(bf16[352,800]{0,1:T(8,128)(2,1)} %copy.403), channel_id=1, source_target_pairs={{33,0},{0,1},{1,32},{32,33},{35,2},{2,3},{3,34},{34,35},{37,4},{4,... | collective-permute-start | bytes 1689608 | tf_op jit(solution)/shard_map/ppermute | solution.py:32
  779.1 379.7 %collective-permute-start.115 = (bf16[88,800]{1,0:T(8,128)(2,1)}, bf16[88,800]{1,0:T(8,128)(2,1)}, u32[]{:S(2)}, u32[]{:S(2)}) collective-permute-start(bf16[88,800]{1,0:T(8,128)(2,1)} %get-tuple-element.170), channel_id=1, source_target_pairs={{8,0},{16,8},{24,16},{0,24},{9,1},{17,9},{25,17},{1,25},{10,2},{18... | collective-permute-start | bytes 422408 | tf_op jit(solution)/shard_map/ppermute | solution.py:32
  787.9 83.6 %collective-permute-start.69 = (bf16[128,3200]{1,0:T(8,128)(2,1)}, bf16[128,3200]{1,0:T(8,128)(2,1)}, u32[]{:S(2)}, u32[]{:S(2)}) collective-permute-start(bf16[128,3200]{1,0:T(8,128)(2,1)} %slice.1414), channel_id=1, source_target_pairs={{64,0},{0,64},{65,1},{1,65},{66,2},{2,66},{67,3},{3,67},{68,4},{4,... | collective-permute-start | bytes 2457608 | tf_op jit(solution)/shard_map/ppermute | solution.py:32
  821.8 85.5 %collective-permute-start.87 = (bf16[400,800]{1,0:T(8,128)(2,1)}, bf16[400,800]{1,0:T(8,128)(2,1)}, u32[]{:S(2)}, u32[]{:S(2)}) collective-permute-start(bf16[400,800]{1,0:T(8,128)(2,1)} %pad_maximum_fusion.31), channel_id=1, source_target_pairs={{8,0},{16,8},{24,16},{0,24},{9,1},{17,9},{25,17},{1,25},{10,2},{18... | collective-permute-start | bytes 1920008 | tf_op jit(solution)/shard_map/ppermute | solution.py:32
  897.2 286.4 %collective-permute-start.114 = (bf16[88,800]{1,0:T(8,128)(2,1)}, bf16[88,800]{1,0:T(8,128)(2,1)}, u32[]{:S(2)}, u32[]{:S(2)}) collective-permute-start(bf16[88,800]{1,0:T(8,128)(2,1)} %get-tuple-element.171), channel_id=1, source_target_pairs={{16,0},{24,8},{0,16},{8,24},{17,1},{25,9},{1,17},{9,25},{18,2},{26... | collective-permute-start | bytes 422408 | tf_op jit(solution)/shard_map/ppermute | solution.py:32
  927.5 84.9 %collective-permute-start.100 = (bf16[800,800]{1,0:T(8,128)(2,1)}, bf16[800,800]{1,0:T(8,128)(2,1)}, u32[]{:S(2)}, u32[]{:S(2)}) collective-permute-start(bf16[800,800]{1,0:T(8,128)(2,1)} %pad_maximum_fusion.11), channel_id=1, source_target_pairs={{1,0},{32,1},{33,32},{0,33},{3,2},{34,3},{35,34},{2,35},{5,4},{36,... | collective-permute-start | bytes 3840008 | tf_op jit(solution)/shard_map/ppermute | solution.py:32
  929.1 83.3 %collective-permute-start.98 = (bf16[800,800]{1,0:T(8,128)(2,1)}, bf16[800,800]{1,0:T(8,128)(2,1)}, u32[]{:S(2)}, u32[]{:S(2)}) collective-permute-start(bf16[800,800]{1,0:T(8,128)(2,1)} %pad_maximum_fusion.10), channel_id=1, source_target_pairs={{33,0},{0,1},{1,32},{32,33},{35,2},{2,3},{3,34},{34,35},{37,4},{4,... | collective-permute-start | bytes 3840008 | tf_op jit(solution)/shard_map/ppermute | solution.py:32
  938.8 136.3 %all-to-all-start.20 = ((bf16[4,25,1408]{2,1,0:T(8,128)(2,1)}), bf16[4,25,1408]{2,1,0:T(8,128)(2,1)}, u32[]{:S(2)}, u32[]{:S(2)}) async-start(bf16[4,25,1408]{2,1,0:T(8,128)(2,1)} %reshape.704), calls=%async_computation.20 | async-start | bytes 720896 | tf_op jit(solution)/shard_map/all_to_all | solution.py:49
  1057.7 91.1 %collective-permute-start.82 = (bf16[200,2144]{1,0:T(8,128)(2,1)}, bf16[200,2144]{1,0:T(8,128)(2,1)}, u32[]{:S(2)}, u32[]{:S(2)}) collective-permute-start(bf16[200,2144]{1,0:T(8,128)(2,1)} %convolution_convert_fusion.4), channel_id=1, source_target_pairs={{2,0},{4,2},{6,4},{0,6},{3,1},{5,3},{7,5},{1,7},{10,8},{12,10},{14... | collective-permute-start | bytes 2572808 | tf_op jit(solution)/shard_map/ppermute | solution.py:32
  1093.3 58.6 %collective-permute-start.80 = (bf16[200,2144]{1,0:T(8,128)(2,1)}, bf16[200,2144]{1,0:T(8,128)(2,1)}, u32[]{:S(2)}, u32[]{:S(2)}) collective-permute-start(bf16[200,2144]{1,0:T(8,128)(2,1)} %convolution_convert_fusion.5), channel_id=1, source_target_pairs={{6,0},{0,2},{2,4},{4,6},{7,1},{1,3},{3,5},{5,7},{14,8},{8,10},{10,... | collective-permute-start | bytes 2572808 | tf_op jit(solution)/shard_map/ppermute | solution.py:32
  1130.2 54.3 %collective-permute-start.91 = (bf16[400,1024]{1,0:T(8,128)(2,1)}, bf16[400,1024]{1,0:T(8,128)(2,1)}, u32[]{:S(2)}, u32[]{:S(2)}) collective-permute-start(bf16[400,1024]{1,0:T(8,128)(2,1)} %pad_maximum_fusion.29), channel_id=1, source_target_pairs={{1,0},{32,1},{33,32},{0,33},{3,2},{34,3},{35,34},{2,35},{5,4},{36,... | collective-permute-start | bytes 2457608 | tf_op jit(solution)/shard_map/ppermute | solution.py:32
  1152.0 55.9 %collective-permute-start.95 = (bf16[400,1152]{1,0:T(8,128)(2,1)}, bf16[400,1152]{1,0:T(8,128)(2,1)}, u32[]{:S(2)}, u32[]{:S(2)}) collective-permute-start(bf16[400,1152]{1,0:T(8,128)(2,1)} %pad_maximum_fusion.22), channel_id=1, source_target_pairs={{8,0},{16,8},{24,16},{0,24},{9,1},{17,9},{25,17},{1,25},{10,2},{18... | collective-permute-start | bytes 2764808 | tf_op jit(solution)/shard_map/ppermute | solution.py:32
  1184.5 67.3 %collective-permute-start.83 = (bf16[400,2144]{1,0:T(8,128)(2,1)}, bf16[400,2144]{1,0:T(8,128)(2,1)}, u32[]{:S(2)}, u32[]{:S(2)}) collective-permute-start(bf16[400,2144]{1,0:T(8,128)(2,1)} %pad_maximum_fusion.5), channel_id=1, source_target_pairs={{2,0},{4,2},{6,4},{0,6},{3,1},{5,3},{7,5},{1,7},{10,8},{12,10},{14... | collective-permute-start | bytes 5145608 | tf_op jit(solution)/shard_map/ppermute | solution.py:32
  1187.9 63.9 %collective-permute-start.81 = (bf16[400,2144]{1,0:T(8,128)(2,1)}, bf16[400,2144]{1,0:T(8,128)(2,1)}, u32[]{:S(2)}, u32[]{:S(2)}) collective-permute-start(bf16[400,2144]{1,0:T(8,128)(2,1)} %pad_maximum_fusion.4), channel_id=1, source_target_pairs={{6,0},{0,2},{2,4},{4,6},{7,1},{1,3},{3,5},{5,7},{14,8},{8,10},{10,... | collective-permute-start | bytes 5145608 | tf_op jit(solution)/shard_map/ppermute | solution.py:32
  (403 other events, 4692.3 us)

commit v2 on v1

--- a/solution.py
+++ b/solution.py
@@ -25,6 +25,8 @@
 EPSILON = 1e-06
 LOG2_E = 1.0 / math.log(2.0)
 FF_PAD = 88
+WIDTH = HEADS * HEAD_DIM
+LANES = -(-WIDTH // 128) * 128
 
 
 def received(a, axis, d):
@@ -60,25 +62,17 @@
 ORDER_A = (("y", "z"), X_RING)
 ORDER_B = (("xh", "z", "xl"), Y_RING)
 ORDER_C = (("xh", "y", "xl"), Z_RING)
+ORDERS = (ORDER_A, ORDER_B, ORDER_C)
+
+
+def together(values):
+    return lax.optimization_barrier(tuple(values))
 
 
 def ring_pieces(a, axis):
     half = a.shape[0] // 2
     up, down = received(a, axis, 1), received(a, axis, -1)
     return [a, up, received(up[:half], axis, 1), received(down[half:], axis, -1), down]
-
-
-def in_order(pieces, axis):
-    own, up, far_low, far_high, down = pieces
-    me = lax.axis_index(axis)
-    out = jnp.zeros((4, *own.shape), own.dtype)
-    out = lax.dynamic_update_index_in_dim(out, own, me, 0)
-    out = lax.dynamic_update_index_in_dim(out, up, lax.rem(me + 1, 4), 0)
-    out = lax.dynamic_update_index_in_dim(out, down, lax.rem(me + 3, 4), 0)
-    far = lax.rem(me + 2, 4)
-    out = lax.dynamic_update_slice(out, far_low[None], (far, 0, 0))
-    out = lax.dynamic_update_slice(out, far_high[None], (far, far_low.shape[0], 0))
-    return out.reshape(4 * own.shape[0], own.shape[1])
 
 
 def ring_whole(a, axis):
@@ -93,8 +87,12 @@
     return out.reshape(4 * a.shape[0], a.shape[1])
 
 
-def plane(shard, order):
-    return shown(shard, order[0]).reshape(16 * shard.shape[0], shard.shape[1])
+def gather_planes(shards, orders, last=()):
+    planes = []
+    for a, order in zip(shards, orders):
+        planes.append(shown(after(a, *last), order[0]).reshape(16 * a.shape[0], a.shape[1]))
+        last = planes[-1:]
+    return planes
 
 
 def ring_sum(pieces, axis):
@@ -123,20 +121,12 @@
     return total
 
 
-def plane_sum(whole, order, rows):
-    return summed(to_low(whole).reshape(16, rows, whole.shape[1]), order[0])
-
-
-def turned_pieces(whole, axis):
-    rows = whole.shape[0] // 4
-    blocks = whole.reshape(4, rows, whole.shape[1])
-    me = lax.axis_index(axis)
-
-    def block(j):
-        return lax.dynamic_index_in_dim(blocks, lax.rem(me + j, 4), 0, keepdims=False)
-
-    far = block(2)
-    return [block(0), block(1), far[: rows // 2], far[rows // 2 :], block(3)]
+def sum_rings(grads, orders):
+    return [to_low(ring_sum(a, order[1])) for a, order in zip(grads, orders)]
+
+
+def sum_planes(rings, orders):
+    return [summed(a.reshape(16, a.shape[0] // 16, a.shape[1]), order[0]) for a, order in zip(rings, orders)]
 
 
 def ring_sum_in_order(whole, axis):
@@ -150,7 +140,12 @@
     return total
 
 
-def picker(order, rows):
+def padded_index(index):
+    return jnp.pad(index, (0, LANES - WIDTH), constant_values=-1)
+
+
+def picker(order, rows, stride=None, offset=0):
+    stride = stride or rows
     ring, inside = np.indices((4, 16 * rows))
     turned = lax.rem(lax.axis_index(order[1]) + jnp.asarray(ring, jnp.int32), 4)
     block, row = inside // rows, jnp.asarray(inside % rows, jnp.int32)
@@ -160,51 +155,222 @@
         xh, y, z, xl = block // 8, turned, block // 2 % 4, block % 2
     else:
         xh, y, z, xl = block // 8, block // 2 % 4, turned, block % 2
-    return ((((xh * 4 + y) * 4 + z) * 2 + xl) * rows + row).reshape(-1)
+    return padded_index(((((xh * 4 + y) * 4 + z) * 2 + xl) * stride + offset + row).reshape(-1))
 
 
 def ff_picker(rows):
-    y, x, z, row = (jnp.asarray(j, jnp.int32) for j in np.indices((4, 4, 4, rows)))
-    y = lax.rem(lax.axis_index(Y_RING) + y, 4)
-    x = lax.rem(lax.axis_index(X_RING) + x, 4)
-    return (((((x // 2) * 4 + y) * 4 + z) * 2 + x % 2) * rows + row).reshape(-1)
-
-
-def one_hot(index, rows):
-    return (jnp.arange(rows, dtype=jnp.int32)[:, None] == index[None, :]).astype(jnp.bfloat16)
-
-
-def piece_bounds(total):
-    k = total // 8
-    return [(0, 2 * k), (2 * k, 4 * k), (4 * k, 5 * k), (5 * k, 6 * k), (6 * k, 8 * k)]
-
-
-def by_pieces(left, pieces):
-    total = 0.0
-    for (start, stop), piece in zip(piece_bounds(left.shape[1]), pieces):
-        total = total + product(left[:, start:stop], piece)
-    return total
-
-
-def by_pieces_nt(left, pieces):
-    return jnp.concatenate([product_nt(left, piece) for piece in pieces], axis=1)
-
-
-def grad_pieces(left, right):
-    return [to_low(product_tn(left[:, start:stop], right)) for start, stop in piece_bounds(left.shape[1])]
-
-
-def to_channels(a):
-    lead, width = a.shape[:-1], a.shape[-1]
-    return lax.optimization_barrier(
-        jnp.swapaxes(a.reshape(*lead, 2, 16, 2, width // 64), -3, -2).reshape(*lead, width)
-    )
-
-
-def from_channels(a):
-    lead, width = a.shape[:-1], a.shape[-1]
-    a = lax.optimization_barrier(a)
-    return jnp.swapaxes(a.reshape(*lead, 2, 2, 16, width // 64), -3, -2).reshape(*lead, width)
+    xh, y, xl, z, row = np.indices((2, 4, 2, 4, rows))
+    index = (((((xh * 4 + y) * 4 + z) * 2 + xl) * rows + row)).reshape(16, 4 * rows)
+    return jnp.asarray(np.pad(index, ((0, 0), (0, LANES // 16 - 4 * rows)), constant_values=-1).reshape(-1), jnp.int32)
+
+
+def gathered(a, axes):
+    return lax.all_gather(a, axes).reshape(-1, a.shape[1])
+
+
+def scattered(a, axes):
+    blocks = a.reshape(lax.axis_size(axes), -1, a.shape[1])
+    return lax.optimization_barrier(lax.psum_scatter(blocks, axes, scatter_dimension=0))
+
+
+HALVES = (WIDTH // 4, WIDTH // 4, WIDTH // 8, WIDTH // 8, WIDTH // 4)
+
+
+def bounds(sizes):
+    stops = np.cumsum(sizes)
+    return [(int(stop - size), int(stop)) for size, stop in zip(sizes, stops)]
+
+
+def rows_of(pieces):
+    return bounds([a.shape[0] for a in pieces])
+
+
+def dot_nn(a, b):
+    return jnp.dot(a, b, preferred_element_type=jnp.float32)
+
+
+def dot_nt(a, b):
+    return lax.dot_general(a, b, (((1,), (1,)), ((), ())), preferred_element_type=jnp.float32)
+
+
+def dot_tn(a, b):
+    return lax.dot_general(a, b, (((0,), (0,)), ((), ())), preferred_element_type=jnp.float32)
+
+
+def whole_call(kernel, operands, outs, flops):
+    sizes = sum(a.size * a.dtype.itemsize for a in (*operands, *outs))
+    return pl.pallas_call(
+        kernel,
+        out_shape=outs,
+        in_specs=[pl.BlockSpec(memory_space=pltpu.VMEM)] * len(operands),
+        out_specs=[pl.BlockSpec(memory_space=pltpu.VMEM)] * len(outs),
+        compiler_params=pltpu.CompilerParams(vmem_limit_bytes=40 * 2**20),
+        cost_estimate=pl.CostEstimate(flops=flops, bytes_accessed=sizes, transcendentals=0),
+    )(*operands)
+
+
+def out_array(rows, cols, low=True):
+    return jax.ShapeDtypeStruct((rows, cols), jnp.bfloat16 if low else jnp.float32)
+
+
+def clear_rest(ref, start):
+    if start < ref.shape[1]:
+        ref[:, start:] = jnp.zeros((ref.shape[0], ref.shape[1] - start), ref.dtype)
+
+
+def nn_kernel(windows, *refs):
+    count = len(windows)
+    lefts, pieces, y_ref = refs[:count], refs[count:-1], refs[-1]
+    width = windows[0][1] - windows[0][0]
+    for at in range(0, width, 512):
+        stop = min(at + 512, width)
+        total = 0.0
+        for left, (low, _) in zip(lefts, windows):
+            for (start, end), piece in zip(rows_of(pieces), pieces):
+                total = total + dot_nn(left[:, start:end], piece[:, low + at : low + stop])
+        y_ref[:, at:stop] = total.astype(y_ref.dtype)
+    clear_rest(y_ref, width)
+
+
+def by_pieces(lefts, pieces, windows, low=True):
+    rows, width = lefts[0].shape[0], windows[0][1] - windows[0][0]
+    flops = 2 * rows * width * sum(a.shape[1] for a in lefts)
+    return whole_call(
+        functools.partial(nn_kernel, windows), (*lefts, *pieces), [out_array(rows, -(-width // 128) * 128 if low else width, low)], flops
+    )[0]
+
+
+def nt_kernel(windows, *refs):
+    count = len(windows)
+    grads, pieces, outs = refs[:count], refs[count:-count], refs[-count:]
+    for grad, (low, high), out in zip(grads, windows, outs):
+        for (start, end), piece in zip(rows_of(pieces), pieces):
+            out[:, start:end] = dot_nt(grad[:, : high - low], piece[:, low:high]).astype(out.dtype)
+        clear_rest(out, rows_of(pieces)[-1][1])
+
+
+def by_pieces_nt(grads, pieces, windows):
+    rows, depth = grads[0].shape[0], sum(a.shape[0] for a in pieces)
+    flops = 2 * rows * depth * sum(a.shape[1] for a in grads)
+    return whole_call(
+        functools.partial(nt_kernel, windows), (*grads, *pieces), [out_array(rows, -(-depth // 128) * 128)] * len(grads), flops
+    )
+
+
+def tn_kernel(sizes, right, *refs):
+    lefts, outs = refs[: -len(sizes)], refs[-len(sizes) :]
+    width = right.shape[1]
+    for k, left in enumerate(lefts):
+        for (start, end), out in zip(bounds(sizes), outs):
+            out[:, k * width : (k + 1) * width] = dot_tn(left[:, start:end], right[...]).astype(out.dtype)
+
+
+def grad_pieces(lefts, right, sizes):
+    outs = [out_array(size, right.shape[1] * len(lefts)) for size in sizes]
+    flops = 2 * right.size * sum(sizes) * len(lefts)
+    return whole_call(functools.partial(tn_kernel, sizes), (right, *lefts), outs, flops)
+
+
+def feed_kernel(x_ref, g_ref, up_ref, down_ref, act_ref, d_ref, y_ref, dx_ref):
+    units = down_ref.shape[0]
+    both = dot_nn(x_ref[...], up_ref[...])
+    gate, up = both[:, :units], both[:, units:]
+    sig = 1.0 / (1.0 + jnp.exp(-gate))
+    silu = gate * sig
+    act = (silu * up).astype(jnp.bfloat16)
+    act_ref[...] = act
+    y_ref[:, :WIDTH] = dot_nn(act, down_ref[...]).astype(y_ref.dtype)
+    clear_rest(y_ref, WIDTH)
+    d_act = dot_nt(g_ref[:, :WIDTH], down_ref[...])
+    d_ref[:, :units] = (d_act * up * (sig * (1.0 + gate * (1.0 - sig)))).astype(d_ref.dtype)
+    d_ref[:, units:] = (d_act * silu).astype(d_ref.dtype)
+    dx_ref[...] = dot_nt(d_ref[...], up_ref[...]).astype(dx_ref.dtype)
+
+
+def feed_forward(x, g, gate_up, down):
+    tokens, width = x.shape
+    units = down.shape[0]
+    block = 256
+
+    def rows(cols):
+        return pl.BlockSpec((block, cols), lambda i: (i, 0))
+
+    def fixed(a):
+        return pl.BlockSpec(a.shape, lambda i: (0, 0))
+
+    return pl.pallas_call(
+        feed_kernel,
+        grid=(tokens // block,),
+        in_specs=[rows(width), rows(width), fixed(gate_up), fixed(down)],
+        out_specs=[rows(units), rows(2 * units), rows(width), rows(width)],
+        out_shape=[out_array(tokens, c) for c in (units, 2 * units, width, width)],
+        compiler_params=pltpu.CompilerParams(
+            dimension_semantics=("arbitrary",), vmem_limit_bytes=48 * 2**20
+        ),
+        cost_estimate=pl.CostEstimate(
+            flops=2 * tokens * width * units * 6, bytes_accessed=2 * tokens * (4 * width + 3 * units), transcendentals=tokens * units
+        ),
+    )(x, g, gate_up, down)
+
+
+def feed_grads_kernel(x_ref, d_ref, act_ref, g_ref, up_ref, down_ref):
+    up_ref[...] = dot_tn(x_ref[...], d_ref[...]).astype(up_ref.dtype)
+    down_ref[...] = dot_tn(act_ref[...], g_ref[:, :WIDTH]).astype(down_ref.dtype)
+
+
+def feed_grads(x, d, act, g):
+    outs = [out_array(x.shape[1], d.shape[1]), out_array(act.shape[1], WIDTH)]
+    flops = 2 * x.shape[0] * x.shape[1] * (d.shape[1] + act.shape[1])
+    return whole_call(feed_grads_kernel, (x, d, act, g), outs, flops)
+
+
+def one_hot(index_ref, start, stop):
+    width = index_ref.shape[1]
+    rows = lax.broadcasted_iota(jnp.int32, (stop - start, width), 0) + start
+    return jnp.where(rows == index_ref[...], 1.0, 0.0).astype(jnp.bfloat16)
+
+
+def turn_kernel(count, *refs):
+    lefts, indices, outs = refs[:count], refs[count : 2 * count], refs[2 * count :]
+    for left, index, out in zip(lefts, indices, outs):
+        total = 0.0
+        for start in range(0, left.shape[1], 400):
+            total = total + dot_nn(left[:, start : start + 400], one_hot(index, start, start + 400))
+        out[...] = total.astype(out.dtype)
+
+
+def turned(lefts, indices):
+    outs = [out_array(a.shape[0], index.shape[0]) for a, index in zip(lefts, indices)]
+    rows = [index.reshape(1, -1) for index in indices]
+    flops = sum(2 * a.size * a.shape[1] for a in lefts)
+    return whole_call(functools.partial(turn_kernel, len(lefts)), (*lefts, *rows), outs, flops)
+
+
+def turn_back_kernel(count, *refs):
+    lefts, indices, outs = refs[:count], refs[count : 2 * count], refs[2 * count :]
+    for start in range(0, outs[0].shape[1], 400):
+        total = 0.0
+        for k, (left, index) in enumerate(zip(lefts, indices)):
+            hot = one_hot(index, start, start + 400)
+            if left.dtype == jnp.float32:
+                high = left[...].astype(jnp.bfloat16)
+                rest = (left[...] - high.astype(jnp.float32)).astype(jnp.bfloat16)
+                part = dot_nt(high, hot) + dot_nt(rest, hot)
+            else:
+                part = dot_nt(left[...], hot)
+            if len(outs) > 1:
+                outs[k][:, start : start + 400] = part.astype(outs[k].dtype)
+            total = total + part
+        if len(outs) == 1:
+            outs[0][:, start : start + 400] = total.astype(outs[0].dtype)
+
+
+def turned_back(lefts, indices, low, summed=False, width=WIDTH):
+    rows = lefts[0].shape[0]
+    outs = [out_array(rows, width, low)] * (1 if summed else len(lefts))
+    hots = [index.reshape(1, -1) for index in indices]
+    flops = sum(2 * a.size * width for a in lefts)
+    return whole_call(functools.partial(turn_back_kernel, len(lefts)), (*lefts, *hots), outs, flops)
 
 
 def join_columns(mine, got):
@@ -230,7 +396,7 @@
 
 def sum_cores(both):
     rows = both.shape[0] // 2
-    return both[:rows] + other_core(to_low(both[rows:])).astype(jnp.float32)
+    return both[:rows].astype(jnp.float32) + other_core(to_low(both[rows:])).astype(jnp.float32)
 
 
 def chain_kernel(reverse, packed_ref, rate_ref, out_ref):
@@ -247,7 +413,7 @@
     lax.fori_loop(0, count, one, jnp.zeros(rate.shape, jnp.float32))
 
 
-def chain_carry(total_step, state, decay_rate, reverse):
+def chain_carry(total_step, state, decay_rate, reverse, others=()):
     count = lax.axis_size(HEAD_BLK)
     states, channels = state.shape
     high = lax.reduce_precision(total_step, 8, 7)
@@ -262,17 +428,18 @@
         functools.partial(chain_kernel, reverse),
         out_shape=jax.ShapeDtypeStruct((count, states, 128), jnp.float32),
     )(dealt(tiles(packed), HEAD_BLK), rate)
-    got = dealt(to_low(chained), HEAD_BLK)[: channels // 128]
+    got = dealt(after(to_low(chained), *others), HEAD_BLK)[: channels // 128]
     return got.transpose(1, 0, 2).reshape(states, channels).astype(jnp.float32)
 
 
-def sum_all(values):
+def sum_all(values, owned):
     count = lax.axis_size(EVERY)
     lines = values.reshape(-1, 128)
     each = -(-lines.shape[0] // count)
-    padded = jnp.pad(lines, ((0, count * each - lines.shape[0]), (0, 0)))
-    mine = summed(padded.reshape(count, each, 128), EVERY)
-    return shown(mine, EVERY).reshape(-1, 128)[: lines.shape[0]].reshape(values.shape)
+    padded = jnp.pad(lines, ((0, count * each - lines.shape[0]), (0, 0))).reshape(count, each, 128)
+    mine = summed(jnp.concatenate([to_low(owned), to_low(padded)], axis=1), EVERY)
+    all_lines = shown(mine[owned.shape[1] :], EVERY).reshape(-1, 128)
+    return all_lines[: lines.shape[0]].reshape(values.shape), mine[: owned.shape[1]]
 
 
 def rms_scale(values, gain):
@@ -326,18 +493,6 @@
 
 def swiglu(gate_val, up_val):
     return jax.nn.silu(gate_val) * up_val
-
-
-def group_scores(queries, window_keys, allowed, group_index, group_size, score_scale):
-    query_part = queries[
-        :, group_index * group_size * HEAD_DIM : (group_index + 1) * group_size * HEAD_DIM
-    ].reshape(queries.shape[0], group_size, HEAD_DIM)
-    key_part = window_keys[:, group_index * HEAD_DIM : (group_index + 1) * HEAD_DIM]
-    raw_scores = (
-        jnp.einsum("qgd,sd->gqs", query_part, key_part, preferred_element_type=jnp.float32)
-        * score_scale
-    )
-    return (jnp.where(allowed[None], raw_scores, -1e30), query_part, key_part)
 
 
 SCAN_TILE = 640
@@ -531,6 +686,88 @@
         scan_back_kernel, operands, "tttmmsss", 5, "ttsmm", scratch, flops=24
     )
     return d_step, d_conv, d_rate, jnp.sum(d_in, axis=-1), jnp.sum(d_out, axis=-1)
+
+
+SCORE_SCALE = 1.0 / math.sqrt(HEAD_DIM)
+GROUP = HEADS // KV_HEADS
+
+
+def attend_kernel(q_ref, window_ref, bias_ref, out_ref, total_ref):
+    keys, values = window_ref[:, :HEAD_DIM], window_ref[:, HEAD_DIM:]
+    for h in range(GROUP):
+        lanes = slice(h * HEAD_DIM, (h + 1) * HEAD_DIM)
+        scores = dot_nt(q_ref[0, :, lanes], keys) * SCORE_SCALE + bias_ref[...]
+        top = jnp.max(scores, axis=1, keepdims=True)
+        weights = jnp.exp(scores - top)
+        total = jnp.sum(weights, axis=1, keepdims=True)
+        low = (weights * (1.0 / total)).astype(jnp.bfloat16)
+        out_ref[0, :, lanes] = dot_nn(low, values).astype(out_ref.dtype)
+        total_ref[0, :, h : h + 1] = top + jnp.log(total)
+
+
+def attend_back_kernel(q_ref, window_ref, bias_ref, total_ref, d_ref, dq_ref, d_window_ref):
+    keys, values = window_ref[:, :HEAD_DIM], window_ref[:, HEAD_DIM:]
+    d_keys = d_values = 0.0
+    for h in range(GROUP):
+        lanes = slice(h * HEAD_DIM, (h + 1) * HEAD_DIM)
+        queries, d_heads = q_ref[0, :, lanes], d_ref[0, :, lanes]
+        weights = jnp.exp(dot_nt(keys, queries) * SCORE_SCALE + bias_ref[...] - total_ref[0, h : h + 1, :])
+        d_weights = dot_nt(values, d_heads)
+        through = jnp.sum(weights * d_weights, axis=0, keepdims=True)
+        d_scores = (weights * (d_weights - through)).astype(jnp.bfloat16)
+        d_values = d_values + dot_nn(weights.astype(jnp.bfloat16), d_heads)
+        d_keys = d_keys + dot_nn(d_scores, queries)
+        dq_ref[0, :, lanes] = (dot_tn(d_scores, keys) * SCORE_SCALE).astype(dq_ref.dtype)
+    d_window_ref[:, :HEAD_DIM] = (d_keys * SCORE_SCALE).astype(d_window_ref.dtype)
+    d_window_ref[:, HEAD_DIM:] = d_values.astype(d_window_ref.dtype)
+
+
+def attend_call(kernel, operands, kinds, outs, out_kinds, rows, span, products):
+    groups = pl.BlockSpec((1, rows, GROUP * HEAD_DIM), lambda i: (i, 0, 0))
+    window = pl.BlockSpec((span, 2 * HEAD_DIM), lambda i: (0, i))
+    specs = {"q": groups, "w": window}
+    for a in (*operands, *outs):
+        specs[a.shape] = pl.BlockSpec(a.shape, lambda i: (0, 0)) if len(a.shape) == 2 else pl.BlockSpec((1, *a.shape[1:]), lambda i: (i, 0, 0))
+    return pl.pallas_call(
+        kernel,
+        grid=(KV_HEADS,),
+        in_specs=[specs[k if k in specs else a.shape] for k, a in zip(kinds, operands)],
+        out_specs=[specs[k if k in specs else a.shape] for k, a in zip(out_kinds, outs)],
+        out_shape=outs,
+        compiler_params=pltpu.CompilerParams(
+            dimension_semantics=("arbitrary",), vmem_limit_bytes=24 * 2**20
+        ),
+        cost_estimate=pl.CostEstimate(
+            flops=2 * products * HEADS * rows * span * HEAD_DIM, bytes_accessed=4 * rows * span, transcendentals=HEADS * rows * span
+        ),
+    )(*operands)
+
+
+def by_groups(a):
+    return a.reshape(a.shape[0], KV_HEADS, GROUP * HEAD_DIM).transpose(1, 0, 2)
+
+
+def from_groups(a):
+    return a.transpose(1, 0, 2).reshape(a.shape[1], HEADS * HEAD_DIM)
+
+
+def attend(queries, window, bias):
+    rows, span = queries.shape[1], window.shape[0]
+    outs = [
+        jax.ShapeDtypeStruct(queries.shape, jnp.bfloat16),
+        jax.ShapeDtypeStruct((KV_HEADS, rows, 8), jnp.float32),
+    ]
+    return attend_call(attend_kernel, (queries, window, bias), "qwb", outs, "qt", rows, span, 2)
+
+
+def attend_back(queries, window, bias_t, totals, d_heads):
+    rows, span = queries.shape[1], window.shape[0]
+    outs = [
+        jax.ShapeDtypeStruct(queries.shape, jnp.bfloat16),
+        jax.ShapeDtypeStruct(window.shape, jnp.bfloat16),
+    ]
+    operands = (queries, window, bias_t, totals.transpose(0, 2, 1), d_heads)
+    return attend_call(attend_back_kernel, operands, "qwbtq", outs, "qw", rows, span, 5)
 
 
 def shards(
@@ -571,59 +808,59 @@
     first_core = core == 0
     tokens = inputs[0].astype(jnp.float32)
 
-    conv_weight, conv_bias, step_bias, log_decay, skip_gain = (
-        to_channels(v) for v in (conv_weight, conv_bias, step_bias, log_decay, skip_gain)
-    )
-
     d_rows = w_query.shape[0]
     c_rows = w_select.shape[0]
     sel_half, step_half = w_select.shape[1], w_step.shape[1]
-    mamba_in = to_channels(w_mamba_in)
-    cut_a, cut_b = 1024, 2176
-    plane_b = plane(mamba_in[:, cut_a:cut_b], ORDER_B)
-    in_b = ring_pieces(plane_b, ORDER_B[1])
-    plane_a = plane(after(mamba_in[:, :cut_a], plane_b), ORDER_A)
-    in_a = ring_pieces(plane_a, ORDER_A[1])
-    plane_c = plane(after(mamba_in[:, cut_b:], plane_a), ORDER_C)
-    in_c = ring_pieces(plane_c, ORDER_C[1])
+    mamba_in = w_mamba_in
+    cut_a, cut_b = 1408, 2816
+    mixed_c = inner - cut_b
+    planes = gather_planes(
+        (
+            mamba_in[:, :cut_a],
+            mamba_in[:, cut_a:cut_b],
+            jnp.concatenate([mamba_in[:, cut_b:], w_query, w_key, w_value], axis=1),
+        ),
+        ORDERS,
+    )
+    parts = [ring_pieces(a, order[1]) for a, order in zip(planes, ORDERS)]
+    half_width = width // 2
+    windows_in = [(0, a[0].shape[1]) for a in parts]
+    windows_out_a, window_out_b = ((0, half_width), (half_width, 2 * half_width)), (0, half_width)
     select_step = jnp.pad(
         jnp.concatenate([w_select, w_step], axis=1), ((0, 0), (0, 128 - sel_half - step_half))
     )
-    select_mine = shown(after(select_step, plane_c), ("xh", "xl", "y", "z")).reshape(inner, 128)
+    select_mine = shown(after(select_step, planes[2]), BLK_SEQ).reshape(inner, 128)
     select_got = other_core(select_mine)
     select_full = join_columns(select_mine[:, :sel_half], select_got[:, :sel_half])
     step_full = join_columns(
         select_mine[:, sel_half : sel_half + step_half], select_got[:, sel_half : sel_half + step_half]
     )
 
-    plane_out_a = plane(after(w_mamba_out, select_mine), ORDER_A)
-    mamba_out_a = in_order(ring_pieces(plane_out_a, ORDER_A[1]), ORDER_A[1])
-    qkv_shard = jnp.concatenate([w_query, w_key, w_value], axis=1)
-    plane_qkv = plane(after(qkv_shard, plane_out_a), ORDER_C)
-    qkv_c = ring_pieces(plane_qkv, ORDER_C[1])
-    plane_out_b = plane(after(w_attn_out, plane_qkv), ORDER_B)
-    attn_out_b = ring_pieces(plane_out_b, ORDER_B[1])
+    out_shards = (jnp.concatenate([w_mamba_out[:d_rows], w_mamba_out[d_rows:]], axis=1), w_attn_out)
 
     ff_rows = w_down.shape[0]
 
     def to_units(w):
-        split = w.reshape(d_rows, 4, 4, 2, ff_rows).transpose(2, 0, 3, 1, 4)
+        split = w.reshape(d_rows, 4, 4, 2, ff_rows).transpose(2, 0, 1, 3, 4)
         return jnp.pad(split, ((0, 0),) * 4 + ((0, FF_PAD - ff_rows),)).reshape(4, d_rows, 8 * FF_PAD)
 
     def from_units(g):
-        split = g.reshape(4, d_rows, 2, 4, FF_PAD)[..., :ff_rows]
-        return split.transpose(1, 3, 0, 2, 4).reshape(d_rows, 32 * ff_rows)
+        split = g.reshape(4, d_rows, 4, 2, FF_PAD)[..., :ff_rows]
+        return split.transpose(1, 2, 0, 3, 4).reshape(d_rows, 32 * ff_rows)
 
     units = 8 * FF_PAD
     gate_up = jnp.concatenate([to_units(w_gate), to_units(w_up)], axis=2)
-    gate_up = dealt(after(gate_up, plane_out_b), Z_RING).reshape(4 * d_rows, 2 * units)
-    gate_up = ring_pieces(ring_whole(gate_up, X_RING), Y_RING)
-    down_cols = jnp.pad(after(w_down, plane_c), ((0, FF_PAD - ff_rows), (0, 0)))
-    down_cols = in_order(ring_pieces(ring_in_order(down_cols, Y_RING), X_RING), X_RING)
-    down_low, down_high = down_cols[:units], down_cols[units:]
-    down_mine = jnp.where(first_core, down_low, down_high)
-    down_theirs = jnp.where(first_core, down_high, down_low)
-    down = join_columns(down_mine, other_core(down_theirs))
+    gate_up_dealt = dealt(after(gate_up, select_mine), Z_RING).reshape(4 * d_rows, 2 * units)
+    gate_up = gathered(jnp.pad(gate_up_dealt, ((0, LANES // 16 - 4 * d_rows), (0, 0))), ("xh", "y", "xl"))
+
+    here = lax.axis_index("xh") == core
+    down = jnp.pad(w_down, ((0, FF_PAD - ff_rows), (0, 0)))
+    down = join_columns(down, other_core(down))
+    down = jnp.where(here, down, received(down, "xh", 1))
+    down_shard = down
+    down = gathered(down, ("y", "xl"))
+
+    out_planes = gather_planes(out_shards, ORDERS[:2], (gate_up_dealt,))
 
     def group_tokens(a):
         return both_tokens(ring_whole(a, Z_RING))
@@ -632,44 +869,41 @@
         return ring_sum_whole(to_low(sum_cores(both)), Z_RING)
 
     grad_out = out_grad[0]
-    grad_out_group = group_tokens(after(grad_out, plane_c))
-
-    pick_a, pick_b, pick_c = (
-        one_hot(picker(order, d_rows), width) for order in (ORDER_A, ORDER_B, ORDER_C)
-    )
-    pick_ff = one_hot(ff_picker(d_rows), width)
-
-    def permuted(a, hot):
-        return to_low(product(a, hot))
+
+    pick_a, pick_b, pick_c = (picker(order, d_rows) for order in ORDERS)
+    pick_ff = ff_picker(d_rows)
+    pick_out = [picker(ORDER_A, d_rows, c_rows, k * d_rows) for k in (0, 1)]
 
     normed, norm_back = jax.vjp(rms_scale, tokens, norm_gain)
-    normed_low = to_low(normed)
-    normed_chip = both_tokens(normed_low)
-    normed_a, normed_b, normed_c = (permuted(normed_chip, hot) for hot in (pick_a, pick_b, pick_c))
-
-    mixed_half = jnp.concatenate(
-        [by_pieces(normed_a, in_a), by_pieces(normed_b, in_b), by_pieces(normed_c, in_c)], axis=1
-    )
-    mixed_mine = mixed_half[:rows_dev]
-    mixed_got = other_core(to_low(mixed_half[rows_dev:]))
-    conv_in = jnp.where(first_core, to_low(mixed_mine), mixed_got)
-    gate_z = jnp.where(first_core, mixed_got.astype(jnp.float32), mixed_mine)
-
-    qkv_half = to_low(by_pieces(normed_c, qkv_c))
+    normed_chip = both_tokens(to_low(normed))
+    normed_a, normed_b, normed_c = turned((normed_chip,) * 3, (pick_a, pick_b, pick_c))
+    normed_c = after(normed_c, out_planes[0], down_shard)
+
     q_cols, k_cols = w_query.shape[1], w_key.shape[1]
-    qkv_mine, qkv_got = qkv_half[:rows_dev], other_core(qkv_half[rows_dev:])
+    projected = [
+        by_pieces((left,), pieces, (window,))
+        for left, pieces, window in zip((normed_a, normed_b, normed_c), parts, windows_in)
+    ]
+    mixed_mine = jnp.concatenate([a[:rows_dev] for a in projected], axis=1)
+    mixed_got = other_core(jnp.concatenate([a[rows_dev:] for a in projected], axis=1))
+    conv_in = jnp.where(first_core, mixed_mine[:, :inner], mixed_got[:, :inner])
+    gate_z = jnp.where(first_core, mixed_got[:, :inner], mixed_mine[:, :inner]).astype(jnp.float32)
+    qkv_cols = q_cols + 2 * k_cols
+    qkv_mine, qkv_got = (a[:, inner : inner + qkv_cols] for a in (mixed_mine, mixed_got))
     queries = join_columns(qkv_mine[:, :q_cols], qkv_got[:, :q_cols])
     keys_low = join_columns(qkv_mine[:, q_cols : q_cols + k_cols], qkv_got[:, q_cols : q_cols + k_cols])
     values_low = join_columns(qkv_mine[:, q_cols + k_cols :], qkv_got[:, q_cols + k_cols :])
-
-    edge_rows = shifted(conv_in[rows_dev - edge_count :], 1)
-    key_value = jnp.concatenate([keys_low, values_low], axis=1)
-    along_z = lax.axis_index(Z_RING)
+    key_value = jnp.stack([a.reshape(rows_dev, KV_HEADS, HEAD_DIM) for a in (keys_low, values_low)], axis=2)
+    key_value = key_value.reshape(rows_dev, 2 * KV_HEADS * HEAD_DIM)
+
+    mamba_out_a, attn_out_b = (
+        ring_pieces(after(a, conv_in), order[1]) for a, order in zip(out_planes, ORDERS)
+    )
+    grad_out_group = group_tokens(jnp.pad(after(grad_out, conv_in), ((0, 0), (0, LANES - width))))
+
     kv_cols = KV_HEADS * HEAD_DIM
-    row = ring_in_order(key_value, Z_RING).reshape(4, rows_dev, 2 * kv_cols)
-    window = jnp.concatenate([shifted(row, 2, ROWS), shifted(row, 1, ROWS), row])
-    window = lax.dynamic_slice_in_dim(window, along_z, reach_blocks + 1).reshape(-1, key_value.shape[1])
-    window_keys, window_values = window[:, :kv_cols], window[:, kv_cols:]
+    window = jnp.concatenate([shifted(key_value, d) for d in range(reach_blocks, 0, -1)] + [key_value], axis=0)
+    edge_rows = after(shifted(conv_in[rows_dev - edge_count :], 1), out_planes[1])
 
     padded_in = jnp.concatenate([edge_rows, conv_in], axis=0).astype(jnp.float32)
     conved, conv_back = jax.vjp(conv_silu, padded_in, conv_weight, conv_bias)
@@ -682,13 +916,14 @@
     step_pre = product_nt(step_raw, step_full)
     (step_size, decay_rate), rate_back = jax.vjp(rate_piece, step_pre, step_bias, log_decay)
     total_step = jnp.sum(step_size, axis=0)
-    drive = step_size * conv_values
+    drive = after(step_size * conv_values, window)
     in_lanes, out_lanes = lanes(in_mat), lanes(out_mat)
     end_state = scan_state(step_size, drive, in_lanes, decay_rate)
+    queries = after(queries, end_state)
     state_in = chain_carry(total_step, end_state, decay_rate, False)
     scan_out = scan_full(step_size, drive, in_lanes, out_lanes, decay_rate, state_in)
     gated, gate_back = jax.vjp(gate_piece, scan_out, conv_values, gate_z, skip_gain)
-    gated_low = to_low(gated)
+    gated_low = after(to_low(gated), grad_out_group)
 
     span_keys = (reach_blocks + 1) * rows_dev
     segment_row = segment_ids[0]
@@ -701,29 +936,20 @@
         span_keys, dtype=jnp.int32
     )[None, :]
     allowed = (gaps >= 0) & (gaps < WINDOW) & (query_segs[:, None] == key_segs[None, :])
-    head_outputs = []
-    log_totals = []
-    for group_index in range(KV_HEADS):
-        scores, query_part, key_part = group_scores(
-            queries, window_keys, allowed, group_index, group_size, score_scale
-        )
-        row_max = jnp.max(scores, axis=-1, keepdims=True)
-        exp_scores = jnp.exp(scores - row_max)
-        row_total = jnp.sum(exp_scores, axis=-1, keepdims=True)
-        log_totals.append(row_max + jnp.log(row_total))
-        weights_low = to_low(exp_scores / row_total)
-        value_part = window_values[:, group_index * HEAD_DIM : (group_index + 1) * HEAD_DIM]
-        head_outputs.append(
-            jnp.einsum(
-                "gqs,sd->qgd", weights_low, value_part, preferred_element_type=jnp.float32
-            ).reshape(rows_dev, group_size * HEAD_DIM)
-        )
-    heads_low = to_low(jnp.concatenate(head_outputs, axis=1))
-
-    heads_b = both_tokens(permuted(heads_low, pick_b))
-    gated_chip = both_tokens(gated_low)
-    branch_out = jnp.concatenate([by_pieces(heads_b, attn_out_b), product(gated_chip, mamba_out_a)], axis=1)
-    half_width = width // 2
+    queries_by_group = by_groups(queries)
+    heads_by_group, score_totals = attend(queries_by_group, window, jnp.where(allowed, 0.0, -1e30))
+    heads_low = from_groups(heads_by_group)
+
+    heads_b, *gated_a = (
+        both_tokens(a) for a in turned((heads_low, gated_low, gated_low), (pick_b, *pick_out))
+    )
+    branch_out = jnp.concatenate(
+        [
+            by_pieces((heads_b,), attn_out_b, (window_out_b,), False),
+            by_pieces(gated_a, mamba_out_a, windows_out_a, False),
+        ],
+        axis=1,
+    )
     out_mine, out_got = branch_out[:rows_dev], other_core(branch_out[rows_dev:])
     attn_out = join_columns(out_mine[:, :half_width], out_got[:, :half_width])
     mamba_out = join_columns(out_mine[:, half_width:], out_got[:, half_width:])
@@ -731,35 +957,23 @@
         merge_piece, tokens, attn_out, mamba_out, attn_gain, mamba_gain
     )
     normed_two, norm_two_back = jax.vjp(rms_scale, hidden_mid, ffn_norm_gain)
-    normed_two_ff = group_tokens(permuted(to_low(normed_two), pick_ff))
-    gate_up_val = by_pieces(normed_two_ff, gate_up)
-    act_val, act_back = jax.vjp(swiglu, gate_up_val[:, :units], gate_up_val[:, units:])
-    act_low = to_low(act_val)
-    d_act = product_nt(grad_out_group, down)
-    d_gate, d_up = act_back(d_act)
-    d_gate_up = jnp.concatenate([to_low(d_gate), to_low(d_up)], axis=1)
-    d_normed_two = group_sum(by_pieces_nt(d_gate_up, gate_up))
-    grad_gate_up = grad_pieces(normed_two_ff, d_gate_up)
-    grad_down = to_low(product_tn(act_low, grad_out_group))
-    output = to_low(hidden_mid + group_sum(product(act_low, down)))[None]
-
-    gate_up_sum = ring_sum_whole(to_low(ring_sum(grad_gate_up, Y_RING)), X_RING)
-    gate_up_sum = dealt(to_low(gate_up_sum).reshape(4, d_rows, 2 * units), Z_RING).astype(jnp.float32)
+    normed_two_ff = group_tokens(turned((to_low(normed_two),), (pick_ff,))[0])
+    act_low, d_gate_up, down_part, d_part = feed_forward(normed_two_ff, grad_out_group, gate_up, down)
+    d_cores = to_low(sum_cores(d_part))
+    d_normed_two = ring_sum_whole(d_cores, Z_RING)
+    act_low, d_gate_up = together((act_low, d_gate_up, d_cores))[:2]
+    grad_gate_up, grad_down = feed_grads(normed_two_ff, d_gate_up, act_low, grad_out_group)
+
+    gate_up_sum = scattered(grad_gate_up, ("xh", "y", "xl"))[: 4 * d_rows].reshape(4, d_rows, 2 * units)
+    gate_up_sum = dealt(gate_up_sum, Z_RING).astype(jnp.float32)
     grad_gate, grad_up = from_units(gate_up_sum[..., :units]), from_units(gate_up_sum[..., units:])
-    down_l, down_r = jnp.split(grad_down, 2, axis=1)
-    down_mine = jnp.where(first_core, down_l, down_r)
-    down_got = other_core(jnp.where(first_core, down_r, down_l))
-    grad_down = jnp.concatenate(
-        [jnp.where(first_core, down_mine, down_got), jnp.where(first_core, down_got, down_mine)], axis=0
-    )
-    grad_down = to_low(ring_sum(turned_pieces(grad_down, X_RING), X_RING))
-    grad_down = ring_sum_in_order(grad_down, Y_RING)[:ff_rows]
-
-    def unpermuted(a, hot):
-        high = lax.reduce_precision(a, 8, 7)
-        return product_nt(to_low(high), hot) + product_nt(to_low(a - high), hot)
-
-    d_mid_norm, grad_ffn_norm = norm_two_back(unpermuted(d_normed_two, pick_ff))
+    grad_down = scattered(grad_down, ("y", "xl")).astype(jnp.float32)
+    grad_down = grad_down + received(to_low(grad_down), "xh", 1).astype(jnp.float32)
+    down_l, down_r = grad_down[:ff_rows, :half_width], grad_down[:ff_rows, half_width:]
+    down_got = other_core(to_low(jnp.where(first_core, down_r, down_l))).astype(jnp.float32)
+    grad_down = jnp.where(here, jnp.where(first_core, down_l, down_r), down_got)
+
+    d_mid_norm, grad_ffn_norm = norm_two_back(turned_back((d_normed_two,), (pick_ff,), False)[0])
     d_mid = grad_out.astype(jnp.float32) + d_mid_norm
     d_tokens_res, d_attn_out, d_mamba_out, grad_attn_gain, grad_mamba_gain = merge_back(d_mid)
     d_attn_low, d_mamba_low = to_low(d_attn_out), to_low(d_mamba_out)
@@ -769,62 +983,50 @@
     )
     d_branch_half = own_columns(d_branch)
     d_attn_half, d_mamba_half = d_branch_half[:, :half_width], d_branch_half[:, half_width:]
-    d_gated = sum_cores(product_nt(d_mamba_half, mamba_out_a))
-    d_heads_b = sum_cores(by_pieces_nt(d_attn_half, attn_out_b))
-    d_heads = to_low(product_nt(to_low(d_heads_b), pick_b))
-    grad_attn_out = plane_sum(ring_sum(grad_pieces(heads_b, d_attn_half), ORDER_B[1]), ORDER_B, d_rows)
-    grad_mamba_out = turned_pieces(to_low(product_tn(gated_chip, d_mamba_half)), ORDER_A[1])
-    grad_mamba_out = plane_sum(ring_sum(grad_mamba_out, ORDER_A[1]), ORDER_A, c_rows)
-
-    query_grads = []
-    key_grads = []
-    value_grads = []
-    for group_index in range(KV_HEADS):
-        scores, query_part, key_part = group_scores(
-            queries, window_keys, allowed, group_index, group_size, score_scale
-        )
-        weights_now = jnp.exp(scores - log_totals[group_index])
-        weights_low = to_low(weights_now)
-        value_part = window_values[:, group_index * HEAD_DIM : (group_index + 1) * HEAD_DIM]
-        head_grad = d_heads[
-            :, group_index * group_size * HEAD_DIM : (group_index + 1) * group_size * HEAD_DIM
-        ].reshape(rows_dev, group_size, HEAD_DIM)
-        d_weights = jnp.einsum(
-            "qgd,sd->gqs", head_grad, value_part, preferred_element_type=jnp.float32
-        )
-        d_scores = to_low(
-            weights_now * (d_weights - jnp.sum(weights_now * d_weights, axis=-1, keepdims=True))
-        )
-        query_grads.append(
-            jnp.einsum(
-                "gqs,sd->qgd", d_scores, key_part, preferred_element_type=jnp.float32
-            ).reshape(rows_dev, group_size * HEAD_DIM)
-            * score_scale
-        )
-        key_grads.append(
-            jnp.einsum("gqs,qgd->sd", d_scores, query_part, preferred_element_type=jnp.float32)
-            * score_scale
-        )
-        value_grads.append(
-            jnp.einsum("gqs,qgd->sd", weights_low, head_grad, preferred_element_type=jnp.float32)
-        )
-    d_queries = to_low(jnp.concatenate(query_grads, axis=1))
-    d_window = jnp.concatenate(key_grads + value_grads, axis=1)
-    d_rows_z = jnp.zeros((12, rows_dev, d_window.shape[1]), jnp.bfloat16)
-    d_rows_z = lax.dynamic_update_slice_in_dim(
-        d_rows_z, to_low(d_window).reshape(reach_blocks + 1, rows_dev, -1), along_z, 0
-    )
-    d_row = (
-        d_rows_z[8:].astype(jnp.float32)
-        + shifted(d_rows_z[4:8], -1, ROWS).astype(jnp.float32)
-        + shifted(d_rows_z[:4], -2, ROWS).astype(jnp.float32)
-    )
-    d_key_value = ring_sum_in_order(to_low(d_row).reshape(4 * rows_dev, 2 * kv_cols), Z_RING)
-    d_keys, d_values = to_low(d_key_value[:, :kv_cols]), to_low(d_key_value[:, kv_cols:])
+    d_gated_a = by_pieces_nt((d_mamba_half, d_mamba_half), mamba_out_a, windows_out_a)
+    d_heads_b = by_pieces_nt((d_attn_half,), attn_out_b, (window_out_b,))
+    d_branch = to_low(sum_cores(jnp.concatenate([*d_gated_a, *d_heads_b], axis=1)))
+    d_gated_a, d_heads_b = [d_branch[:, k * LANES : (k + 1) * LANES] for k in (0, 1)], d_branch[:, 2 * LANES :]
+    d_gated = turned_back(d_gated_a, pick_out, False, True, inner)[0]
+    d_heads = turned_back((d_heads_b,), (pick_b,), True)[0]
 
     d_scan, d_conv_gate, d_gate_z, grad_skip = gate_back(d_gated)
     d_state_in = adjoint_state(step_size, d_scan, out_lanes, decay_rate)
-    d_end = chain_carry(total_step, d_state_in, decay_rate, True)
+    d_heads, d_attn_half, d_mamba_half, down_part = together(
+        (d_heads, d_attn_half, d_mamba_half, down_part, d_state_in)
+    )[:4]
+    output = to_low(hidden_mid + group_sum(down_part)[:, :width])[None]
+
+    d_queries, d_window = attend_back(
+        queries_by_group, window, jnp.where(allowed.T, 0.0, -1e30), score_totals, by_groups(d_heads)
+    )
+    d_queries = from_groups(d_queries)
+    d_key_value = d_window[reach_blocks * rows_dev :].astype(jnp.float32)
+    for d in range(1, reach_blocks + 1):
+        piece = d_window[(reach_blocks - d) * rows_dev : (reach_blocks - d + 1) * rows_dev]
+        d_key_value = d_key_value + shifted(piece, -d).astype(jnp.float32)
+    d_key_value = to_low(d_key_value).reshape(rows_dev, KV_HEADS, 2, HEAD_DIM)
+    d_keys, d_values = (d_key_value[:, :, k].reshape(rows_dev, kv_cols) for k in (0, 1))
+
+    kv_half = kv_cols // 2
+    d_qkv_half = own_columns(
+        jnp.concatenate(
+            [
+                d_queries[:, :q_cols],
+                d_keys[:, :kv_half],
+                d_values[:, :kv_half],
+                d_queries[:, q_cols:],
+                d_keys[:, kv_half:],
+                d_values[:, kv_half:],
+            ],
+            axis=1,
+        )
+    )
+    rings = sum_rings(
+        (grad_pieces(gated_a, d_mamba_half, HALVES), grad_pieces((heads_b,), d_attn_half, HALVES)), ORDERS[:2]
+    )
+
+    d_end = chain_carry(total_step, d_state_in, decay_rate, True, rings)
     d_step, d_conv_scan, d_rate, d_in_mat, d_out_mat = scan_back(
         step_size, conv_values, d_scan, in_lanes, out_lanes, decay_rate, state_in, d_end
     )
@@ -840,55 +1042,41 @@
     d_conv_in = d_padded[edge_count:] + jnp.concatenate(
         [jnp.zeros((rows_dev - edge_count, inner), jnp.float32), edge_back], axis=0
     )
+    d_conv_in = after(d_conv_in, gate_up_sum)
     d_mixed_half = own_columns(to_low(jnp.concatenate([d_conv_in, d_gate_z], axis=1)))
-    kv_half = kv_cols // 2
-    d_qkv_half = own_columns(
-        jnp.concatenate(
-            [
-                d_queries[:, : q_cols],
-                d_keys[:, :kv_half],
-                d_values[:, :kv_half],
-                d_queries[:, q_cols :],
-                d_keys[:, kv_half:],
-                d_values[:, kv_half:],
-            ],
-            axis=1,
-        )
-    )
-    d_mixed_a, d_mixed_b = d_mixed_half[:, :cut_a], d_mixed_half[:, cut_a:cut_b]
-    d_mixed_c = jnp.concatenate([d_mixed_half[:, cut_b:], d_qkv_half], axis=1)
-
-    both_halves = [
-        jnp.pad(
-            jnp.concatenate([sel, stp], axis=1), ((0, 0), (0, 128 - sel_half - step_half))
-        )
-        for sel, stp in zip(jnp.split(grad_select, 2, axis=1), jnp.split(grad_step_w, 2, axis=1))
-    ]
-    select_mine = jnp.where(first_core, both_halves[0], both_halves[1])
-    select_theirs = jnp.where(first_core, both_halves[1], both_halves[0])
-    select_sum = to_low(select_mine + other_core(to_low(select_theirs)).astype(jnp.float32))
-    select_sum = summed(select_sum.reshape(64, c_rows, 128), ("xh", "xl", "y", "z"))
-    ring_a = ring_sum(grad_pieces(normed_a, d_mixed_a), ORDER_A[1])
-    ring_b = ring_sum(grad_pieces(normed_b, d_mixed_b), ORDER_B[1])
-    ring_c = ring_sum(grad_pieces(normed_c, d_mixed_c), ORDER_C[1])
-    sum_a = plane_sum(ring_a, ORDER_A, d_rows)
-    sum_b = plane_sum(ring_b, ORDER_B, d_rows)
-    sum_c = plane_sum(ring_c, ORDER_C, d_rows)
-    mixed_c = inner - cut_b
-    grad_mamba_in = from_channels(
-        jnp.concatenate([sum_a, sum_b, sum_c[:, :mixed_c]], axis=1)
-    )
-    grad_query = sum_c[:, mixed_c : mixed_c + q_cols]
-    grad_key = sum_c[:, mixed_c + q_cols : mixed_c + q_cols + k_cols]
-    grad_value = sum_c[:, mixed_c + q_cols + k_cols :]
-    grad_select, grad_step = select_sum[:, :sel_half], select_sum[:, sel_half : sel_half + step_half]
-
-    d_normed_c = by_pieces_nt(d_mixed_c[:, :mixed_c], in_c) + by_pieces_nt(d_qkv_half, qkv_c)
-    d_normed = (
-        product_nt(to_low(by_pieces_nt(d_mixed_a, in_a)), pick_a)
-        + product_nt(to_low(by_pieces_nt(d_mixed_b, in_b)), pick_b)
-        + product_nt(to_low(d_normed_c), pick_c)
-    )
+    d_mixed_a, d_mixed_b, d_mixed_c = (
+        d_mixed_half[:, :cut_a],
+        d_mixed_half[:, cut_a:cut_b],
+        jnp.concatenate([d_mixed_half[:, cut_b:], d_qkv_half], axis=1),
+    )
+
+    ring_a, ring_b, ring_c = sum_rings(
+        [
+            grad_pieces((left,), grad, HALVES)
+            for left, grad in ((normed_a, d_mixed_a), (normed_b, d_mixed_b), (normed_c, d_mixed_c))
+        ],
+        ORDERS,
+    )
+    sum_a, sum_b, sum_c = sum_planes(
+        [jnp.concatenate([ring_a, rings[0]], axis=1), jnp.concatenate([ring_b, rings[1]], axis=1), ring_c], ORDERS
+    )
+    sum_a, out_sum_a = sum_a[:, :cut_a], sum_a[:, cut_a:]
+    sum_b, grad_attn_out = sum_b[:, : cut_b - cut_a], sum_b[:, cut_b - cut_a :]
+    grad_mamba_out = jnp.concatenate([out_sum_a[:, :half_width], out_sum_a[:, half_width:]], axis=0)
+    grad_mamba_in = jnp.concatenate([sum_a, sum_b, sum_c[:, :mixed_c]], axis=1)
+    grad_qkv = sum_c[:, mixed_c:]
+    grad_query = grad_qkv[:, :q_cols]
+    grad_key, grad_value = grad_qkv[:, q_cols : q_cols + k_cols], grad_qkv[:, q_cols + k_cols :]
+
+    d_normed = turned_back(
+        [
+            by_pieces_nt((grad,), pieces, (window,))[0]
+            for grad, pieces, window in zip((d_mixed_a, d_mixed_b, d_mixed_c), parts, windows_in)
+        ],
+        (pick_a, pick_b, pick_c),
+        False,
+        True,
+    )[0]
     d_tokens_norm, grad_norm = norm_back(sum_cores(d_normed))
     input_grad = to_low(d_tokens_res + d_tokens_norm)[None]
 
@@ -905,11 +1093,19 @@
     )
     channel_rows = [a.reshape(-1, inner) for a in smalls[1:6]]
     gains = jnp.concatenate([smalls[0], *smalls[6:]]).reshape(-1, inner)
-    totals = sum_all(jnp.concatenate([gains, *channel_rows]))
+    select_rows = jnp.stack(
+        [
+            jnp.pad(jnp.concatenate([sel, stp], axis=1), ((0, 0), (0, 128 - sel_half - step_half)))
+            for sel, stp in zip(jnp.split(grad_select, 2, axis=1), jnp.split(grad_step_w, 2, axis=1))
+        ]
+    )
+    select_rows = select_rows.reshape(128, c_rows, 128)
+    totals, select_sum = sum_all(jnp.concatenate([gains, *channel_rows]), select_rows)
+    grad_select, grad_step = select_sum[:, :sel_half], select_sum[:, sel_half : sel_half + step_half]
     gain_sums = totals[: gains.shape[0]].reshape(4, width)
     at, channel_sums = gains.shape[0], []
     for a in channel_rows:
-        channel_sums.append(from_channels(totals[at : at + a.shape[0]]))
+        channel_sums.append(totals[at : at + a.shape[0]])
         at += a.shape[0]
     totals = [
         gain_sums[0],

time: 1320 us -> 1250 us (0.947)
  matrix products: 263 us -> 12.9 us
  Pallas kernels: 54.4 us -> 196 us
  waiting for transfers between devices: 292 us -> 331 us
    pallas_call x0 -> x26, Pallas kernels: none -> 142 us  [the longest x23 88.7 us: whole_call(): pl.pallas_call(kernel, out_shape=outs, in_specs=[pl.BlockSpec(memory_spac...]
    dot_general x39 -> x2, matrix products: 91.9 us -> 3.95 us  [product(): return jnp.dot(left, right, preferred_element_type=jnp.float32)]
    dot_general x40 -> x2, matrix products: 84.4 us -> 8.22 us  [product_nt(): lax.dot_general(left, right, (((1,), (1,)), ((), ())), preferred_element_...]
    dot_general x29 -> x2, matrix products: 51.5 us -> 0.74 us  [product_tn(): lax.dot_general(left, right, (((0,), (0,)), ((), ())), preferred_element_...]
    ppermute x6 -> x18, starting transfers between devices: 10.9 us -> 52.7 us  [shifted(): lax.ppermute(a, axis, [(i - distance, i) for i in range(n) if 0 <= i - di...]
    ppermute x110 -> x72, waiting for transfers between devices: 141 us -> 180 us  [received(): return lax.ppermute(a, axis, [((i + d) % n, i) for i in range(n)])]
    unnamed x600 -> x532, local copies, waits for them, and re-layouts: 37.2 us -> 74.8 us
    dot_general x30 -> x0, matrix products: 34.9 us -> none  [the longest x5 13 us: shards(): jnp.einsum('qgd,sd->gqs', head_grad, value_part, preferred_element_type=j...]
  transfers between devices with their start and end apart: 137 -> 111, of which waited for: 44 -> 41; matrix products, arithmetic and copies ran while one was open for 44% -> 26% of each run, Pallas kernels for 4% -> 14%
where the time goes in v2:
time: 1250 us; the launch traced here: 1240 us
  waiting for transfers between devices  331 us (26%)
  starting transfers between devices  312 us (25%)
  local copies, waits for them, and re-layouts  229 us (18%)
  Pallas kernels  196 us (16%)
  other arithmetic  139 us (11%)
  between operations  18.1 us (1%)
  matrix products  12.9 us (1%)
    ppermute x72, waiting for transfers between devices, received(): return lax.ppermute(a, axis, [((i + d) % n, i) for i in range(n)])  180 us
    all_to_all x17, waiting for transfers between devices, dealt(): return lax.all_to_all(blocks, axis, 0, 0, tiled=True)  147 us
    all_to_all x17, starting transfers between devices, dealt(): return lax.all_to_all(blocks, axis, 0, 0, tiled=True)  138 us
    ppermute x72, starting transfers between devices, received(): return lax.ppermute(a, axis, [((i + d) % n, i) for i in range(n)])  121 us
    pallas_call x23, Pallas kernels, whole_call(): pl.pallas_call(kernel, out_shape=outs, in_specs=[pl.BlockSpec(memory_spac...  88.7 us
    unnamed x532, local copies, waits for them, and re-layouts  74.8 us
    ppermute x18, starting transfers between devices, shifted(): lax.ppermute(a, axis, [(i - distance, i) for i in range(n) if 0 <= i - di...  52.7 us
    pallas_call x4, Pallas kernels, scan_call(): pl.pallas_call(kernel, grid=(channels // SCAN_TILE,), in_specs=[kinds[k]...  48.6 us
  transfers between devices with their start and end apart: 111, of which 41 were waited for; matrix products, arithmetic and copies ran while one was open for 26% of the time, Pallas kernels for 14%

profile of v2, /device:TPU:0, one launch (start us, length us, event | category | flops | bytes accessed | tf_op | source)
XLA Modules:
  0.0 1237.7 jit_solution(15206963410237374829)
XLA Ops:
  11.6 8.3 all-to-all-start
  23.9 18.5 %all-to-all-done = bf16[16,25,1408]{2,1,0:T(8,128)(2,1)} async-done(((bf16[16,25,1408]{2,1,0:T(8,128)(2,1)}), bf16[16,25,1408]{2,1,0:T(8,128)(2,1)}, u32[]{:S(2)}, u32[]{:S(2)}) %all-to-all-start) | async-done | bytes 1126432 | tf_op jit(solution)/shard_map/all_to_all | solution.py:51
  57.2 15.6 %all-to-all-done.1 = bf16[16,25,1408]{2,1,0:T(8,128)(2,1)} async-done(((bf16[16,25,1408]{2,1,0:T(8,128)(2,1)}), bf16[16,25,1408]{2,1,0:T(8,128)(2,1)}, u32[]{:S(2)}, u32[]{:S(2)}) %all-to-all-start.1) | async-done | bytes 1126432 | tf_op jit(solution)/shard_map/all_to_all | solution.py:51
  90.3 32.8 %all-to-all-done.2 = bf16[16,25,1504]{2,1,0:T(8,128)(2,1)} async-done(((bf16[16,25,1504]{2,1,0:T(8,128)(2,1)}), bf16[16,25,1504]{2,1,0:T(8,128)(2,1)}, u32[]{:S(2)}, u32[]{:S(2)}) %all-to-all-start.2) | async-done | bytes 1203232 | tf_op jit(solution)/shard_map/all_to_all | solution.py:51
  132.9 18.5 %collective-permute-done.9.refs_5_ = bf16[400,1408]{1,0:T(8,128)(2,1)} collective-permute-done((bf16[400,1408]{1,0:T(8,128)(2,1)S(1)}, bf16[400,1408]{1,0:T(8,128)(2,1)}, u32[]{:S(2)}, u32[]{:S(2)}) %collective-permute-start.9) | collective-permute-done | bytes 1126432 | tf_op jit(solution)/shard_map/ppermute | solution.py:34
  213.6 18.6 %collective-permute-done.14.refs_4_ = bf16[200,1408]{1,0:T(8,128)(2,1)S(1)} collective-permute-done((bf16[200,1408]{1,0:T(8,128)(2,1)}, bf16[200,1408]{1,0:T(8,128)(2,1)S(1)}, u32[]{:S(2)}, u32[]{:S(2)}) %collective-permute-start.14) | collective-permute-done | bytes 563232 | tf_op jit(solution)/shard_map/ppermute | solution.py:34
  260.7 19.9 %all-to-all-done.6 = bf16[16,25,800]{2,1,0:T(8,128)(2,1)} async-done(((bf16[16,25,800]{2,1,0:T(8,128)(2,1)}), bf16[16,25,800]{2,1,0:T(8,128)(2,1)}, u32[]{:S(2)}, u32[]{:S(2)}) %all-to-all-start.6) | async-done | bytes 640032 | tf_op jit(solution)/shard_map/all_to_all | solution.py:51
  356.4 9.6 collective-permute-start.31
  377.7 21.8 %all-to-all-start.7 = ((bf16[64,18,128]{2,1,0:T(8,128)(2,1)}), bf16[64,18,128]{2,1,0:T(8,128)(2,1)}, u32[]{:S(2)}, u32[]{:S(2)}) async-start(bf16[64,18,128]{2,1,0:T(8,128)(2,1)} %bitcast.112), calls=%async_computation.7 | async-start | bytes 786432 | tf_op jit(solution)/shard_map/all_to_all | solution.py:51
  406.9 13.6 %shard_map.593 = (bf16[5,128,320]{2,1,0:T(8,128)(2,1)S(1)}, f32[5,128,8]{2,1,0:T(8,128)S(1)}) custom-call(bf16[5,128,320]{2,1,0:T(8,128)(2,1)S(1)} %bitcast.97, bf16[1152,640]{1,0:T(8,128)(2,1)S(1)} %copy-done.107, f32[128,1152]{1,0:T(8,128)S(1)} %copy-done.91), custom_call_target="tpu_custom_call" | custom-call | flops 943718400 | bytes 589824 | tf_op jit(solution)/shard_map/pallas_call | solution.py:731
  437.1 10.6 all-to-all-start.8
  457.6 9.6 all-to-all-done.8
  473.5 10.7 shard_map.595
  507.4 11.2 collective-permute-done.40.refs_5_
  543.8 10.1 collective-permute-done.42
  556.6 8.0 collective-permute-done.44
  571.3 23.7 %shard_map.600 = (bf16[1024,704]{1,0:T(8,128)(2,1)S(1)}, bf16[1024,1408]{1,0:T(8,128)(2,1)}, bf16[1024,1664]{1,0:T(8,128)(2,1)}, bf16[1024,1664]{1,0:T(8,128)(2,1)}) custom-call(bf16[1024,1664]{1,0:T(8,128)(2,1)} %constant_dynamic-update-slice_fusion.20.x_ref, bf16[1024,1664]{1,0:T(8,128)(2,1)} %constant_dynamic-update-slice_fusion.9.g_ref, ...), custom_call_target="tpu_custom_call" | custom-call | flops 14394851328 | bytes 17956864 | tf_op jit(solution)/shard_map/pallas_call | solution.py:301
  606.2 11.1 shard_map.611
  676.2 16.0 %shard_map.614 = (bf16[5,128,320]{2,1,0:T(8,128)(2,1)S(1)}, bf16[1152,640]{1,0:T(8,128)(2,1)S(1)}) custom-call(bf16[5,128,320]{2,1,0:T(8,128)(2,1)S(1)} %bitcast.98, bf16[1152,640]{1,0:T(8,128)(2,1)S(1)} %copy-done.108, f32[1152,128]{1,0:T(8,128)S(1)} %copy-done.92, f32[5,8,128]{2,1,0:T(8,128)S(1)} %bitcast.102, bf16[5,128,320]{2,1,0:T(8,128)(2,1)S(1)} %bitcast.100), custom_call_target="tpu_custom_call" | custom-call | flops 2359296000 | bytes 589824 | tf_op jit(solution)/shard_map/pallas_call | solution.py:731
  709.0 14.1 %all-to-all-start.9 = ((bf16[64,18,128]{2,1,0:T(8,128)(2,1)}), bf16[64,18,128]{2,1,0:T(8,128)(2,1)}, u32[]{:S(2)}, u32[]{:S(2)}) async-start(bf16[64,18,128]{2,1,0:T(8,128)(2,1)} %bitcast.111), calls=%async_computation.9 | async-start | bytes 786432 | tf_op jit(solution)/shard_map/all_to_all | solution.py:51
  750.8 9.7 collective-permute-start.56
  817.0 11.6 collective-permute-done.57
  828.5 12.1 collective-permute-done.59
  844.0 19.3 %all-to-all-start.10 = ((bf16[64,16,128]{2,1,0:T(8,128)(2,1)}), bf16[64,16,128]{2,1,0:T(8,128)(2,1)}, u32[]{:S(2)}, u32[]{:S(2)}) async-start(bf16[64,16,128]{2,1,0:T(8,128)(2,1)} %convert_element_type.399), calls=%async_computation.10 | async-start | bytes 524288 | tf_op jit(solution)/shard_map/all_to_all | solution.py:51
  880.7 26.5 %shard_map.610 = (f32[128,3200]{1,0:T(8,128)S(1)}, f32[128,3200]{1,0:T(8,128)S(1)}, f32[16,3200]{1,0:T(8,128)S(1)}, f32[128,16,128]{2,1,0:T(8,128)S(1)}, f32[128,16,128]{2,1,0:T(8,128)S(1)}) custom-call(f32[128,3200]{1,0:T(8,128)S(1)} %copy-done.33, f32[128,3200]{1,0:T(8,128)S(1)} %copy-done.41, f32[128,3200]{1,0:T(8,128)S(1)} %copy-done.35, ...), custom_call_target="tpu_custom_call" | custom-call | flops 157286400 | bytes 6553600 | tf_op jit(solution)/shard_map/pallas_call | solution.py:645
  1029.6 26.3 %collective-permute-done.76 = bf16[200,1504]{1,0:T(8,128)(2,1)S(1)} collective-permute-done((bf16[200,1504]{1,0:T(8,128)(2,1)}, bf16[200,1504]{1,0:T(8,128)(2,1)S(1)}, u32[]{:S(2)}, u32[]{:S(2)}) %collective-permute-start.76) | collective-permute-done | bytes 601632 | tf_op jit(solution)/shard_map/ppermute | solution.py:34
  1077.3 14.8 %collective-permute-done.77 = bf16[400,1504]{1,0:T(8,128)(2,1)} collective-permute-done((bf16[400,1504]{1,0:T(8,128)(2,1)}, bf16[400,1504]{1,0:T(8,128)(2,1)}, u32[]{:S(2)}, u32[]{:S(2)}) %collective-permute-start.77) | collective-permute-done | bytes 1203232 | tf_op jit(solution)/shard_map/ppermute | solution.py:34
  1110.6 9.3 all-to-all-start.14
  1131.9 12.3 all-to-all-done.14
  1155.0 10.8 collective-permute-done.85
  1173.2 12.2 all-to-all-done.15
  1214.0 12.6 %all-to-all-done.16 = bf16[16,25,3008]{2,1,0:T(8,128)(2,1)} async-done(((bf16[16,25,3008]{2,1,0:T(8,128)(2,1)}), bf16[16,25,3008]{2,1,0:T(8,128)(2,1)}, u32[]{:S(2)}, u32[]{:S(2)}) %all-to-all-start.16) | async-done | bytes 2406432 | tf_op jit(solution)/shard_map/all_to_all | solution.py:51
  (1062 shorter events, 739.6 us)
Async XLA Ops:
  9.6 150.1 %collective-permute-start = (bf16[128,1600]{1,0:T(8,128)(2,1)S(1)}, bf16[128,1600]{1,0:T(8,128)(2,1)}, u32[]{:S(2)}, u32[]{:S(2)}) collective-permute-start(bf16[128,1600]{1,0:T(8,128)(2,1)S(1)} %fusion.19), channel_id=1, source_target_pairs={{64,0},{0,64},{65,1},{1,65},{66,2},{2,66},{67,3},{3,67},{68,4},{4,... | collective-permute-start | bytes 1228808 | tf_op jit(solution)/shard_map/ppermute | solution.py:34
  49.9 519.7 %all-gather.7.cloned.1.call-start = ((), (), s32[]{:S(2)}) async-start(), calls=%async_computation.20 | async-start | bytes 2635776 | tf_op jit(solution)/shard_map/all_gather | solution.py:168
  76.6 46.5 %all-to-all-start.2 = ((bf16[16,25,1504]{2,1,0:T(8,128)(2,1)}), bf16[16,25,1504]{2,1,0:T(8,128)(2,1)}, u32[]{:S(2)}, u32[]{:S(2)}) async-start(bf16[16,25,1504]{2,1,0:T(8,128)(2,1)} %broadcast_in_dim.44), calls=%async_computation.2 | async-start | bytes 3145728 | tf_op jit(solution)/shard_map/all_to_all | solution.py:51
  82.2 69.3 %collective-permute-start.9 = (bf16[400,1408]{1,0:T(8,128)(2,1)S(1)}, bf16[400,1408]{1,0:T(8,128)(2,1)}, u32[]{:S(2)}, u32[]{:S(2)}) collective-permute-start(bf16[400,1408]{1,0:T(8,128)(2,1)S(1)} %reshape.386.refs_1_), channel_id=1, source_target_pairs={{33,0},{0,1},{1,32},{32,33},{35,2},{2,3},{3,34},{34,35},{37,4},{4,... | collective-permute-start | bytes 3379208 | tf_op jit(solution)/shard_map/ppermute | solution.py:34
  84.0 70.7 %collective-permute-start.7 = (bf16[400,1408]{1,0:T(8,128)(2,1)S(1)}, bf16[400,1408]{1,0:T(8,128)(2,1)}, u32[]{:S(2)}, u32[]{:S(2)}) collective-permute-start(bf16[400,1408]{1,0:T(8,128)(2,1)S(1)} %reshape.386.refs_1_), channel_id=1, source_target_pairs={{1,0},{32,1},{33,32},{0,33},{3,2},{34,3},{35,34},{2,35},{5,4},{36,... | collective-permute-start | bytes 3379208 | tf_op jit(solution)/shard_map/ppermute | solution.py:34
  85.4 75.5 %collective-permute-start.11 = (bf16[400,1408]{1,0:T(8,128)(2,1)}, bf16[400,1408]{1,0:T(8,128)(2,1)}, u32[]{:S(2)}, u32[]{:S(2)}) collective-permute-start(bf16[400,1408]{1,0:T(8,128)(2,1)} %reshape.387.refs_1_), channel_id=1, source_target_pairs={{8,0},{16,8},{24,16},{0,24},{9,1},{17,9},{25,17},{1,25},{10,2},{18... | collective-permute-start | bytes 3379208 | tf_op jit(solution)/shard_map/ppermute | solution.py:34
  90.3 96.1 %collective-permute-start.13 = (bf16[400,1408]{1,0:T(8,128)(2,1)}, bf16[400,1408]{1,0:T(8,128)(2,1)}, u32[]{:S(2)}, u32[]{:S(2)}) collective-permute-start(bf16[400,1408]{1,0:T(8,128)(2,1)} %reshape.387.refs_1_), channel_id=1, source_target_pairs={{24,0},{0,8},{8,16},{16,24},{25,1},{1,9},{9,17},{17,25},{26,2},{2,... | collective-permute-start | bytes 3379208 | tf_op jit(solution)/shard_map/ppermute | solution.py:34
  151.5 54.6 %collective-permute-start.3 = (bf16[400,1504]{1,0:T(8,128)(2,1)S(1)}, bf16[400,1504]{1,0:T(8,128)(2,1)}, u32[]{:S(2)}, u32[]{:S(2)}) collective-permute-start(bf16[400,1504]{1,0:T(8,128)(2,1)S(1)} %reshape.388.refs_1_), channel_id=1, source_target_pairs={{2,0},{4,2},{6,4},{0,6},{3,1},{5,3},{7,5},{1,7},{10,8},{12,10},{14... | collective-permute-start | bytes 3609608 | tf_op jit(solution)/shard_map/ppermute | solution.py:34
  154.7 56.0 %collective-permute-start.5 = (bf16[400,1504]{1,0:T(8,128)(2,1)S(1)}, bf16[400,1504]{1,0:T(8,128)(2,1)}, u32[]{:S(2)}, u32[]{:S(2)}) collective-permute-start(bf16[400,1504]{1,0:T(8,128)(2,1)S(1)} %reshape.388.refs_1_), channel_id=1, source_target_pairs={{6,0},{0,2},{2,4},{4,6},{7,1},{1,3},{3,5},{5,7},{14,8},{8,10},{10,... | collective-permute-start | bytes 3609608 | tf_op jit(solution)/shard_map/ppermute | solution.py:34
  199.2 370.4 %all-gather.5.cloned.1.call-start = ((), (), s32[]{:S(2)}) async-start(), calls=%async_computation.19 | async-start | bytes 4978688 | tf_op jit(solution)/shard_map/all_gather | solution.py:168
  284.8 141.2 %collective-permute-start.26 = (bf16[128,1664]{1,0:T(8,128)(2,1)}, bf16[128,1664]{1,0:T(8,128)(2,1)}, u32[]{:S(2)}, u32[]{:S(2)}) collective-permute-start(bf16[128,1664]{1,0:T(8,128)(2,1)} %get-tuple-element.357), channel_id=1, source_target_pairs={{2,0},{4,2},{6,4},{0,6},{3,1},{5,3},{7,5},{1,7},{10,8},{12,10},{14... | collective-permute-start | bytes 1277960 | tf_op jit(solution)/shard_map/ppermute | solution.py:34
  285.4 140.6 %collective-permute-start.27 = (bf16[128,1664]{1,0:T(8,128)(2,1)}, bf16[128,1664]{1,0:T(8,128)(2,1)}, u32[]{:S(2)}, u32[]{:S(2)}) collective-permute-start(bf16[128,1664]{1,0:T(8,128)(2,1)} %get-tuple-element.357), channel_id=1, source_target_pairs={{4,0},{6,2},{0,4},{2,6},{5,1},{7,3},{1,5},{3,7},{12,8},{14,10},{8,... | collective-permute-start | bytes 1277960 | tf_op jit(solution)/shard_map/ppermute | solution.py:34
  288.3 139.7 %collective-permute-start.28 = (bf16[128,1664]{1,0:T(8,128)(2,1)}, bf16[128,1664]{1,0:T(8,128)(2,1)}, u32[]{:S(2)}, u32[]{:S(2)}) collective-permute-start(bf16[128,1664]{1,0:T(8,128)(2,1)} %get-tuple-element.357), channel_id=1, source_target_pairs={{6,0},{0,2},{2,4},{4,6},{7,1},{1,3},{3,5},{5,7},{14,8},{8,10},{10,... | collective-permute-start | bytes 1277960 | tf_op jit(solution)/shard_map/ppermute | solution.py:34
  356.4 95.0 %collective-permute-start.31 = (bf16[400,800]{1,0:T(8,128)(2,1)S(1)}, bf16[400,800]{1,0:T(8,128)(2,1)}, u32[]{:S(2)}, u32[]{:S(2)}) collective-permute-start(bf16[400,800]{1,0:T(8,128)(2,1)S(1)} %reshape.392.refs_1_), channel_id=1, source_target_pairs={{8,0},{16,8},{24,16},{0,24},{9,1},{17,9},{25,17},{1,25},{10,2},{18... | collective-permute-start | bytes 1920008 | tf_op jit(solution)/shard_map/ppermute | solution.py:34
  366.0 89.9 %collective-permute-start.33 = (bf16[400,800]{1,0:T(8,128)(2,1)S(1)}, bf16[400,800]{1,0:T(8,128)(2,1)}, u32[]{:S(2)}, u32[]{:S(2)}) collective-permute-start(bf16[400,800]{1,0:T(8,128)(2,1)S(1)} %reshape.392.refs_1_), channel_id=1, source_target_pairs={{24,0},{0,8},{8,16},{16,24},{25,1},{1,9},{9,17},{17,25},{26,2},{2,... | collective-permute-start | bytes 1920008 | tf_op jit(solution)/shard_map/ppermute | solution.py:34
  377.7 54.9 %all-to-all-start.7 = ((bf16[64,18,128]{2,1,0:T(8,128)(2,1)}), bf16[64,18,128]{2,1,0:T(8,128)(2,1)}, u32[]{:S(2)}, u32[]{:S(2)}) async-start(bf16[64,18,128]{2,1,0:T(8,128)(2,1)} %bitcast.112), calls=%async_computation.7 | async-start | bytes 786432 | tf_op jit(solution)/shard_map/all_to_all | solution.py:51
  426.0 62.6 %collective-permute-start.37 = (bf16[400,1600]{1,0:T(8,128)(2,1)S(1)}, bf16[400,1600]{1,0:T(8,128)(2,1)}, u32[]{:S(2)}, u32[]{:S(2)}) collective-permute-start(bf16[400,1600]{1,0:T(8,128)(2,1)S(1)} %reshape.391.refs_2_), channel_id=1, source_target_pairs={{1,0},{32,1},{33,32},{0,33},{3,2},{34,3},{35,34},{2,35},{5,4},{36,... | collective-permute-start | bytes 3840008 | tf_op jit(solution)/shard_map/ppermute | solution.py:34
  426.0 64.6 %collective-permute-start.39 = (bf16[400,1600]{1,0:T(8,128)(2,1)S(1)}, bf16[400,1600]{1,0:T(8,128)(2,1)}, u32[]{:S(2)}, u32[]{:S(2)}) collective-permute-start(bf16[400,1600]{1,0:T(8,128)(2,1)S(1)} %reshape.391.refs_2_), channel_id=1, source_target_pairs={{33,0},{0,1},{1,32},{32,33},{35,2},{2,3},{3,34},{34,35},{37,4},{4,... | collective-permute-start | bytes 3840008 | tf_op jit(solution)/shard_map/ppermute | solution.py:34
  430.8 61.0 %collective-permute-start.29 = (bf16[512,1664]{1,0:T(8,128)(2,1)}, bf16[512,1664]{1,0:T(8,128)(2,1)}, u32[]{:S(2)}, u32[]{:S(2)}) collective-permute-start(bf16[512,1664]{1,0:T(8,128)(2,1)} %pad_maximum_fusion.4), channel_id=1, source_target_pairs={{64,0},{0,64},{65,1},{1,65},{66,2},{2,66},{67,3},{3,67},{68,4},{4,... | collective-permute-start | bytes 5111816 | tf_op jit(solution)/shard_map/ppermute | solution.py:34
  447.7 492.5 %reduce-scatter.11.cloned.1.call-start = ((), (), s32[]{:S(2)}) async-start(), calls=%async_computation.22 | async-start | bytes 2635776
  453.2 47.3 %collective-permute-start.32 = (bf16[200,800]{1,0:T(8,128)(2,1)}, bf16[200,800]{1,0:T(8,128)(2,1)}, u32[]{:S(2)}, u32[]{:S(2)}) collective-permute-start(bf16[200,800]{1,0:T(8,128)(2,1)} %slice.673), channel_id=1, source_target_pairs={{8,0},{16,8},{24,16},{0,24},{9,1},{17,9},{25,17},{1,25},{10,2},{18... | collective-permute-start | bytes 960008 | tf_op jit(solution)/shard_map/ppermute | solution.py:34
  618.8 328.8 %reduce-scatter.9.cloned.1.call-start = ((), (), s32[]{:S(2)}) async-start(), calls=%async_computation.21 | async-start | bytes 4978688
  709.0 93.3 %all-to-all-start.9 = ((bf16[64,18,128]{2,1,0:T(8,128)(2,1)}), bf16[64,18,128]{2,1,0:T(8,128)(2,1)}, u32[]{:S(2)}, u32[]{:S(2)}) async-start(bf16[64,18,128]{2,1,0:T(8,128)(2,1)} %bitcast.111), calls=%async_computation.9 | async-start | bytes 786432 | tf_op jit(solution)/shard_map/all_to_all | solution.py:51
  763.4 50.4 %collective-permute-start.52 = (bf16[512,1664]{1,0:T(8,128)(2,1)}, bf16[512,1664]{1,0:T(8,128)(2,1)}, u32[]{:S(2)}, u32[]{:S(2)}) collective-permute-start(bf16[512,1664]{1,0:T(8,128)(2,1)} %slice.562), channel_id=1, source_target_pairs={{64,0},{0,64},{65,1},{1,65},{66,2},{2,66},{67,3},{3,67},{68,4},{4,... | collective-permute-start | bytes 5111816 | tf_op jit(solution)/shard_map/ppermute | solution.py:34
  810.9 155.0 %collective-permute-start.74 = (bf16[128,1120]{1,0:T(8,128)(2,1)}, bf16[128,1120]{1,0:T(8,128)(2,1)}, u32[]{:S(2)}, u32[]{:S(2)}) collective-permute-start(bf16[128,1120]{1,0:T(8,128)(2,1)} %get-tuple-element.349), channel_id=1, source_target_pairs={{64,0},{0,64},{65,1},{1,65},{66,2},{2,66},{67,3},{3,67},{68,4},{4,... | collective-permute-start | bytes 860168 | tf_op jit(solution)/shard_map/ppermute | solution.py:34
  866.0 265.8 %collective-permute-start.53 = (bf16[128,1664]{1,0:T(8,128)(2,1)}, bf16[128,1664]{1,0:T(8,128)(2,1)}, u32[]{:S(2)}, u32[]{:S(2)}) collective-permute-start(bf16[128,1664]{1,0:T(8,128)(2,1)} %get-tuple-element.298), channel_id=1, source_target_pairs={{6,0},{0,2},{2,4},{4,6},{7,1},{1,3},{3,5},{5,7},{14,8},{8,10},{10,... | collective-permute-start | bytes 1277960 | tf_op jit(solution)/shard_map/ppermute | solution.py:34
  988.8 74.0 %collective-permute-start.86 = (bf16[200,1408]{1,0:T(8,128)(2,1)}, bf16[200,1408]{1,0:T(8,128)(2,1)}, u32[]{:S(2)}, u32[]{:S(2)}) collective-permute-start(bf16[200,1408]{1,0:T(8,128)(2,1)} %get-tuple-element.160), channel_id=1, source_target_pairs={{1,0},{32,1},{33,32},{0,33},{3,2},{34,3},{35,34},{2,35},{5,4},{36,... | collective-permute-start | bytes 1689608 | tf_op jit(solution)/shard_map/ppermute | solution.py:34
  1014.3 54.3 %all-to-all-start.12 = ((bf16[128,55,128]{2,1,0:T(8,128)(2,1)}), bf16[128,55,128]{2,1,0:T(8,128)(2,1)}, u32[]{:S(2)}, u32[]{:S(2)}) async-start(bf16[128,55,128]{2,1,0:T(8,128)(2,1)} %pad_maximum_fusion.3), calls=%async_computation.12 | async-start | bytes 3670016 | tf_op jit(solution)/shard_map/all_to_all | solution.py:51
  1027.1 95.0 %collective-permute-start.81 = (bf16[400,1408]{1,0:T(8,128)(2,1)}, bf16[400,1408]{1,0:T(8,128)(2,1)}, u32[]{:S(2)}, u32[]{:S(2)}) collective-permute-start(bf16[400,1408]{1,0:T(8,128)(2,1)} %pad_maximum_fusion.12), channel_id=1, source_target_pairs={{24,0},{0,8},{8,16},{16,24},{25,1},{1,9},{9,17},{17,25},{26,2},{2,... | collective-permute-start | bytes 3379208 | tf_op jit(solution)/shard_map/ppermute | solution.py:34
  1062.8 61.2 %collective-permute-start.83 = (bf16[400,1408]{1,0:T(8,128)(2,1)}, bf16[400,1408]{1,0:T(8,128)(2,1)}, u32[]{:S(2)}, u32[]{:S(2)}) collective-permute-start(bf16[400,1408]{1,0:T(8,128)(2,1)} %pad_maximum_fusion.13), channel_id=1, source_target_pairs={{8,0},{16,8},{24,16},{0,24},{9,1},{17,9},{25,17},{1,25},{10,2},{18... | collective-permute-start | bytes 3379208 | tf_op jit(solution)/shard_map/ppermute | solution.py:34
  1092.1 56.5 %collective-permute-start.54 = (bf16[128,1664]{1,0:T(8,128)(2,1)}, bf16[128,1664]{1,0:T(8,128)(2,1)}, u32[]{:S(2)}, u32[]{:S(2)}) collective-permute-start(bf16[128,1664]{1,0:T(8,128)(2,1)} %get-tuple-element.297), channel_id=1, source_target_pairs={{4,0},{6,2},{0,4},{2,6},{5,1},{7,3},{1,5},{3,7},{12,8},{14,10},{8,... | collective-permute-start | bytes 1277960 | tf_op jit(solution)/shard_map/ppermute | solution.py:34
  1100.7 48.0 %collective-permute-start.55 = (bf16[128,1664]{1,0:T(8,128)(2,1)}, bf16[128,1664]{1,0:T(8,128)(2,1)}, u32[]{:S(2)}, u32[]{:S(2)}) collective-permute-start(bf16[128,1664]{1,0:T(8,128)(2,1)} %get-tuple-element.296), channel_id=1, source_target_pairs={{2,0},{4,2},{6,4},{0,6},{3,1},{5,3},{7,5},{1,7},{10,8},{12,10},{14... | collective-permute-start | bytes 1277960 | tf_op jit(solution)/shard_map/ppermute | solution.py:34
  (330 other events, 4020.9 us)
Sparse Core Ops, SparseCore 0:
  52.4 88.9 all-gather.6
  238.6 121.5 all-gather.4
  618.9 52.6 reduce-scatter.10
  674.0 154.0 reduce-scatter.8

commit v3 on v2

--- a/solution.py
+++ b/solution.py
@@ -413,7 +413,7 @@
     lax.fori_loop(0, count, one, jnp.zeros(rate.shape, jnp.float32))
 
 
-def chain_carry(total_step, state, decay_rate, reverse, others=()):
+def chain_carry(total_step, state, decay_rate, reverse):
     count = lax.axis_size(HEAD_BLK)
     states, channels = state.shape
     high = lax.reduce_precision(total_step, 8, 7)
@@ -428,7 +428,7 @@
         functools.partial(chain_kernel, reverse),
         out_shape=jax.ShapeDtypeStruct((count, states, 128), jnp.float32),
     )(dealt(tiles(packed), HEAD_BLK), rate)
-    got = dealt(after(to_low(chained), *others), HEAD_BLK)[: channels // 128]
+    got = dealt(to_low(chained), HEAD_BLK)[: channels // 128]
     return got.transpose(1, 0, 2).reshape(states, channels).astype(jnp.float32)
 
 
@@ -837,6 +837,10 @@
     )
 
     out_shards = (jnp.concatenate([w_mamba_out[:d_rows], w_mamba_out[d_rows:]], axis=1), w_attn_out)
+    out_planes = [
+        gathered(after(out_shards[0], planes[0]), ORDER_A[0]),
+        *gather_planes(out_shards[1:], ORDERS[1:2], (select_mine,)),
+    ]
 
     ff_rows = w_down.shape[0]
 
@@ -850,7 +854,7 @@
 
     units = 8 * FF_PAD
     gate_up = jnp.concatenate([to_units(w_gate), to_units(w_up)], axis=2)
-    gate_up_dealt = dealt(after(gate_up, select_mine), Z_RING).reshape(4 * d_rows, 2 * units)
+    gate_up_dealt = dealt(after(gate_up, out_planes[1]), Z_RING).reshape(4 * d_rows, 2 * units)
     gate_up = gathered(jnp.pad(gate_up_dealt, ((0, LANES // 16 - 4 * d_rows), (0, 0))), ("xh", "y", "xl"))
 
     here = lax.axis_index("xh") == core
@@ -860,8 +864,6 @@
     down_shard = down
     down = gathered(down, ("y", "xl"))
 
-    out_planes = gather_planes(out_shards, ORDERS[:2], (gate_up_dealt,))
-
     def group_tokens(a):
         return both_tokens(ring_whole(a, Z_RING))
 
@@ -877,7 +879,7 @@
     normed, norm_back = jax.vjp(rms_scale, tokens, norm_gain)
     normed_chip = both_tokens(to_low(normed))
     normed_a, normed_b, normed_c = turned((normed_chip,) * 3, (pick_a, pick_b, pick_c))
-    normed_c = after(normed_c, out_planes[0], down_shard)
+    normed_c = after(normed_c, gate_up_dealt, down_shard)
 
     q_cols, k_cols = w_query.shape[1], w_key.shape[1]
     projected = [
@@ -901,9 +903,12 @@
     )
     grad_out_group = group_tokens(jnp.pad(after(grad_out, conv_in), ((0, 0), (0, LANES - width))))
 
+    along_z = lax.axis_index(Z_RING)
     kv_cols = KV_HEADS * HEAD_DIM
-    window = jnp.concatenate([shifted(key_value, d) for d in range(reach_blocks, 0, -1)] + [key_value], axis=0)
-    edge_rows = after(shifted(conv_in[rows_dev - edge_count :], 1), out_planes[1])
+    row = ring_in_order(key_value, Z_RING).reshape(4, rows_dev, 2 * kv_cols)
+    edge_rows = after(shifted(conv_in[rows_dev - edge_count :], 1), row)
+    window = jnp.concatenate([shifted(row, 2, ROWS), shifted(row, 1, ROWS), row])
+    window = lax.dynamic_slice_in_dim(window, along_z, reach_blocks + 1).reshape(-1, key_value.shape[1])
 
     padded_in = jnp.concatenate([edge_rows, conv_in], axis=0).astype(jnp.float32)
     conved, conv_back = jax.vjp(conv_silu, padded_in, conv_weight, conv_bias)
@@ -916,7 +921,7 @@
     step_pre = product_nt(step_raw, step_full)
     (step_size, decay_rate), rate_back = jax.vjp(rate_piece, step_pre, step_bias, log_decay)
     total_step = jnp.sum(step_size, axis=0)
-    drive = after(step_size * conv_values, window)
+    drive = step_size * conv_values
     in_lanes, out_lanes = lanes(in_mat), lanes(out_mat)
     end_state = scan_state(step_size, drive, in_lanes, decay_rate)
     queries = after(queries, end_state)
@@ -1001,10 +1006,16 @@
         queries_by_group, window, jnp.where(allowed.T, 0.0, -1e30), score_totals, by_groups(d_heads)
     )
     d_queries = from_groups(d_queries)
-    d_key_value = d_window[reach_blocks * rows_dev :].astype(jnp.float32)
-    for d in range(1, reach_blocks + 1):
-        piece = d_window[(reach_blocks - d) * rows_dev : (reach_blocks - d + 1) * rows_dev]
-        d_key_value = d_key_value + shifted(piece, -d).astype(jnp.float32)
+    d_rows_z = jnp.zeros((12, rows_dev, d_window.shape[1]), jnp.bfloat16)
+    d_rows_z = lax.dynamic_update_slice_in_dim(
+        d_rows_z, d_window.reshape(reach_blocks + 1, rows_dev, -1), along_z, 0
+    )
+    d_row = (
+        d_rows_z[8:].astype(jnp.float32)
+        + shifted(d_rows_z[4:8], -1, ROWS).astype(jnp.float32)
+        + shifted(d_rows_z[:4], -2, ROWS).astype(jnp.float32)
+    )
+    d_key_value = ring_sum_in_order(to_low(d_row).reshape(4 * rows_dev, 2 * kv_cols), Z_RING)
     d_key_value = to_low(d_key_value).reshape(rows_dev, KV_HEADS, 2, HEAD_DIM)
     d_keys, d_values = (d_key_value[:, :, k].reshape(rows_dev, kv_cols) for k in (0, 1))
 
@@ -1026,7 +1037,7 @@
         (grad_pieces(gated_a, d_mamba_half, HALVES), grad_pieces((heads_b,), d_attn_half, HALVES)), ORDERS[:2]
     )
 
-    d_end = chain_carry(total_step, d_state_in, decay_rate, True, rings)
+    d_end = chain_carry(total_step, d_state_in, decay_rate, True)
     d_step, d_conv_scan, d_rate, d_in_mat, d_out_mat = scan_back(
         step_size, conv_values, d_scan, in_lanes, out_lanes, decay_rate, state_in, d_end
     )
@@ -1042,7 +1053,6 @@
     d_conv_in = d_padded[edge_count:] + jnp.concatenate(
         [jnp.zeros((rows_dev - edge_count, inner), jnp.float32), edge_back], axis=0
     )
-    d_conv_in = after(d_conv_in, gate_up_sum)
     d_mixed_half = own_columns(to_low(jnp.concatenate([d_conv_in, d_gate_z], axis=1)))
     d_mixed_a, d_mixed_b, d_mixed_c = (
         d_mixed_half[:, :cut_a],
@@ -1050,24 +1060,12 @@
         jnp.concatenate([d_mixed_half[:, cut_b:], d_qkv_half], axis=1),
     )
 
-    ring_a, ring_b, ring_c = sum_rings(
-        [
-            grad_pieces((left,), grad, HALVES)
-            for left, grad in ((normed_a, d_mixed_a), (normed_b, d_mixed_b), (normed_c, d_mixed_c))
-        ],
-        ORDERS,
-    )
-    sum_a, sum_b, sum_c = sum_planes(
-        [jnp.concatenate([ring_a, rings[0]], axis=1), jnp.concatenate([ring_b, rings[1]], axis=1), ring_c], ORDERS
-    )
-    sum_a, out_sum_a = sum_a[:, :cut_a], sum_a[:, cut_a:]
-    sum_b, grad_attn_out = sum_b[:, : cut_b - cut_a], sum_b[:, cut_b - cut_a :]
-    grad_mamba_out = jnp.concatenate([out_sum_a[:, :half_width], out_sum_a[:, half_width:]], axis=0)
-    grad_mamba_in = jnp.concatenate([sum_a, sum_b, sum_c[:, :mixed_c]], axis=1)
-    grad_qkv = sum_c[:, mixed_c:]
-    grad_query = grad_qkv[:, :q_cols]
-    grad_key, grad_value = grad_qkv[:, q_cols : q_cols + k_cols], grad_qkv[:, q_cols + k_cols :]
-
+    pieces = [
+        grad_pieces((left,), grad, HALVES)
+        for left, grad in ((normed_a, d_mixed_a), (normed_b, d_mixed_b), (normed_c, d_mixed_c))
+    ]
+    d_mixed_a, d_mixed_b, d_mixed_c = together((d_mixed_a, d_mixed_b, d_mixed_c, *(p[0] for p in pieces)))[:3]
+    ring_a, ring_b, ring_c = sum_rings(pieces, ORDERS)
     d_normed = turned_back(
         [
             by_pieces_nt((grad,), pieces, (window,))[0]
@@ -1100,6 +1098,7 @@
         ]
     )
     select_rows = select_rows.reshape(128, c_rows, 128)
+    select_rows = after(select_rows, gate_up_sum, grad_down)
     totals, select_sum = sum_all(jnp.concatenate([gains, *channel_rows]), select_rows)
     grad_select, grad_step = select_sum[:, :sel_half], select_sum[:, sel_half : sel_half + step_half]
     gain_sums = totals[: gains.shape[0]].reshape(4, width)
@@ -1115,6 +1114,19 @@
         channel_sums[4][0],
         *gain_sums[1:],
     ]
+    ring_a, ring_b, ring_c = together((ring_a, ring_b, ring_c, select_sum))[:3]
+    sum_a, sum_b, sum_c = sum_planes(
+        [jnp.concatenate([ring_a, rings[0]], axis=1), jnp.concatenate([ring_b, rings[1]], axis=1), ring_c], ORDERS
+    )
+    sum_a, out_sum_a = sum_a[:, :cut_a], sum_a[:, cut_a:]
+    sum_b, grad_attn_out = sum_b[:, : cut_b - cut_a], sum_b[:, cut_b - cut_a :]
+    grad_mamba_out = jnp.concatenate([out_sum_a[:, :half_width], out_sum_a[:, half_width:]], axis=0)
+    grad_mamba_in = jnp.concatenate([sum_a, sum_b, sum_c[:, :mixed_c]], axis=1)
+    grad_qkv = sum_c[:, mixed_c:]
+    grad_query = grad_qkv[:, :q_cols]
+    grad_key, grad_value = grad_qkv[:, q_cols : q_cols + k_cols], grad_qkv[:, q_cols + k_cols :]
+
+
     return (
         output,
         input_grad,

time: 1250 us -> 1160 us (0.928)
  starting transfers between devices: 312 us -> 262 us
  other arithmetic: 139 us -> 112 us
  local copies, waits for them, and re-layouts: 229 us -> 209 us
    ppermute x18 -> x6, starting transfers between devices: 52.7 us -> 18.8 us  [shifted(): lax.ppermute(a, axis, [(i - distance, i) for i in range(n) if 0 <= i - di...]
    all_to_all x17 -> x16, starting transfers between devices: 138 us -> 107 us  [dealt(): return lax.all_to_all(blocks, axis, 0, 0, tiled=True)]
    all_to_all x17 -> x16, waiting for transfers between devices: 147 us -> 173 us  [dealt(): return lax.all_to_all(blocks, axis, 0, 0, tiled=True)]
    ppermute x72 -> x78, waiting for transfers between devices: 180 us -> 155 us  [received(): return lax.ppermute(a, axis, [((i + d) % n, i) for i in range(n)])]
    unnamed x532 -> x476, local copies, waits for them, and re-layouts: 74.8 us -> 58.6 us
    ppermute x72 -> x78, starting transfers between devices: 121 us -> 136 us  [received(): return lax.ppermute(a, axis, [((i + d) % n, i) for i in range(n)])]
    convert_element_type x16 -> x17, other arithmetic: 30.5 us -> 26 us  [to_low(): return values.astype(jnp.bfloat16)]
  transfers between devices with their start and end apart: 111 -> 105, of which waited for: 41 -> 40; matrix products, arithmetic and copies ran while one was open for 26% -> 25% of each run, Pallas kernels for 14% -> 14%
where the time goes in v3:
time: 1160 us; the launch traced here: 1140 us
  waiting for transfers between devices  328 us (28%)
  starting transfers between devices  262 us (23%)
  local copies, waits for them, and re-layouts  209 us (18%)
  Pallas kernels  194 us (17%)
  other arithmetic  112 us (10%)
  between operations  18.1 us (2%)
  matrix products  16.8 us (1%)
    all_to_all x16, waiting for transfers between devices, dealt(): return lax.all_to_all(blocks, axis, 0, 0, tiled=True)  173 us
    ppermute x78, waiting for transfers between devices, received(): return lax.ppermute(a, axis, [((i + d) % n, i) for i in range(n)])  155 us
    ppermute x78, starting transfers between devices, received(): return lax.ppermute(a, axis, [((i + d) % n, i) for i in range(n)])  136 us
    all_to_all x16, starting transfers between devices, dealt(): return lax.all_to_all(blocks, axis, 0, 0, tiled=True)  107 us
    pallas_call x23, Pallas kernels, whole_call(): pl.pallas_call(kernel, out_shape=outs, in_specs=[pl.BlockSpec(memory_spac...  87.1 us
    unnamed x476, local copies, waits for them, and re-layouts  58.6 us
    pallas_call x4, Pallas kernels, scan_call(): pl.pallas_call(kernel, grid=(channels // SCAN_TILE,), in_specs=[kinds[k]...  48.6 us
    pallas_call x2, Pallas kernels, attend_call(): pl.pallas_call(kernel, grid=(KV_HEADS,), in_specs=[specs[k if k in specs...  29.6 us
  transfers between devices with their start and end apart: 105, of which 40 were waited for; matrix products, arithmetic and copies ran while one was open for 25% of the time, Pallas kernels for 14%

profile of v3, /device:TPU:0, one launch (start us, length us, event | category | flops | bytes accessed | tf_op | source)
XLA Modules:
  0.0 1141.5 jit_solution(5655068583211900734)
XLA Ops:
  9.4 8.3 all-to-all-start
  19.0 21.0 %all-to-all-done = bf16[16,25,1408]{2,1,0:T(8,128)(2,1)} async-done(((bf16[16,25,1408]{2,1,0:T(8,128)(2,1)}), bf16[16,25,1408]{2,1,0:T(8,128)(2,1)}, u32[]{:S(2)}, u32[]{:S(2)}) %all-to-all-start) | async-done | bytes 1126432 | tf_op jit(solution)/shard_map/all_to_all | solution.py:51
  54.7 19.3 %all-to-all-done.1 = bf16[16,25,1408]{2,1,0:T(8,128)(2,1)} async-done(((bf16[16,25,1408]{2,1,0:T(8,128)(2,1)}), bf16[16,25,1408]{2,1,0:T(8,128)(2,1)}, u32[]{:S(2)}, u32[]{:S(2)}) %all-to-all-start.1) | async-done | bytes 1126432 | tf_op jit(solution)/shard_map/all_to_all | solution.py:51
  89.5 20.3 %all-to-all-done.2 = bf16[16,25,1504]{2,1,0:T(8,128)(2,1)} async-done(((bf16[16,25,1504]{2,1,0:T(8,128)(2,1)}), bf16[16,25,1504]{2,1,0:T(8,128)(2,1)}, u32[]{:S(2)}, u32[]{:S(2)}) %all-to-all-start.2) | async-done | bytes 1203232 | tf_op jit(solution)/shard_map/all_to_all | solution.py:51
  134.7 8.1 all-to-all-start.3
  164.1 22.7 %collective-permute-done.10.refs_4_ = bf16[200,1408]{1,0:T(8,128)(2,1)S(1)} collective-permute-done((bf16[200,1408]{1,0:T(8,128)(2,1)S(1)}, bf16[200,1408]{1,0:T(8,128)(2,1)S(1)}, u32[]{:S(2)}, u32[]{:S(2)}) %collective-permute-start.10) | collective-permute-done | bytes 563232 | tf_op jit(solution)/shard_map/ppermute | solution.py:34
  271.5 8.2 collective-permute-done.17
  314.1 9.9 all-to-all-start.6
  365.3 25.8 %all-to-all-done.7 = bf16[64,16,128]{2,1,0:T(8,128)(2,1)} async-done(((bf16[64,16,128]{2,1,0:T(8,128)(2,1)}), bf16[64,16,128]{2,1,0:T(8,128)(2,1)}, u32[]{:S(2)}, u32[]{:S(2)}) %all-to-all-start.7) | async-done | bytes 262176 | tf_op jit(solution)/shard_map/all_to_all | solution.py:51
  397.4 10.7 shard_map.595
  415.5 13.6 %shard_map.593 = (bf16[5,128,320]{2,1,0:T(8,128)(2,1)S(1)}, f32[5,128,8]{2,1,0:T(8,128)S(1)}) custom-call(bf16[5,128,320]{2,1,0:T(8,128)(2,1)S(1)} %bitcast.116, bf16[1152,640]{1,0:T(8,128)(2,1)S(1)} %bitcast.113, f32[128,1152]{1,0:T(8,128)S(1)} %copy-done.72), custom_call_target="tpu_custom_call" | custom-call | flops 943718400 | bytes 589824 | tf_op jit(solution)/shard_map/pallas_call | solution.py:731
  435.8 17.5 %collective-permute-start.35 = (bf16[200,1600]{1,0:T(8,128)(2,1)S(1)}, bf16[200,1600]{1,0:T(8,128)(2,1)S(1)}, u32[]{:S(2)}, u32[]{:S(2)}) collective-permute-start(bf16[200,1600]{1,0:T(8,128)(2,1)S(1)} %slice.652), channel_id=1, source_target_pairs={{1,0},{32,1},{33,32},{0,33},{3,2},{34,3},{35,34},{2,35},{5,4},{36,... | collective-permute-start | bytes 1920008 | tf_op jit(solution)/shard_map/ppermute | solution.py:34
  468.2 13.2 %collective-permute-done.37.refs_5_ = bf16[200,1600]{1,0:T(8,128)(2,1)S(1)} collective-permute-done((bf16[200,1600]{1,0:T(8,128)(2,1)S(1)}, bf16[200,1600]{1,0:T(8,128)(2,1)S(1)}, u32[]{:S(2)}, u32[]{:S(2)}) %collective-permute-start.37) | collective-permute-done | bytes 640032 | tf_op jit(solution)/shard_map/ppermute | solution.py:34
  506.2 10.1 collective-permute-done.39
  518.7 8.0 collective-permute-done.41
  533.6 23.7 %shard_map.600 = (bf16[1024,704]{1,0:T(8,128)(2,1)S(1)}, bf16[1024,1408]{1,0:T(8,128)(2,1)}, bf16[1024,1664]{1,0:T(8,128)(2,1)}, bf16[1024,1664]{1,0:T(8,128)(2,1)}) custom-call(bf16[1024,1664]{1,0:T(8,128)(2,1)} %constant_dynamic-update-slice_fusion.11.x_ref, bf16[1024,1664]{1,0:T(8,128)(2,1)} %constant_dynamic-update-slice_fusion.g_ref, ...), custom_call_target="tpu_custom_call" | custom-call | flops 14394851328 | bytes 17956864 | tf_op jit(solution)/shard_map/pallas_call | solution.py:301
  565.8 10.1 shard_map.617
  583.5 17.8 %collective-permute-done.44 = bf16[128,1664]{1,0:T(8,128)(2,1)S(1)} collective-permute-done((bf16[128,1664]{1,0:T(8,128)(2,1)S(1)}, bf16[128,1664]{1,0:T(8,128)(2,1)S(1)}, u32[]{:S(2)}, u32[]{:S(2)}) %collective-permute-start.44) | collective-permute-done | bytes 426016 | tf_op jit(solution)/shard_map/ppermute | solution.py:34
  656.8 15.9 %shard_map.609 = (bf16[5,128,320]{2,1,0:T(8,128)(2,1)S(1)}, bf16[1152,640]{1,0:T(8,128)(2,1)S(1)}) custom-call(bf16[5,128,320]{2,1,0:T(8,128)(2,1)S(1)} %bitcast.117, bf16[1152,640]{1,0:T(8,128)(2,1)S(1)} %bitcast.114, f32[1152,128]{1,0:T(8,128)S(1)} %copy-done.73, f32[5,8,128]{2,1,0:T(8,128)S(1)} %bitcast.121, bf16[5,128,320]{2,1,0:T(8,128)(2,1)S(1)} %bitcast.119), custom_call_target="tpu_custom_call" | custom-call | flops 2359296000 | bytes 589824 | tf_op jit(solution)/shard_map/pallas_call | solution.py:731
  715.6 7.7 all-to-all-start.9
  743.9 26.5 %shard_map.608 = (f32[128,3200]{1,0:T(8,128)S(1)}, f32[128,3200]{1,0:T(8,128)S(1)}, f32[16,3200]{1,0:T(8,128)S(1)}, f32[128,16,128]{2,1,0:T(8,128)S(1)}, f32[128,16,128]{2,1,0:T(8,128)S(1)}) custom-call(f32[128,3200]{1,0:T(8,128)S(1)} %copy-done.31, f32[128,3200]{1,0:T(8,128)S(1)} %copy-done.37, f32[128,3200]{1,0:T(8,128)S(1)} %copy-done.33, ...), custom_call_target="tpu_custom_call" | custom-call | flops 157286400 | bytes 6553600 | tf_op jit(solution)/shard_map/pallas_call | solution.py:645
  841.7 10.5 collective-permute-start.64
  852.3 10.7 collective-permute-start.66
  883.5 13.4 %collective-permute-done.69 = bf16[400,1408]{1,0:T(8,128)(2,1)S(1)} collective-permute-done((bf16[400,1408]{1,0:T(8,128)(2,1)S(1)}, bf16[400,1408]{1,0:T(8,128)(2,1)S(1)}, u32[]{:S(2)}, u32[]{:S(2)}) %collective-permute-start.69) | collective-permute-done | bytes 1126432 | tf_op jit(solution)/shard_map/ppermute | solution.py:34
  909.0 16.3 %collective-permute-done.73 = bf16[400,1504]{1,0:T(8,128)(2,1)S(1)} collective-permute-done((bf16[400,1504]{1,0:T(8,128)(2,1)S(1)}, bf16[400,1504]{1,0:T(8,128)(2,1)S(1)}, u32[]{:S(2)}, u32[]{:S(2)}) %collective-permute-start.73) | collective-permute-done | bytes 1203232 | tf_op jit(solution)/shard_map/ppermute | solution.py:34
  962.9 8.8 all-to-all-done.13
  994.1 17.0 %all-to-all-done.14 = bf16[16,25,2208]{2,1,0:T(8,128)(2,1)} async-done(((bf16[16,25,2208]{2,1,0:T(8,128)(2,1)}), bf16[16,25,2208]{2,1,0:T(8,128)(2,1)}, u32[]{:S(2)}, u32[]{:S(2)}) %all-to-all-start.14) | async-done | bytes 1766432 | tf_op jit(solution)/shard_map/all_to_all | solution.py:51
  1028.7 7.6 all-to-all-start.15
  1055.8 18.2 %all-to-all-done.15 = bf16[16,25,3008]{2,1,0:T(8,128)(2,1)} async-done(((bf16[16,25,3008]{2,1,0:T(8,128)(2,1)}), bf16[16,25,3008]{2,1,0:T(8,128)(2,1)}, u32[]{:S(2)}, u32[]{:S(2)}) %all-to-all-start.15) | async-done | bytes 2406432 | tf_op jit(solution)/shard_map/all_to_all | solution.py:51
  1074.0 9.9 all-to-all-start.11
  1096.9 14.2 %all-to-all-done.11 = bf16[128,55,128]{2,1,0:T(8,128)(2,1)S(1)} async-done(((bf16[128,55,128]{2,1,0:T(8,128)(2,1)}), bf16[128,55,128]{2,1,0:T(8,128)(2,1)S(1)}, u32[]{:S(2)}, u32[]{:S(2)}) %all-to-all-start.11) | async-done | bytes 1802272 | tf_op jit(solution)/shard_map/all_to_all | solution.py:51
  1122.1 8.5 all-to-all-done.12
  (1005 shorter events, 669.8 us)
Async XLA Ops:
  17.7 195.2 %all-gather.12.cloned.1.call-start = ((), (), s32[]{:S(2)}) async-start(), calls=%async_computation.20 | async-start | bytes 1810432 | tf_op jit(solution)/shard_map/all_gather | solution.py:168
  51.2 480.8 %all-gather.10.cloned.1.call-start = ((), (), s32[]{:S(2)}) async-start(), calls=%async_computation.19 | async-start | bytes 2635776 | tf_op jit(solution)/shard_map/all_gather | solution.py:168
  53.0 61.4 %collective-permute-start.9 = (bf16[400,1408]{1,0:T(8,128)(2,1)S(1)}, bf16[400,1408]{1,0:T(8,128)(2,1)}, u32[]{:S(2)}, u32[]{:S(2)}) collective-permute-start(bf16[400,1408]{1,0:T(8,128)(2,1)S(1)} %reshape.395.refs_1_), channel_id=1, source_target_pairs={{33,0},{0,1},{1,32},{32,33},{35,2},{2,3},{3,34},{34,35},{37,4},{4,... | collective-permute-start | bytes 3379208 | tf_op jit(solution)/shard_map/ppermute | solution.py:34
  85.6 62.5 %collective-permute-start.11 = (bf16[400,1408]{1,0:T(8,128)(2,1)}, bf16[400,1408]{1,0:T(8,128)(2,1)}, u32[]{:S(2)}, u32[]{:S(2)}) collective-permute-start(bf16[400,1408]{1,0:T(8,128)(2,1)} %reshape.396.refs_1_), channel_id=1, source_target_pairs={{8,0},{16,8},{24,16},{0,24},{9,1},{17,9},{25,17},{1,25},{10,2},{18... | collective-permute-start | bytes 3379208 | tf_op jit(solution)/shard_map/ppermute | solution.py:34
  89.5 70.0 %collective-permute-start.13 = (bf16[400,1408]{1,0:T(8,128)(2,1)}, bf16[400,1408]{1,0:T(8,128)(2,1)}, u32[]{:S(2)}, u32[]{:S(2)}) collective-permute-start(bf16[400,1408]{1,0:T(8,128)(2,1)} %reshape.396.refs_1_), channel_id=1, source_target_pairs={{24,0},{0,8},{8,16},{16,24},{25,1},{1,9},{9,17},{17,25},{26,2},{2,... | collective-permute-start | bytes 3379208 | tf_op jit(solution)/shard_map/ppermute | solution.py:34
  111.6 93.4 %collective-permute-start.3 = (bf16[400,1504]{1,0:T(8,128)(2,1)S(1)}, bf16[400,1504]{1,0:T(8,128)(2,1)}, u32[]{:S(2)}, u32[]{:S(2)}) collective-permute-start(bf16[400,1504]{1,0:T(8,128)(2,1)S(1)} %reshape.397.refs_1_), channel_id=1, source_target_pairs={{2,0},{4,2},{6,4},{0,6},{3,1},{5,3},{7,5},{1,7},{10,8},{12,10},{14... | collective-permute-start | bytes 3609608 | tf_op jit(solution)/shard_map/ppermute | solution.py:34
  114.4 95.6 %collective-permute-start.5 = (bf16[400,1504]{1,0:T(8,128)(2,1)S(1)}, bf16[400,1504]{1,0:T(8,128)(2,1)}, u32[]{:S(2)}, u32[]{:S(2)}) collective-permute-start(bf16[400,1504]{1,0:T(8,128)(2,1)S(1)} %reshape.397.refs_1_), channel_id=1, source_target_pairs={{6,0},{0,2},{2,4},{4,6},{7,1},{1,3},{3,5},{5,7},{14,8},{8,10},{10,... | collective-permute-start | bytes 3609608 | tf_op jit(solution)/shard_map/ppermute | solution.py:34
  134.7 59.5 %all-to-all-start.3 = ((bf16[64,50,128]{2,1,0:T(8,128)(2,1)}), bf16[64,50,128]{2,1,0:T(8,128)(2,1)}, u32[]{:S(2)}, u32[]{:S(2)}) async-start(bf16[64,50,128]{2,1,0:T(8,128)(2,1)} %broadcast_in_dim.64), calls=%async_computation.3 | async-start | bytes 1835008 | tf_op jit(solution)/shard_map/all_to_all | solution.py:51
  159.5 55.3 %collective-permute-start.12 = (bf16[200,1408]{1,0:T(8,128)(2,1)}, bf16[200,1408]{1,0:T(8,128)(2,1)}, u32[]{:S(2)}, u32[]{:S(2)}) collective-permute-start(bf16[200,1408]{1,0:T(8,128)(2,1)} %slice.623), channel_id=1, source_target_pairs={{8,0},{16,8},{24,16},{0,24},{9,1},{17,9},{25,17},{1,25},{10,2},{18... | collective-permute-start | bytes 1689608 | tf_op jit(solution)/shard_map/ppermute | solution.py:34
  227.7 304.3 %all-gather.8.cloned.1.call-start = ((), (), s32[]{:S(2)}) async-start(), calls=%async_computation.18 | async-start | bytes 4978688 | tf_op jit(solution)/shard_map/all_gather | solution.py:168
  254.0 74.7 %collective-permute-start.23 = (bf16[128,1664]{1,0:T(8,128)(2,1)}, bf16[128,1664]{1,0:T(8,128)(2,1)}, u32[]{:S(2)}, u32[]{:S(2)}) collective-permute-start(bf16[128,1664]{1,0:T(8,128)(2,1)} %get-tuple-element.362), channel_id=1, source_target_pairs={{2,0},{4,2},{6,4},{0,6},{3,1},{5,3},{7,5},{1,7},{10,8},{12,10},{14... | collective-permute-start | bytes 1277960 | tf_op jit(solution)/shard_map/ppermute | solution.py:34
  255.5 78.0 %collective-permute-start.24 = (bf16[128,1664]{1,0:T(8,128)(2,1)}, bf16[128,1664]{1,0:T(8,128)(2,1)}, u32[]{:S(2)}, u32[]{:S(2)}) collective-permute-start(bf16[128,1664]{1,0:T(8,128)(2,1)} %get-tuple-element.362), channel_id=1, source_target_pairs={{4,0},{6,2},{0,4},{2,6},{5,1},{7,3},{1,5},{3,7},{12,8},{14,10},{8,... | collective-permute-start | bytes 1277960 | tf_op jit(solution)/shard_map/ppermute | solution.py:34
  279.7 55.7 %collective-permute-start.25 = (bf16[128,1664]{1,0:T(8,128)(2,1)}, bf16[128,1664]{1,0:T(8,128)(2,1)}, u32[]{:S(2)}, u32[]{:S(2)}) collective-permute-start(bf16[128,1664]{1,0:T(8,128)(2,1)} %get-tuple-element.362), channel_id=1, source_target_pairs={{6,0},{0,2},{2,4},{4,6},{7,1},{1,3},{3,5},{5,7},{14,8},{8,10},{10,... | collective-permute-start | bytes 1277960 | tf_op jit(solution)/shard_map/ppermute | solution.py:34
  287.5 70.1 %collective-permute-start.28 = (bf16[400,800]{1,0:T(8,128)(2,1)S(1)}, bf16[400,800]{1,0:T(8,128)(2,1)}, u32[]{:S(2)}, u32[]{:S(2)}) collective-permute-start(bf16[400,800]{1,0:T(8,128)(2,1)S(1)} %reshape.399.refs_1_), channel_id=1, source_target_pairs={{8,0},{16,8},{24,16},{0,24},{9,1},{17,9},{25,17},{1,25},{10,2},{18... | collective-permute-start | bytes 1920008 | tf_op jit(solution)/shard_map/ppermute | solution.py:34
  293.8 69.7 %collective-permute-start.30 = (bf16[400,800]{1,0:T(8,128)(2,1)S(1)}, bf16[400,800]{1,0:T(8,128)(2,1)}, u32[]{:S(2)}, u32[]{:S(2)}) collective-permute-start(bf16[400,800]{1,0:T(8,128)(2,1)S(1)} %reshape.399.refs_1_), channel_id=1, source_target_pairs={{24,0},{0,8},{8,16},{16,24},{25,1},{1,9},{9,17},{17,25},{26,2},{2,... | collective-permute-start | bytes 1920008 | tf_op jit(solution)/shard_map/ppermute | solution.py:34
  328.7 106.0 %collective-permute-start.34 = (bf16[400,1600]{1,0:T(8,128)(2,1)S(1)}, bf16[400,1600]{1,0:T(8,128)(2,1)}, u32[]{:S(2)}, u32[]{:S(2)}) collective-permute-start(bf16[400,1600]{1,0:T(8,128)(2,1)S(1)} %reshape.452.refs_2_), channel_id=1, source_target_pairs={{1,0},{32,1},{33,32},{0,33},{3,2},{34,3},{35,34},{2,35},{5,4},{36,... | collective-permute-start | bytes 3840008 | tf_op jit(solution)/shard_map/ppermute | solution.py:34
  333.5 119.8 %collective-permute-start.36 = (bf16[400,1600]{1,0:T(8,128)(2,1)S(1)}, bf16[400,1600]{1,0:T(8,128)(2,1)}, u32[]{:S(2)}, u32[]{:S(2)}) collective-permute-start(bf16[400,1600]{1,0:T(8,128)(2,1)S(1)} %reshape.452.refs_2_), channel_id=1, source_target_pairs={{33,0},{0,1},{1,32},{32,33},{35,2},{2,3},{3,34},{34,35},{37,4},{4,... | collective-permute-start | bytes 3840008 | tf_op jit(solution)/shard_map/ppermute | solution.py:34
  335.3 75.8 %collective-permute-start.21 = (bf16[4,128,640]{2,1,0:T(8,128)(2,1)}, bf16[4,128,640]{2,1,0:T(8,128)(2,1)}, u32[]{:S(2)}, u32[]{:S(2)}) collective-permute-start(bf16[4,128,640]{2,1,0:T(8,128)(2,1)} %constant_dynamic-update-slice_fusion.17), channel_id=1, source_target_pairs={{0,16},{8,24},{16,32},{24,40},{32,48},{40,56},{48,64},{56,72},{64,... | collective-permute-start | bytes 1966088 | tf_op jit(solution)/shard_map/ppermute | solution.py:43
  354.8 637.6 %reduce-scatter.9.cloned.1.call-start = ((), (), s32[]{:S(2)}) async-start(), calls=%async_computation.21 | async-start | bytes 4978688
  357.6 55.7 %collective-permute-start.22 = (bf16[4,128,640]{2,1,0:T(8,128)(2,1)}, bf16[4,128,640]{2,1,0:T(8,128)(2,1)}, u32[]{:S(2)}, u32[]{:S(2)}) collective-permute-start(bf16[4,128,640]{2,1,0:T(8,128)(2,1)} %constant_dynamic-update-slice_fusion.17), channel_id=1, source_target_pairs={{0,8},{8,16},{16,24},{24,32},{32,40},{40,48},{48,56},{56,64},{64,7... | collective-permute-start | bytes 1966088 | tf_op jit(solution)/shard_map/ppermute | solution.py:43
  363.5 91.0 %collective-permute-start.26 = (bf16[512,1664]{1,0:T(8,128)(2,1)}, bf16[512,1664]{1,0:T(8,128)(2,1)}, u32[]{:S(2)}, u32[]{:S(2)}) collective-permute-start(bf16[512,1664]{1,0:T(8,128)(2,1)} %pad_maximum_fusion.5), channel_id=1, source_target_pairs={{64,0},{0,64},{65,1},{1,65},{66,2},{2,66},{67,3},{3,67},{68,4},{4,... | collective-permute-start | bytes 5111816 | tf_op jit(solution)/shard_map/ppermute | solution.py:34
  577.3 460.3 %reduce-scatter.11.cloned.1.call-start = ((), (), s32[]{:S(2)}) async-start(), calls=%async_computation.22 | async-start | bytes 2635776
  650.5 153.7 %collective-permute-start.80 = (bf16[200,1600]{1,0:T(8,128)(2,1)}, bf16[200,1600]{1,0:T(8,128)(2,1)}, u32[]{:S(2)}, u32[]{:S(2)}) collective-permute-start(bf16[200,1600]{1,0:T(8,128)(2,1)} %get-tuple-element.167), channel_id=1, source_target_pairs={{33,0},{0,1},{1,32},{32,33},{35,2},{2,3},{3,34},{34,35},{37,4},{4,... | collective-permute-start | bytes 1920008 | tf_op jit(solution)/shard_map/ppermute | solution.py:34
  691.7 114.4 %collective-permute-start.82 = (bf16[200,1600]{1,0:T(8,128)(2,1)}, bf16[200,1600]{1,0:T(8,128)(2,1)}, u32[]{:S(2)}, u32[]{:S(2)}) collective-permute-start(bf16[200,1600]{1,0:T(8,128)(2,1)} %get-tuple-element.169), channel_id=1, source_target_pairs={{1,0},{32,1},{33,32},{0,33},{3,2},{34,3},{35,34},{2,35},{5,4},{36,... | collective-permute-start | bytes 1920008 | tf_op jit(solution)/shard_map/ppermute | solution.py:34
  697.8 109.6 %collective-permute-start.55 = (bf16[4,128,640]{1,2,0:T(8,128)(2,1)}, bf16[4,128,640]{1,2,0:T(8,128)(2,1)}, u32[]{:S(2)}, u32[]{:S(2)}) collective-permute-start(bf16[4,128,640]{1,2,0:T(8,128)(2,1)} %get-tuple-element.297), channel_id=1, source_target_pairs={{8,0},{16,8},{24,16},{32,24},{40,32},{48,40},{56,48},{64,56},{72,6... | collective-permute-start | bytes 1966088 | tf_op jit(solution)/shard_map/ppermute | solution.py:43
  723.4 84.0 %collective-permute-start.56 = (bf16[4,128,640]{1,2,0:T(8,128)(2,1)}, bf16[4,128,640]{1,2,0:T(8,128)(2,1)}, u32[]{:S(2)}, u32[]{:S(2)}) collective-permute-start(bf16[4,128,640]{1,2,0:T(8,128)(2,1)} %get-tuple-element.298), channel_id=1, source_target_pairs={{16,0},{24,8},{32,16},{40,24},{48,32},{56,40},{64,48},{72,56},{80,... | collective-permute-start | bytes 1966088 | tf_op jit(solution)/shard_map/ppermute | solution.py:43
  796.0 182.8 %collective-permute-start.49 = (bf16[512,1664]{1,0:T(8,128)(2,1)}, bf16[512,1664]{1,0:T(8,128)(2,1)}, u32[]{:S(2)}, u32[]{:S(2)}) collective-permute-start(bf16[512,1664]{1,0:T(8,128)(2,1)} %slice.544), channel_id=1, source_target_pairs={{64,0},{0,64},{65,1},{1,65},{66,2},{2,66},{67,3},{3,67},{68,4},{4,... | collective-permute-start | bytes 5111816 | tf_op jit(solution)/shard_map/ppermute | solution.py:34
  925.3 63.7 %collective-permute-start.81 = (bf16[400,1600]{1,0:T(8,128)(2,1)}, bf16[400,1600]{1,0:T(8,128)(2,1)}, u32[]{:S(2)}, u32[]{:S(2)}) collective-permute-start(bf16[400,1600]{1,0:T(8,128)(2,1)} %pad_maximum_fusion.8), channel_id=1, source_target_pairs={{33,0},{0,1},{1,32},{32,33},{35,2},{2,3},{3,34},{34,35},{37,4},{4,... | collective-permute-start | bytes 3840008 | tf_op jit(solution)/shard_map/ppermute | solution.py:34
  925.4 63.6 %collective-permute-start.83 = (bf16[400,1600]{1,0:T(8,128)(2,1)}, bf16[400,1600]{1,0:T(8,128)(2,1)}, u32[]{:S(2)}, u32[]{:S(2)}) collective-permute-start(bf16[400,1600]{1,0:T(8,128)(2,1)} %pad_maximum_fusion.9), channel_id=1, source_target_pairs={{1,0},{32,1},{33,32},{0,33},{3,2},{34,3},{35,34},{2,35},{5,4},{36,... | collective-permute-start | bytes 3840008 | tf_op jit(solution)/shard_map/ppermute | solution.py:34
  982.4 66.4 %collective-permute-start.50 = (bf16[128,1664]{1,0:T(8,128)(2,1)}, bf16[128,1664]{1,0:T(8,128)(2,1)}, u32[]{:S(2)}, u32[]{:S(2)}) collective-permute-start(bf16[128,1664]{1,0:T(8,128)(2,1)} %get-tuple-element.308), channel_id=1, source_target_pairs={{6,0},{0,2},{2,4},{4,6},{7,1},{1,3},{3,5},{5,7},{14,8},{8,10},{10,... | collective-permute-start | bytes 1277960 | tf_op jit(solution)/shard_map/ppermute | solution.py:34
  984.3 64.6 %collective-permute-start.51 = (bf16[128,1664]{1,0:T(8,128)(2,1)}, bf16[128,1664]{1,0:T(8,128)(2,1)}, u32[]{:S(2)}, u32[]{:S(2)}) collective-permute-start(bf16[128,1664]{1,0:T(8,128)(2,1)} %get-tuple-element.307), channel_id=1, source_target_pairs={{4,0},{6,2},{0,4},{2,6},{5,1},{7,3},{1,5},{3,7},{12,8},{14,10},{8,... | collective-permute-start | bytes 1277960 | tf_op jit(solution)/shard_map/ppermute | solution.py:34
  987.0 61.9 %collective-permute-start.52 = (bf16[128,1664]{1,0:T(8,128)(2,1)}, bf16[128,1664]{1,0:T(8,128)(2,1)}, u32[]{:S(2)}, u32[]{:S(2)}) collective-permute-start(bf16[128,1664]{1,0:T(8,128)(2,1)} %get-tuple-element.306), channel_id=1, source_target_pairs={{2,0},{4,2},{6,4},{0,6},{3,1},{5,3},{7,5},{1,7},{10,8},{12,10},{14... | collective-permute-start | bytes 1277960 | tf_op jit(solution)/shard_map/ppermute | solution.py:34
  (300 other events, 3864.4 us)
Sparse Core Ops, SparseCore 0:
  41.7 68.5 all-gather.11
  112.0 80.9 all-gather.9
  239.7 120.9 all-gather.7
  577.5 119.3 reduce-scatter.8
  699.3 74.0 reduce-scatter.10

commit v4 on v3

--- a/solution.py
+++ b/solution.py
@@ -432,14 +432,22 @@
     return got.transpose(1, 0, 2).reshape(states, channels).astype(jnp.float32)
 
 
-def sum_all(values, owned):
+def sum_parts(values, owned):
     count = lax.axis_size(EVERY)
     lines = values.reshape(-1, 128)
     each = -(-lines.shape[0] // count)
     padded = jnp.pad(lines, ((0, count * each - lines.shape[0]), (0, 0))).reshape(count, each, 128)
     mine = summed(jnp.concatenate([to_low(owned), to_low(padded)], axis=1), EVERY)
-    all_lines = shown(mine[owned.shape[1] :], EVERY).reshape(-1, 128)
-    return all_lines[: lines.shape[0]].reshape(values.shape), mine[: owned.shape[1]]
+    return mine[owned.shape[1] :], mine[: owned.shape[1]]
+
+
+def show_parts(mine, shape, local):
+    rows = -(-local.shape[0] // 128)
+    lines = jnp.pad(local, (0, rows * 128 - local.shape[0])).reshape(rows, 128)
+    got = shown(jnp.concatenate([mine, lines], axis=0), EVERY)
+    each = mine.shape[0]
+    totals = got[:, :each].reshape(-1, 128)[: shape[0] * shape[1] // 128].reshape(shape)
+    return totals, jnp.sum(got[:, each:], axis=0).reshape(-1)[: local.shape[0]]
 
 
 def rms_scale(values, gain):
@@ -1090,7 +1098,7 @@
         grad_ffn_norm,
     )
     channel_rows = [a.reshape(-1, inner) for a in smalls[1:6]]
-    gains = jnp.concatenate([smalls[0], *smalls[6:]]).reshape(-1, inner)
+    gains = jnp.concatenate([*smalls[6:], jnp.zeros((width,), jnp.float32)]).reshape(-1, inner)
     select_rows = jnp.stack(
         [
             jnp.pad(jnp.concatenate([sel, stp], axis=1), ((0, 0), (0, 128 - sel_half - step_half)))
@@ -1098,23 +1106,24 @@
         ]
     )
     select_rows = select_rows.reshape(128, c_rows, 128)
-    select_rows = after(select_rows, gate_up_sum, grad_down)
-    totals, select_sum = sum_all(jnp.concatenate([gains, *channel_rows]), select_rows)
-    grad_select, grad_step = select_sum[:, :sel_half], select_sum[:, sel_half : sel_half + step_half]
+    small_rows = jnp.concatenate([gains, *channel_rows])
+    small_part, select_sum = sum_parts(small_rows, select_rows)
+    totals, norm_sum = show_parts(small_part, small_rows.shape, grad_norm)
     gain_sums = totals[: gains.shape[0]].reshape(4, width)
     at, channel_sums = gains.shape[0], []
     for a in channel_rows:
         channel_sums.append(totals[at : at + a.shape[0]])
         at += a.shape[0]
     totals = [
-        gain_sums[0],
+        norm_sum,
         channel_sums[0],
         *(channel_sums[k][0] for k in (1, 2)),
         channel_sums[3],
         channel_sums[4][0],
-        *gain_sums[1:],
+        *gain_sums[:3],
     ]
-    ring_a, ring_b, ring_c = together((ring_a, ring_b, ring_c, select_sum))[:3]
+    ring_a, ring_b, ring_c, select_sum = together((ring_a, ring_b, ring_c, select_sum))
+    grad_select, grad_step = select_sum[:, :sel_half], select_sum[:, sel_half : sel_half + step_half]
     sum_a, sum_b, sum_c = sum_planes(
         [jnp.concatenate([ring_a, rings[0]], axis=1), jnp.concatenate([ring_b, rings[1]], axis=1), ring_c], ORDERS
     )

time: 1160 us -> 1180 us (1.017)
  waiting for transfers between devices: 328 us -> 302 us
  local copies, waits for them, and re-layouts: 209 us -> 232 us
  starting transfers between devices: 262 us -> 274 us
    all_to_all x16, starting transfers between devices: 107 us -> 137 us  [dealt(): return lax.all_to_all(blocks, axis, 0, 0, tiled=True)]
    all_to_all x16, waiting for transfers between devices: 173 us -> 154 us  [dealt(): return lax.all_to_all(blocks, axis, 0, 0, tiled=True)]
    ppermute x78, starting transfers between devices: 136 us -> 118 us  [received(): return lax.ppermute(a, axis, [((i + d) % n, i) for i in range(n)])]
    unnamed x476 -> x494, local copies, waits for them, and re-layouts: 58.6 us -> 69.5 us
  transfers between devices with their start and end apart: 105 -> 105, of which waited for: 40 -> 36; matrix products, arithmetic and copies ran while one was open for 25% -> 27% of each run, Pallas kernels for 14% -> 15%
where the time goes in v4:
time: 1180 us; the launch traced here: 1160 us
  waiting for transfers between devices  302 us (26%)
  starting transfers between devices  274 us (23%)
  local copies, waits for them, and re-layouts  232 us (20%)
  Pallas kernels  195 us (17%)
  other arithmetic  122 us (10%)
  between operations  18.1 us (2%)
  matrix products  17.4 us (1%)
    all_to_all x16, waiting for transfers between devices, dealt(): return lax.all_to_all(blocks, axis, 0, 0, tiled=True)  154 us
    ppermute x78, waiting for transfers between devices, received(): return lax.ppermute(a, axis, [((i + d) % n, i) for i in range(n)])  148 us
    all_to_all x16, starting transfers between devices, dealt(): return lax.all_to_all(blocks, axis, 0, 0, tiled=True)  137 us
    ppermute x78, starting transfers between devices, received(): return lax.ppermute(a, axis, [((i + d) % n, i) for i in range(n)])  118 us
    pallas_call x23, Pallas kernels, whole_call(): pl.pallas_call(kernel, out_shape=outs, in_specs=[pl.BlockSpec(memory_spac...  87.2 us
    unnamed x494, local copies, waits for them, and re-layouts  69.5 us
    pallas_call x4, Pallas kernels, scan_call(): pl.pallas_call(kernel, grid=(channels // SCAN_TILE,), in_specs=[kinds[k]...  48.6 us
    pallas_call x2, Pallas kernels, attend_call(): pl.pallas_call(kernel, grid=(KV_HEADS,), in_specs=[specs[k if k in specs...  29.6 us
  transfers between devices with their start and end apart: 105, of which 36 were waited for; matrix products, arithmetic and copies ran while one was open for 27% of the time, Pallas kernels for 15%

profile of v4, /device:TPU:0, one launch (start us, length us, event | category | flops | bytes accessed | tf_op | source)
XLA Modules:
  0.0 1160.1 jit_solution(1574625950793775894)
XLA Ops:
  9.4 8.3 all-to-all-start
  19.0 21.0 %all-to-all-done = bf16[16,25,1408]{2,1,0:T(8,128)(2,1)} async-done(((bf16[16,25,1408]{2,1,0:T(8,128)(2,1)}), bf16[16,25,1408]{2,1,0:T(8,128)(2,1)}, u32[]{:S(2)}, u32[]{:S(2)}) %all-to-all-start) | async-done | bytes 1126432 | tf_op jit(solution)/shard_map/all_to_all | solution.py:51
  54.7 19.3 %all-to-all-done.1 = bf16[16,25,1408]{2,1,0:T(8,128)(2,1)} async-done(((bf16[16,25,1408]{2,1,0:T(8,128)(2,1)}), bf16[16,25,1408]{2,1,0:T(8,128)(2,1)}, u32[]{:S(2)}, u32[]{:S(2)}) %all-to-all-start.1) | async-done | bytes 1126432 | tf_op jit(solution)/shard_map/all_to_all | solution.py:51
  89.4 20.3 %all-to-all-done.2 = bf16[16,25,1504]{2,1,0:T(8,128)(2,1)} async-done(((bf16[16,25,1504]{2,1,0:T(8,128)(2,1)}), bf16[16,25,1504]{2,1,0:T(8,128)(2,1)}, u32[]{:S(2)}, u32[]{:S(2)}) %all-to-all-start.2) | async-done | bytes 1203232 | tf_op jit(solution)/shard_map/all_to_all | solution.py:51
  134.7 8.1 all-to-all-start.3
  164.1 22.8 %collective-permute-done.10.refs_4_ = bf16[200,1408]{1,0:T(8,128)(2,1)S(1)} collective-permute-done((bf16[200,1408]{1,0:T(8,128)(2,1)S(1)}, bf16[200,1408]{1,0:T(8,128)(2,1)S(1)}, u32[]{:S(2)}, u32[]{:S(2)}) %collective-permute-start.10) | collective-permute-done | bytes 563232 | tf_op jit(solution)/shard_map/ppermute | solution.py:34
  197.4 7.5 all-to-all-start.4
  271.5 8.2 collective-permute-done.17
  314.2 9.9 all-to-all-start.6
  347.6 7.3 all-to-all-start.7
  365.4 25.8 %all-to-all-done.7 = bf16[64,16,128]{2,1,0:T(8,128)(2,1)} async-done(((bf16[64,16,128]{2,1,0:T(8,128)(2,1)}), bf16[64,16,128]{2,1,0:T(8,128)(2,1)}, u32[]{:S(2)}, u32[]{:S(2)}) %all-to-all-start.7) | async-done | bytes 262176 | tf_op jit(solution)/shard_map/all_to_all | solution.py:51
  397.5 10.7 shard_map.595
  415.6 13.7 %shard_map.593 = (bf16[5,128,320]{2,1,0:T(8,128)(2,1)S(1)}, f32[5,128,8]{2,1,0:T(8,128)S(1)}) custom-call(bf16[5,128,320]{2,1,0:T(8,128)(2,1)S(1)} %bitcast.121, bf16[1152,640]{1,0:T(8,128)(2,1)S(1)} %bitcast.118, f32[128,1152]{1,0:T(8,128)S(1)} %copy-done.76), custom_call_target="tpu_custom_call" | custom-call | flops 943718400 | bytes 589824 | tf_op jit(solution)/shard_map/pallas_call | solution.py:739
  435.9 17.5 %collective-permute-start.35 = (bf16[200,1600]{1,0:T(8,128)(2,1)S(1)}, bf16[200,1600]{1,0:T(8,128)(2,1)S(1)}, u32[]{:S(2)}, u32[]{:S(2)}) collective-permute-start(bf16[200,1600]{1,0:T(8,128)(2,1)S(1)} %slice.659), channel_id=1, source_target_pairs={{1,0},{32,1},{33,32},{0,33},{3,2},{34,3},{35,34},{2,35},{5,4},{36,... | collective-permute-start | bytes 1920008 | tf_op jit(solution)/shard_map/ppermute | solution.py:34
  468.1 13.3 %collective-permute-done.37.refs_5_ = bf16[200,1600]{1,0:T(8,128)(2,1)S(1)} collective-permute-done((bf16[200,1600]{1,0:T(8,128)(2,1)S(1)}, bf16[200,1600]{1,0:T(8,128)(2,1)S(1)}, u32[]{:S(2)}, u32[]{:S(2)}) %collective-permute-start.37) | collective-permute-done | bytes 640032 | tf_op jit(solution)/shard_map/ppermute | solution.py:34
  506.2 10.1 collective-permute-done.39
  518.7 8.0 collective-permute-done.41
  534.0 23.7 %shard_map.600 = (bf16[1024,704]{1,0:T(8,128)(2,1)S(1)}, bf16[1024,1408]{1,0:T(8,128)(2,1)}, bf16[1024,1664]{1,0:T(8,128)(2,1)}, bf16[1024,1664]{1,0:T(8,128)(2,1)}) custom-call(bf16[1024,1664]{1,0:T(8,128)(2,1)} %constant_dynamic-update-slice_fusion.11.x_ref, bf16[1024,1664]{1,0:T(8,128)(2,1)} %constant_dynamic-update-slice_fusion.g_ref, ...), custom_call_target="tpu_custom_call" | custom-call | flops 14394851328 | bytes 17956864 | tf_op jit(solution)/shard_map/pallas_call | solution.py:301
  569.2 10.1 shard_map.619
  646.7 15.9 %shard_map.609 = (bf16[5,128,320]{2,1,0:T(8,128)(2,1)S(1)}, bf16[1152,640]{1,0:T(8,128)(2,1)S(1)}) custom-call(bf16[5,128,320]{2,1,0:T(8,128)(2,1)S(1)} %bitcast.122, bf16[1152,640]{1,0:T(8,128)(2,1)S(1)} %bitcast.119, f32[1152,128]{1,0:T(8,128)S(1)} %copy-done.77, f32[5,8,128]{2,1,0:T(8,128)S(1)} %bitcast.126, bf16[5,128,320]{2,1,0:T(8,128)(2,1)S(1)} %bitcast.124), custom_call_target="tpu_custom_call" | custom-call | flops 2359296000 | bytes 589824 | tf_op jit(solution)/shard_map/pallas_call | solution.py:739
  701.1 8.3 all-to-all-start.9
  727.4 26.5 %shard_map.608 = (f32[128,3200]{1,0:T(8,128)S(1)}, f32[128,3200]{1,0:T(8,128)S(1)}, f32[16,3200]{1,0:T(8,128)S(1)}, f32[128,16,128]{2,1,0:T(8,128)S(1)}, f32[128,16,128]{2,1,0:T(8,128)S(1)}) custom-call(f32[128,3200]{1,0:T(8,128)S(1)} %copy-done.31, f32[128,3200]{1,0:T(8,128)S(1)} %copy-done.37, f32[128,3200]{1,0:T(8,128)S(1)} %copy-done.33, ...), custom_call_target="tpu_custom_call" | custom-call | flops 157286400 | bytes 6553600 | tf_op jit(solution)/shard_map/pallas_call | solution.py:653
  762.6 7.7 multiply_reduce_fusion.4
  789.9 41.7 %all-to-all-start.10 = ((bf16[128,55,128]{2,1,0:T(8,128)(2,1)}), bf16[128,55,128]{2,1,0:T(8,128)(2,1)}, u32[]{:S(2)}, u32[]{:S(2)}) async-start(bf16[128,55,128]{2,1,0:T(8,128)(2,1)} %pad_maximum_fusion.3), calls=%async_computation.10 | async-start | bytes 3670016 | tf_op jit(solution)/shard_map/all_to_all | solution.py:51
  846.5 12.1 %collective-permute-done.57 = bf16[128,640]{0,1:T(8,128)(2,1)S(1)} collective-permute-done((bf16[128,640]{0,1:T(8,128)(2,1)S(1)}, bf16[128,640]{0,1:T(8,128)(2,1)S(1)}, u32[]{:S(2)}, u32[]{:S(2)}) %collective-permute-start.57) | collective-permute-done | bytes 163872 | tf_op jit(solution)/shard_map/ppermute | solution.py:34
  917.1 6.5 collective-permute-done.66
  989.3 20.9 %collective-permute-done.71 = bf16[400,1504]{1,0:T(8,128)(2,1)S(1)} collective-permute-done((bf16[400,1504]{1,0:T(8,128)(2,1)}, bf16[400,1504]{1,0:T(8,128)(2,1)S(1)}, u32[]{:S(2)}, u32[]{:S(2)}) %collective-permute-start.71) | collective-permute-done | bytes 1203232 | tf_op jit(solution)/shard_map/ppermute | solution.py:34
  1032.0 12.5 %all-to-all-done.12 = bf16[16,25,1504]{2,1,0:T(8,128)(2,1)} async-done(((bf16[16,25,1504]{2,1,0:T(8,128)(2,1)}), bf16[16,25,1504]{2,1,0:T(8,128)(2,1)}, u32[]{:S(2)}, u32[]{:S(2)}) %all-to-all-start.12) | async-done | bytes 1203232 | tf_op jit(solution)/shard_map/all_to_all | solution.py:51
  1064.1 20.0 %all-to-all-done.13 = bf16[16,25,2208]{2,1,0:T(8,128)(2,1)} async-done(((bf16[16,25,2208]{2,1,0:T(8,128)(2,1)}), bf16[16,25,2208]{2,1,0:T(8,128)(2,1)}, u32[]{:S(2)}, u32[]{:S(2)}) %all-to-all-start.13) | async-done | bytes 1766432 | tf_op jit(solution)/shard_map/all_to_all | solution.py:51
  1084.1 6.5 all-to-all-start.14
  1116.0 17.4 %all-to-all-done.14 = bf16[16,25,3008]{2,1,0:T(8,128)(2,1)S(1)} async-done(((bf16[16,25,3008]{2,1,0:T(8,128)(2,1)}), bf16[16,25,3008]{2,1,0:T(8,128)(2,1)S(1)}, u32[]{:S(2)}, u32[]{:S(2)}) %all-to-all-start.14) | async-done | bytes 2406432 | tf_op jit(solution)/shard_map/all_to_all | solution.py:51
  1141.4 6.4 all-to-all-done.15
  (1028 shorter events, 673.8 us)
Async XLA Ops:
  17.7 195.3 %all-gather.12.cloned.1.call-start = ((), (), s32[]{:S(2)}) async-start(), calls=%async_computation.20 | async-start | bytes 1810432 | tf_op jit(solution)/shard_map/all_gather | solution.py:168
  51.1 481.2 %all-gather.10.cloned.1.call-start = ((), (), s32[]{:S(2)}) async-start(), calls=%async_computation.19 | async-start | bytes 2635776 | tf_op jit(solution)/shard_map/all_gather | solution.py:168
  53.0 61.4 %collective-permute-start.9 = (bf16[400,1408]{1,0:T(8,128)(2,1)S(1)}, bf16[400,1408]{1,0:T(8,128)(2,1)}, u32[]{:S(2)}, u32[]{:S(2)}) collective-permute-start(bf16[400,1408]{1,0:T(8,128)(2,1)S(1)} %reshape.400.refs_1_), channel_id=1, source_target_pairs={{33,0},{0,1},{1,32},{32,33},{35,2},{2,3},{3,34},{34,35},{37,4},{4,... | collective-permute-start | bytes 3379208 | tf_op jit(solution)/shard_map/ppermute | solution.py:34
  85.5 62.5 %collective-permute-start.11 = (bf16[400,1408]{1,0:T(8,128)(2,1)}, bf16[400,1408]{1,0:T(8,128)(2,1)}, u32[]{:S(2)}, u32[]{:S(2)}) collective-permute-start(bf16[400,1408]{1,0:T(8,128)(2,1)} %reshape.401.refs_1_), channel_id=1, source_target_pairs={{8,0},{16,8},{24,16},{0,24},{9,1},{17,9},{25,17},{1,25},{10,2},{18... | collective-permute-start | bytes 3379208 | tf_op jit(solution)/shard_map/ppermute | solution.py:34
  89.4 70.0 %collective-permute-start.13 = (bf16[400,1408]{1,0:T(8,128)(2,1)}, bf16[400,1408]{1,0:T(8,128)(2,1)}, u32[]{:S(2)}, u32[]{:S(2)}) collective-permute-start(bf16[400,1408]{1,0:T(8,128)(2,1)} %reshape.401.refs_1_), channel_id=1, source_target_pairs={{24,0},{0,8},{8,16},{16,24},{25,1},{1,9},{9,17},{17,25},{26,2},{2,... | collective-permute-start | bytes 3379208 | tf_op jit(solution)/shard_map/ppermute | solution.py:34
  111.5 93.5 %collective-permute-start.3 = (bf16[400,1504]{1,0:T(8,128)(2,1)S(1)}, bf16[400,1504]{1,0:T(8,128)(2,1)}, u32[]{:S(2)}, u32[]{:S(2)}) collective-permute-start(bf16[400,1504]{1,0:T(8,128)(2,1)S(1)} %reshape.402.refs_1_), channel_id=1, source_target_pairs={{2,0},{4,2},{6,4},{0,6},{3,1},{5,3},{7,5},{1,7},{10,8},{12,10},{14... | collective-permute-start | bytes 3609608 | tf_op jit(solution)/shard_map/ppermute | solution.py:34
  114.3 95.7 %collective-permute-start.5 = (bf16[400,1504]{1,0:T(8,128)(2,1)S(1)}, bf16[400,1504]{1,0:T(8,128)(2,1)}, u32[]{:S(2)}, u32[]{:S(2)}) collective-permute-start(bf16[400,1504]{1,0:T(8,128)(2,1)S(1)} %reshape.402.refs_1_), channel_id=1, source_target_pairs={{6,0},{0,2},{2,4},{4,6},{7,1},{1,3},{3,5},{5,7},{14,8},{8,10},{10,... | collective-permute-start | bytes 3609608 | tf_op jit(solution)/shard_map/ppermute | solution.py:34
  134.7 59.6 %all-to-all-start.3 = ((bf16[64,50,128]{2,1,0:T(8,128)(2,1)}), bf16[64,50,128]{2,1,0:T(8,128)(2,1)}, u32[]{:S(2)}, u32[]{:S(2)}) async-start(bf16[64,50,128]{2,1,0:T(8,128)(2,1)} %broadcast_in_dim.66), calls=%async_computation.3 | async-start | bytes 1835008 | tf_op jit(solution)/shard_map/all_to_all | solution.py:51
  227.7 304.6 %all-gather.8.cloned.1.call-start = ((), (), s32[]{:S(2)}) async-start(), calls=%async_computation.18 | async-start | bytes 4978688 | tf_op jit(solution)/shard_map/all_gather | solution.py:168
  254.1 74.7 %collective-permute-start.23 = (bf16[128,1664]{1,0:T(8,128)(2,1)}, bf16[128,1664]{1,0:T(8,128)(2,1)}, u32[]{:S(2)}, u32[]{:S(2)}) collective-permute-start(bf16[128,1664]{1,0:T(8,128)(2,1)} %get-tuple-element.361), channel_id=1, source_target_pairs={{2,0},{4,2},{6,4},{0,6},{3,1},{5,3},{7,5},{1,7},{10,8},{12,10},{14... | collective-permute-start | bytes 1277960 | tf_op jit(solution)/shard_map/ppermute | solution.py:34
  255.6 78.1 %collective-permute-start.24 = (bf16[128,1664]{1,0:T(8,128)(2,1)}, bf16[128,1664]{1,0:T(8,128)(2,1)}, u32[]{:S(2)}, u32[]{:S(2)}) collective-permute-start(bf16[128,1664]{1,0:T(8,128)(2,1)} %get-tuple-element.361), channel_id=1, source_target_pairs={{4,0},{6,2},{0,4},{2,6},{5,1},{7,3},{1,5},{3,7},{12,8},{14,10},{8,... | collective-permute-start | bytes 1277960 | tf_op jit(solution)/shard_map/ppermute | solution.py:34
  287.5 70.1 %collective-permute-start.28 = (bf16[400,800]{1,0:T(8,128)(2,1)S(1)}, bf16[400,800]{1,0:T(8,128)(2,1)}, u32[]{:S(2)}, u32[]{:S(2)}) collective-permute-start(bf16[400,800]{1,0:T(8,128)(2,1)S(1)} %reshape.404.refs_1_), channel_id=1, source_target_pairs={{8,0},{16,8},{24,16},{0,24},{9,1},{17,9},{25,17},{1,25},{10,2},{18... | collective-permute-start | bytes 1920008 | tf_op jit(solution)/shard_map/ppermute | solution.py:34
  293.8 69.8 %collective-permute-start.30 = (bf16[400,800]{1,0:T(8,128)(2,1)S(1)}, bf16[400,800]{1,0:T(8,128)(2,1)}, u32[]{:S(2)}, u32[]{:S(2)}) collective-permute-start(bf16[400,800]{1,0:T(8,128)(2,1)S(1)} %reshape.404.refs_1_), channel_id=1, source_target_pairs={{24,0},{0,8},{8,16},{16,24},{25,1},{1,9},{9,17},{17,25},{26,2},{2,... | collective-permute-start | bytes 1920008 | tf_op jit(solution)/shard_map/ppermute | solution.py:34
  328.8 105.9 %collective-permute-start.34 = (bf16[400,1600]{1,0:T(8,128)(2,1)S(1)}, bf16[400,1600]{1,0:T(8,128)(2,1)}, u32[]{:S(2)}, u32[]{:S(2)}) collective-permute-start(bf16[400,1600]{1,0:T(8,128)(2,1)S(1)} %reshape.458.refs_2_), channel_id=1, source_target_pairs={{1,0},{32,1},{33,32},{0,33},{3,2},{34,3},{35,34},{2,35},{5,4},{36,... | collective-permute-start | bytes 3840008 | tf_op jit(solution)/shard_map/ppermute | solution.py:34
  333.6 119.7 %collective-permute-start.36 = (bf16[400,1600]{1,0:T(8,128)(2,1)S(1)}, bf16[400,1600]{1,0:T(8,128)(2,1)}, u32[]{:S(2)}, u32[]{:S(2)}) collective-permute-start(bf16[400,1600]{1,0:T(8,128)(2,1)S(1)} %reshape.458.refs_2_), channel_id=1, source_target_pairs={{33,0},{0,1},{1,32},{32,33},{35,2},{2,3},{3,34},{34,35},{37,4},{4,... | collective-permute-start | bytes 3840008 | tf_op jit(solution)/shard_map/ppermute | solution.py:34
  335.4 75.7 %collective-permute-start.21 = (bf16[4,128,640]{2,1,0:T(8,128)(2,1)}, bf16[4,128,640]{2,1,0:T(8,128)(2,1)}, u32[]{:S(2)}, u32[]{:S(2)}) collective-permute-start(bf16[4,128,640]{2,1,0:T(8,128)(2,1)} %constant_dynamic-update-slice_fusion.17), channel_id=1, source_target_pairs={{0,16},{8,24},{16,32},{24,40},{32,48},{40,56},{48,64},{56,72},{64,... | collective-permute-start | bytes 1966088 | tf_op jit(solution)/shard_map/ppermute | solution.py:43
  354.9 701.8 %reduce-scatter.11.cloned.1.call-start = ((), (), s32[]{:S(2)}) async-start(), calls=%async_computation.22 | async-start | bytes 2635776
  363.7 90.9 %collective-permute-start.26 = (bf16[512,1664]{1,0:T(8,128)(2,1)}, bf16[512,1664]{1,0:T(8,128)(2,1)}, u32[]{:S(2)}, u32[]{:S(2)}) collective-permute-start(bf16[512,1664]{1,0:T(8,128)(2,1)} %pad_maximum_fusion.4), channel_id=1, source_target_pairs={{64,0},{0,64},{65,1},{1,65},{66,2},{2,66},{67,3},{3,67},{68,4},{4,... | collective-permute-start | bytes 5111816 | tf_op jit(solution)/shard_map/ppermute | solution.py:34
  580.7 554.4 %reduce-scatter.9.cloned.1.call-start = ((), (), s32[]{:S(2)}) async-start(), calls=%async_computation.21 | async-start | bytes 4978688
  637.3 205.8 %collective-permute-start.78 = (bf16[200,1600]{1,0:T(8,128)(2,1)}, bf16[200,1600]{1,0:T(8,128)(2,1)}, u32[]{:S(2)}, u32[]{:S(2)}) collective-permute-start(bf16[200,1600]{1,0:T(8,128)(2,1)} %get-tuple-element.160), channel_id=1, source_target_pairs={{33,0},{0,1},{1,32},{32,33},{35,2},{2,3},{3,34},{34,35},{37,4},{4,... | collective-permute-start | bytes 1920008 | tf_op jit(solution)/shard_map/ppermute | solution.py:34
  637.3 238.3 %collective-permute-start.80 = (bf16[200,1600]{1,0:T(8,128)(2,1)}, bf16[200,1600]{1,0:T(8,128)(2,1)}, u32[]{:S(2)}, u32[]{:S(2)}) collective-permute-start(bf16[200,1600]{1,0:T(8,128)(2,1)} %get-tuple-element.162), channel_id=1, source_target_pairs={{1,0},{32,1},{33,32},{0,33},{3,2},{34,3},{35,34},{2,35},{5,4},{36,... | collective-permute-start | bytes 1920008 | tf_op jit(solution)/shard_map/ppermute | solution.py:34
  682.7 153.9 %collective-permute-start.55 = (bf16[4,128,640]{1,2,0:T(8,128)(2,1)}, bf16[4,128,640]{1,2,0:T(8,128)(2,1)}, u32[]{:S(2)}, u32[]{:S(2)}) collective-permute-start(bf16[4,128,640]{1,2,0:T(8,128)(2,1)} %get-tuple-element.296), channel_id=1, source_target_pairs={{8,0},{16,8},{24,16},{32,24},{40,32},{48,40},{56,48},{64,56},{72,6... | collective-permute-start | bytes 1966088 | tf_op jit(solution)/shard_map/ppermute | solution.py:43
  709.5 127.1 %collective-permute-start.56 = (bf16[4,128,640]{1,2,0:T(8,128)(2,1)}, bf16[4,128,640]{1,2,0:T(8,128)(2,1)}, u32[]{:S(2)}, u32[]{:S(2)}) collective-permute-start(bf16[4,128,640]{1,2,0:T(8,128)(2,1)} %get-tuple-element.297), channel_id=1, source_target_pairs={{16,0},{24,8},{32,16},{40,24},{48,32},{56,40},{64,48},{72,56},{80,... | collective-permute-start | bytes 1966088 | tf_op jit(solution)/shard_map/ppermute | solution.py:43
  771.5 60.2 %collective-permute-start.53 = (bf16[3,3200]{1,0:T(4,128)(2,1)}, bf16[3,3200]{1,0:T(4,128)(2,1)S(1)}, u32[]{:S(2)}, u32[]{:S(2)}) collective-permute-start(bf16[3,3200]{1,0:T(4,128)(2,1)} %slice.839), channel_id=1, source_target_pairs={{2,0},{4,2},{6,4},{8,6},{10,8},{12,10},{14,12},{16,14},{18,16},{20... | collective-permute-start | bytes 57608 | tf_op jit(solution)/shard_map/ppermute | solution.py:43
  789.9 164.3 %all-to-all-start.10 = ((bf16[128,55,128]{2,1,0:T(8,128)(2,1)}), bf16[128,55,128]{2,1,0:T(8,128)(2,1)}, u32[]{:S(2)}, u32[]{:S(2)}) async-start(bf16[128,55,128]{2,1,0:T(8,128)(2,1)} %pad_maximum_fusion.3), calls=%async_computation.10 | async-start | bytes 3670016 | tf_op jit(solution)/shard_map/all_to_all | solution.py:51
  831.7 188.2 %collective-permute-start.49 = (bf16[512,1664]{1,0:T(8,128)(2,1)}, bf16[512,1664]{1,0:T(8,128)(2,1)}, u32[]{:S(2)}, u32[]{:S(2)}) collective-permute-start(bf16[512,1664]{1,0:T(8,128)(2,1)} %slice.549), channel_id=1, source_target_pairs={{64,0},{0,64},{65,1},{1,65},{66,2},{2,66},{67,3},{3,67},{68,4},{4,... | collective-permute-start | bytes 5111816 | tf_op jit(solution)/shard_map/ppermute | solution.py:34
  957.3 56.9 %all-to-all-start.11 = ((f32[128,18,128]{2,1,0:T(8,128)}), f32[128,18,128]{2,1,0:T(8,128)}, u32[]{:S(2)}, u32[]{:S(2)}) async-start(f32[128,18,128]{2,1,0:T(8,128)} %broadcast_in_dim.153), calls=%async_computation.11 | async-start | bytes 3145728 | tf_op jit(solution)/shard_map/all_to_all | solution.py:51
  979.4 74.0 %collective-permute-start.79 = (bf16[400,1600]{1,0:T(8,128)(2,1)}, bf16[400,1600]{1,0:T(8,128)(2,1)}, u32[]{:S(2)}, u32[]{:S(2)}) collective-permute-start(bf16[400,1600]{1,0:T(8,128)(2,1)} %pad_maximum_fusion.8), channel_id=1, source_target_pairs={{33,0},{0,1},{1,32},{32,33},{35,2},{2,3},{3,34},{34,35},{37,4},{4,... | collective-permute-start | bytes 3840008 | tf_op jit(solution)/shard_map/ppermute | solution.py:34
  981.8 71.6 %collective-permute-start.81 = (bf16[400,1600]{1,0:T(8,128)(2,1)}, bf16[400,1600]{1,0:T(8,128)(2,1)}, u32[]{:S(2)}, u32[]{:S(2)}) collective-permute-start(bf16[400,1600]{1,0:T(8,128)(2,1)} %pad_maximum_fusion.9), channel_id=1, source_target_pairs={{1,0},{32,1},{33,32},{0,33},{3,2},{34,3},{35,34},{2,35},{5,4},{36,... | collective-permute-start | bytes 3840008 | tf_op jit(solution)/shard_map/ppermute | solution.py:34
  1023.6 69.3 %collective-permute-start.50 = (bf16[128,1664]{1,0:T(8,128)(2,1)}, bf16[128,1664]{1,0:T(8,128)(2,1)}, u32[]{:S(2)}, u32[]{:S(2)}) collective-permute-start(bf16[128,1664]{1,0:T(8,128)(2,1)} %get-tuple-element.307), channel_id=1, source_target_pairs={{6,0},{0,2},{2,4},{4,6},{7,1},{1,3},{3,5},{5,7},{14,8},{8,10},{10,... | collective-permute-start | bytes 1277960 | tf_op jit(solution)/shard_map/ppermute | solution.py:34
  1024.2 68.7 %collective-permute-start.51 = (bf16[128,1664]{1,0:T(8,128)(2,1)}, bf16[128,1664]{1,0:T(8,128)(2,1)}, u32[]{:S(2)}, u32[]{:S(2)}) collective-permute-start(bf16[128,1664]{1,0:T(8,128)(2,1)} %get-tuple-element.306), channel_id=1, source_target_pairs={{4,0},{6,2},{0,4},{2,6},{5,1},{7,3},{1,5},{3,7},{12,8},{14,10},{8,... | collective-permute-start | bytes 1277960 | tf_op jit(solution)/shard_map/ppermute | solution.py:34
  1027.2 65.6 %collective-permute-start.52 = (bf16[128,1664]{1,0:T(8,128)(2,1)}, bf16[128,1664]{1,0:T(8,128)(2,1)}, u32[]{:S(2)}, u32[]{:S(2)}) collective-permute-start(bf16[128,1664]{1,0:T(8,128)(2,1)} %get-tuple-element.305), channel_id=1, source_target_pairs={{2,0},{4,2},{6,4},{0,6},{3,1},{5,3},{7,5},{1,7},{10,8},{12,10},{14... | collective-permute-start | bytes 1277960 | tf_op jit(solution)/shard_map/ppermute | solution.py:34
  (310 other events, 4240.4 us)
Sparse Core Ops, SparseCore 0:
  41.7 68.3 all-gather.11
  111.8 81.1 all-gather.9
  239.7 121.0 all-gather.7
  580.8 52.3 reduce-scatter.10
  635.6 136.9 reduce-scatter.8
